TPU v7x, 128 devices: a whole 4x4x4 slice. The times are simulated.
128 devices in a mesh: rep: 4 (over x), fsdp: 32 (over z, y, core).
Axes of the slice: x: 4, y: 4, z: 4, core: 2. Of those that a mesh axis runs over, the one named last changes fastest.
Arguments:
- grads: bfloat16 [4, 256, 512, 512], P('rep', None, 'fsdp'), may hold values from -2 to 2
- owner_table: int32 [256, 1], replicated, may hold values from 0 to 31; in each aligned block of 64 rows (0 to 63, 64 to 127, ...) at most 3 rows name the same one
- left_stats: float32 [4, 32, 3, 512, 512], P('rep', 'fsdp'), may hold values from -1 to 100, as said below
- right_stats: float32 [4, 32, 3, 512, 512], P('rep', 'fsdp'), may hold values from -1 to 100, as said below
- left_roots: bfloat16 [4, 32, 3, 512, 512], P('rep', 'fsdp'), may hold values from -1 to 6, as said below
- right_roots: bfloat16 [4, 32, 3, 512, 512], P('rep', 'fsdp'), may hold values from -1 to 6, as said below
Outputs:
- preconditioned: bfloat16 [256, 512, 512], P('rep', 'fsdp')
- left_updated: float32 [4, 32, 3, 512, 512], P('rep', 'fsdp')
- right_updated: float32 [4, 32, 3, 512, 512], P('rep', 'fsdp')
- left_root_new: bfloat16 [4, 32, 512, 512], P('rep', 'fsdp')
- right_root_new: bfloat16 [4, 32, 512, 512], P('rep', 'fsdp')
Inputs may be any that keep to these rules, and one draw needn't show every extreme that they name: `owner_table`: block b belongs to replica group b // 64. Among the 64 blocks of one group no owner is named more than 3 times, and in some group one owner is named exactly 3 times. `left_stats`: each matrix is symmetric positive definite. `right_stats`: each matrix is symmetric positive definite. `left_roots`: each matrix is symmetric positive definite. `right_roots`: each matrix is symmetric positive definite.
All inputs are finite; a program needn't handle non-finite values.
Results may differ from a plain program's by a relative error of at most 0.015.
Values may be sent and summed in bfloat16 or wider, within the bound.
No kernel may reach another device: no remote copies, remote signals or barrier semaphores. Data moves between devices by JAX's collectives and lax.ppermute only.
A program may use at most 128 MiB of HBM per device.

v0:
```python
import jax
import jax.numpy as jnp
from jax import lax
from jax.sharding import PartitionSpec as P

ITERS = 2


DECAY_RATE = 0.9
ROOT_RIDGE = 1e-06
GRAFT_EPS = 1e-12
NORM_EPS = 1e-12


def slot_positions(owner_row, most_slots):
    count_rows = owner_row.shape[0]
    order_ids = jnp.arange(count_rows, dtype=jnp.int32)
    same_owner = owner_row[:, None] == owner_row[None, :]
    earlier = order_ids[None, :] < order_ids[:, None]
    slot_rank = jnp.sum((same_owner & earlier).astype(jnp.int32), axis=1)
    return owner_row * most_slots + slot_rank


def slot_blocks(position, total_slots):
    count_rows = position.shape[0]
    order_ids = jnp.arange(count_rows, dtype=jnp.int32)
    matches = position[None, :] == jnp.arange(total_slots, dtype=jnp.int32)[:, None]
    block_index = jnp.sum(jnp.where(matches, order_ids[None, :], 0), axis=1)
    occupied = jnp.any(matches, axis=1)
    return (block_index, occupied)


def batch_mul(left_mat, right_mat):
    return jnp.einsum("bij,bjk->bik", left_mat, right_mat, precision=lax.Precision.HIGHEST)


def fourth_root(stacked):
    side_count = stacked.shape[-1]
    identity_mat = jnp.eye(side_count, dtype=jnp.float32)
    frob_norm = side_count * jnp.sqrt(jnp.mean(stacked * stacked, axis=(1, 2)) + NORM_EPS)
    scaled = stacked * (2.5 / frob_norm)[:, None, None]
    root_est = jnp.broadcast_to(identity_mat, stacked.shape)
    for newton_turn in range(ITERS):
        factor = (5.0 * identity_mat - scaled) * 0.25
        square = batch_mul(factor, factor)
        fourth = batch_mul(square, square)
        root_est = batch_mul(root_est, factor)
        scaled = batch_mul(fourth, scaled)
    return root_est


def refresh(blocks, live_slots, left_prev, right_prev, left_given, right_given):
    gram_left = jnp.einsum("sij,skj->sik", blocks, blocks, preferred_element_type=jnp.float32)
    gram_right = jnp.einsum("sji,sjk->sik", blocks, blocks, preferred_element_type=jnp.float32)
    keep_mask = live_slots[:, None, None]
    new_left = jnp.where(
        keep_mask, DECAY_RATE * left_prev + (1.0 - DECAY_RATE) * gram_left, left_prev
    )
    new_right = jnp.where(
        keep_mask, DECAY_RATE * right_prev + (1.0 - DECAY_RATE) * gram_right, right_prev
    )
    side_count = blocks.shape[-1]
    identity_mat = jnp.eye(side_count, dtype=jnp.float32)
    roots = fourth_root(jnp.stack([new_left[0], new_right[0]]) + ROOT_RIDGE * identity_mat)
    root_pair = roots.astype(jnp.bfloat16)
    left_use = jnp.concatenate([root_pair[0:1], left_given[1:]], axis=0)
    right_use = jnp.concatenate([root_pair[1:2], right_given[1:]], axis=0)
    right_applied = jnp.einsum(
        "sij,sjk->sik", blocks, right_use, preferred_element_type=jnp.float32
    ).astype(jnp.bfloat16)
    raw_out = jnp.einsum(
        "sij,sjk->sik", left_use, right_applied, preferred_element_type=jnp.float32
    )
    grad_power = jnp.mean(jnp.square(blocks.astype(jnp.float32)), axis=(1, 2))
    out_power = jnp.mean(raw_out * raw_out, axis=(1, 2))
    graft_scale = jnp.sqrt(grad_power) / jnp.sqrt(out_power + GRAFT_EPS)
    slot_out = (raw_out * graft_scale[:, None, None]).astype(jnp.bfloat16)
    return (slot_out, new_left, new_right, root_pair[0], root_pair[1])


def on_device(grads, owner_table, left_stats, right_stats, left_roots, right_roots):
    groups = lax.axis_size("rep")
    owners = lax.axis_size("fsdp")
    group_id = lax.axis_index("rep")
    owner_id = lax.axis_index("fsdp")
    local_grads = grads[0]
    total_blocks = local_grads.shape[0]
    slab_rows = local_grads.shape[1]
    side_count = local_grads.shape[2]
    share = total_blocks // groups
    most_slots = left_stats.shape[2]
    owner_row = lax.dynamic_slice_in_dim(owner_table[:, 0], group_id * share, share)
    position = slot_positions(owner_row, most_slots)
    block_index, occupied = slot_blocks(position, owners * most_slots)
    summed = lax.psum(local_grads.astype(jnp.float32).astype(jnp.bfloat16), "rep").astype(
        jnp.float32
    )
    summed = lax.dynamic_slice_in_dim(summed, group_id * share, share, 0)
    gradient = summed.astype(jnp.bfloat16)
    picked = jnp.take(gradient, block_index, axis=0)
    outgoing = jnp.where(occupied[:, None, None], picked, jnp.zeros_like(picked))
    outgoing = outgoing.reshape(owners, most_slots, slab_rows, side_count)
    arrived = lax.all_to_all(outgoing, "fsdp", split_axis=0, concat_axis=2, tiled=True)
    blocks = arrived[0]
    own_count = jnp.sum((owner_row == owner_id).astype(jnp.int32))
    live_slots = jnp.arange(most_slots, dtype=jnp.int32) < own_count
    slot_out, new_left, new_right, left_new, right_new = refresh(
        blocks, live_slots, left_stats[0, 0], right_stats[0, 0], left_roots[0, 0], right_roots[0, 0]
    )
    sending = slot_out.reshape(most_slots, owners, slab_rows, side_count)
    returned = lax.all_to_all(sending, "fsdp", split_axis=1, concat_axis=0, tiled=True)
    returned = returned.reshape(owners * most_slots, slab_rows, side_count)
    preconditioned = jnp.take(returned, position, axis=0)
    return (
        preconditioned,
        new_left[None, None],
        new_right[None, None],
        left_new[None, None],
        right_new[None, None],
    )


def solution(mesh):
    in_specs = (
        P("rep", None, "fsdp", None),
        P(),
        P("rep", "fsdp", None, None, None),
        P("rep", "fsdp", None, None, None),
        P("rep", "fsdp", None, None, None),
        P("rep", "fsdp", None, None, None),
    )
    out_specs = (
        P("rep", "fsdp", None),
        P("rep", "fsdp", None, None, None),
        P("rep", "fsdp", None, None, None),
        P("rep", "fsdp", None, None),
        P("rep", "fsdp", None, None),
    )
    return jax.shard_map(
        on_device, mesh=mesh, in_specs=in_specs, out_specs=out_specs, check_vma=False
    )
```

profile of v0, /device:TPU:0, one launch (start us, length us, event | category | flops | bytes accessed | tf_op | source)
XLA Modules:
  0.0 216.0 jit_solution(6861243504238005371)
XLA Ops:
  7.2 0.7 all-reduce.2.cloned.1.call-update
  7.9 0.7 fusion.36
  9.3 96.3 %all-reduce.2.cloned.1.call-done = bf16[256,16,512]{2,1,0:T(8,128)(2,1)} async-done(((bf16[256,16,512]{2,1,0:T(8,128)(2,1)}), bf16[256,16,512]{2,1,0:T(8,128)(2,1)}) %all-reduce.2.cloned.1.call-update) | async-done | bytes 4194320 | tf_op jit(solution)/shard_map/psum | solution.py:95
  105.6 1.3 convert_convert_fusion
  106.9 0.7 gather_fusion
  107.6 1.4 select_select_fusion
  109.0 7.3 %all-to-all-start = ((bf16[32,3,16,512]{3,2,1,0:T(8,128)(2,1)}), bf16[32,3,16,512]{3,2,1,0:T(8,128)(2,1)S(1)}, u32[]{:S(2)}, u32[]{:S(2)}) async-start(bf16[32,3,16,512]{3,2,1,0:T(8,128)(2,1)} %select_select_fusion), calls=%async_computation | async-start | bytes 3145728 | tf_op jit(solution)/shard_map/all_to_all | solution.py:103
  116.3 0.8 iota_compare_fusion.3
  117.1 1.1 fusion.33
  118.3 1.3 fusion.31
  119.5 1.5 slice_bitcast_fusion
  121.0 19.2 %all-to-all-done = bf16[32,3,16,512]{3,2,1,0:T(8,128)(2,1)S(1)} async-done(((bf16[32,3,16,512]{3,2,1,0:T(8,128)(2,1)}), bf16[32,3,16,512]{3,2,1,0:T(8,128)(2,1)S(1)}, u32[]{:S(2)}, u32[]{:S(2)}) %all-to-all-start) | async-done | bytes 1572896 | tf_op jit(solution)/shard_map/all_to_all | solution.py:103
  140.2 1.2 copy-done.1
  141.4 1.7 copy.23
  143.1 0.7 copy-done.6
  143.8 1.3 bitcast_select_fusion.1
  145.7 1.4 bitcast_select_fusion
  147.6 1.1 copy-done.4
  149.2 4.2 %fusion.7 = f32[2,512,512]{2,1,0:T(8,128)S(1)} fusion(f32[2]{0:T(128)S(1)} %multiply_divide_fusion, f32[512,512]{1,0:T(8,128)S(1)} %copy-done, f32[1,512,512]{2,1,0:T(8,128)S(1)} %slice.39, f32[1,512,512]{2,1,0:T(8,128)S(1)} %slice.38, f32[512,512]{1,0:T(8,128)S(1)} %get-tuple-element.15), kind=kOutput, calls=%fused_computation.20 | convolution fusion | flops 3223846912 | bytes 6291464 | tf_op jit(solution)/shard_map/bij,bjk->bik/dot_general | solution.py:34
  153.3 3.5 %fusion.47 = f32[2,512,512]{2,1,0:T(8,128)S(1)} fusion(f32[2,512,512]{2,1,0:T(8,128)S(1)} %fusion.7), kind=kOutput, calls=%fused_computation.78 | convolution fusion | flops 3221225472 | bytes 4194304 | tf_op jit(solution)/shard_map/bij,bjk->bik/dot_general | solution.py:34
  156.9 4.0 %fusion.5 = f32[2,512,512]{2,1,0:T(8,128)S(1)} fusion(f32[2,512,512]{2,1,0:T(8,128)S(1)} %fusion.47, f32[2]{0:T(128)S(1)} %multiply_divide_fusion, f32[1,512,512]{2,1,0:T(8,128)S(1)} %slice.39, f32[1,512,512]{2,1,0:T(8,128)S(1)} %slice.38, f32[512,512]{1,0:T(8,128)S(1)} %get-tuple-element.15), kind=kOutput, calls=%fused_computation.18 | convolution fusion | flops 3222798336 | bytes 7340040 | tf_op jit(solution)/shard_map/bij,bjk->bik/dot_general | solution.py:34
  160.9 3.9 %fusion.8 = f32[2,512,512]{2,1,0:T(8,128)S(1)} fusion(f32[2]{0:T(128)S(1)} %multiply_divide_fusion, f32[512,512]{1,0:T(8,128)S(1)} %copy-done, f32[512,512]{1,0:T(8,128)S(1)} %copy-done.5, f32[1,512,512]{2,1,0:T(8,128)S(1)} %slice.39, f32[1,512,512]{2,1,0:T(8,128)S(1)} %slice.38, f32[512,512]{1,0:T(8,128)S(1)} %get-tuple-element.15), kind=kOutput, calls=%fused_computation.21 | convolution fusion | flops 3223846912 | bytes 7340040 | tf_op jit(solution)/shard_map/bij,bjk->bik/dot_general | solution.py:34
  164.8 3.7 %fusion.16 = bf16[2,512,512]{2,1,0:T(8,128)(2,1)S(1)} fusion(f32[2,512,512]{2,1,0:T(8,128)S(1)} %fusion.8, f32[2,512,512]{2,1,0:T(8,128)S(1)} %fusion.5, f32[512,512]{1,0:T(8,128)S(1)} %copy-done), kind=kOutput, calls=%fused_computation.31 | convolution fusion | flops 3222798336 | bytes 6291456 | tf_op jit(solution)/shard_map/bij,bjk->bik/dot_general | solution.py:34
  168.5 1.4 slice_bitcast_fusion.2
  169.9 5.4 %multiply_reduce_fusion = (f32[3]{0:T(128)S(1)}, f32[3,512,512]{2,1,0:T(8,128)}) fusion(bf16[3,512,512]{2,1,0:T(8,128)(2,1)S(1)} %bitcast.63, bf16[2,512,512]{2,1,0:T(8,128)(2,1)} %get-tuple-element.17, bf16[1,512,512]{2,1,0:T(8,128)(2,1)} %get-tuple-element.11, bf16[2,512,512]{2,1,0:T(8,128)(2,1)} %get-tuple-element.18, ...), kind=kOutput, calls=%fused_computation.9 | convolution fusion | flops 1614544896 | bytes 7864332 | tf_op jit(solution)/shard_map/sij,sjk->sik/dot_general | solution.py:71
  175.4 0.5 multiply_reduce_fusion.1
  175.9 2.4 %multiply_convert_fusion = bf16[3,512,512]{2,1,0:T(8,128)(2,1)S(1)} fusion(f32[3,512,512]{2,1,0:T(8,128)} %get-tuple-element.14, f32[3]{0:T(128)S(1)} %rsqrt_multiply_fusion), kind=kLoop, calls=%fused_computation.8 | loop fusion | flops 1572864 | bytes 4718604 | tf_op jit(solution)/shard_map/convert_element_type | solution.py:77
  178.2 1.3 copy.25
  179.5 4.0 %all-to-all-start.1 = ((bf16[3,32,16,512]{3,2,0,1:T(8,128)(2,1)}), bf16[3,32,16,512]{3,2,0,1:T(8,128)(2,1)S(1)}, u32[]{:S(2)}, u32[]{:S(2)}) async-start(bf16[3,32,16,512]{3,2,0,1:T(8,128)(2,1)} %copy.25), calls=%async_computation.1 | async-start | bytes 3145728 | tf_op jit(solution)/shard_map/all_to_all | solution.py:111
  183.6 23.8 %all-to-all-done.1 = bf16[3,32,16,512]{3,2,0,1:T(8,128)(2,1)S(1)} async-done(((bf16[3,32,16,512]{3,2,0,1:T(8,128)(2,1)}), bf16[3,32,16,512]{3,2,0,1:T(8,128)(2,1)S(1)}, u32[]{:S(2)}, u32[]{:S(2)}) %all-to-all-start.1) | async-done | bytes 1572896 | tf_op jit(solution)/shard_map/all_to_all | solution.py:111
  207.4 0.6 gather_fusion.1
  208.0 1.1 broadcast_select_fusion
  (36 shorter events, 2.3 us)
Async XLA Ops:
  7.2 98.4 %all-reduce.2.cloned.1.call-start = ((), (), s32[]{:S(2)}) async-start(), calls=%async_computation.2 | async-start | bytes 8388608 | tf_op jit(solution)/shard_map/psum | solution.py:95
  7.2 0.7 copy-start.10
  109.0 31.2 %all-to-all-start = ((bf16[32,3,16,512]{3,2,1,0:T(8,128)(2,1)}), bf16[32,3,16,512]{3,2,1,0:T(8,128)(2,1)S(1)}, u32[]{:S(2)}, u32[]{:S(2)}) async-start(bf16[32,3,16,512]{3,2,1,0:T(8,128)(2,1)} %select_select_fusion), calls=%async_computation | async-start | bytes 3145728 | tf_op jit(solution)/shard_map/all_to_all | solution.py:103
  116.3 3.2 %copy-start.8 = (bf16[1,1,3,512,512]{4,3,2,1,0:T(8,128)(2,1)S(1)}, bf16[1,1,3,512,512]{4,3,2,1,0:T(8,128)(2,1)}, u32[]{:S(2)}) copy-start(bf16[1,1,3,512,512]{4,3,2,1,0:T(8,128)(2,1)} %param.11) | copy-start | bytes 4718596
  116.3 3.2 %copy-start.9 = (bf16[1,1,3,512,512]{4,3,2,1,0:T(8,128)(2,1)S(1)}, bf16[1,1,3,512,512]{4,3,2,1,0:T(8,128)(2,1)}, u32[]{:S(2)}) copy-start(bf16[1,1,3,512,512]{4,3,2,1,0:T(8,128)(2,1)} %param.10) | copy-start | bytes 4718596
  140.2 1.2 copy-start.1
  141.4 2.4 %copy-start.6 = (f32[1,1,3,512,512]{4,3,2,1,0:T(8,128)S(1)}, f32[1,1,3,512,512]{4,3,2,1,0:T(8,128)}, u32[]{:S(2)}) copy-start(f32[1,1,3,512,512]{4,3,2,1,0:T(8,128)} %param.8) | copy-start | bytes 9437188
  143.8 1.9 copy-start.7
  145.1 1.9 copy-start.3
  147.0 1.7 copy-start.4
  147.1 2.0 copy-start
  156.9 4.0 %copy-start.5 = (f32[512,512]{1,0:T(8,128)S(1)}, f32[512,512]{1,0:T(8,128)}, u32[]{:S(2)}) copy-start(f32[512,512]{1,0:T(8,128)} %fusion.33) | copy-start | bytes 3145732
  169.9 5.4 %copy-start.2 = (bf16[32,3,16,512]{3,2,1,0:T(8,128)(2,1)S(1)}, bf16[32,3,16,512]{3,2,1,0:T(8,128)(2,1)}, u32[]{:S(2)}) copy-start(bf16[32,3,16,512]{3,2,1,0:T(8,128)(2,1)} %copy-done.1) | copy-start | bytes 4718596
  179.5 27.9 %all-to-all-start.1 = ((bf16[3,32,16,512]{3,2,0,1:T(8,128)(2,1)}), bf16[3,32,16,512]{3,2,0,1:T(8,128)(2,1)S(1)}, u32[]{:S(2)}, u32[]{:S(2)}) async-start(bf16[3,32,16,512]{3,2,0,1:T(8,128)(2,1)} %copy.25), calls=%async_computation.1 | async-start | bytes 3145728 | tf_op jit(solution)/shard_map/all_to_all | solution.py:111
Sparse Core Ops, SparseCore 0:
  10.4 95.1 all-reduce.1
where the time goes:
time: 216 us
  waiting for transfers between devices  140 us (65%)
  matrix products  27.4 us (13%)
  between operations  14.3 us (7%)
  other arithmetic  11.6 us (5%)
  local copies, waits for them, and re-layouts  11.4 us (5%)
  starting transfers between devices  11.3 us (5%)
    psum x1, waiting for transfers between devices, on_device(): lax.psum(local_grads.astype(jnp.float32).astype(jnp.bfloat16), 'rep')  96.3 us
    all_to_all x1, waiting for transfers between devices, on_device(): lax.all_to_all(sending, 'fsdp', split_axis=1, concat_axis=0, tiled=True)  23.8 us
    dot_general x5, matrix products, batch_mul(): jnp.einsum('bij,bjk->bik', left_mat, right_mat, precision=lax.Precision.H...  19.3 us
    all_to_all x1, waiting for transfers between devices, on_device(): lax.all_to_all(outgoing, 'fsdp', split_axis=0, concat_axis=2, tiled=True)  19.2 us
    all_to_all x1, starting transfers between devices, on_device(): lax.all_to_all(outgoing, 'fsdp', split_axis=0, concat_axis=2, tiled=True)  7.26 us
    dot_general x1, matrix products, refresh(): jnp.einsum('sij,sjk->sik', left_use, right_applied, preferred_element_typ...  5.42 us
  transfers between devices with their start and end apart: 3, of which 3 were waited for; matrix products, arithmetic and copies ran while one was open for 3% of the time, Pallas kernels for 0%

commit v1 on v0

v1 whole, which is shorter than its diff:
```python
import functools

import jax
import jax.numpy as jnp
from jax import lax
from jax.experimental import pallas as pl
from jax.experimental.pallas import tpu as pltpu
from jax.sharding import PartitionSpec as P

DECAY_RATE = 0.9
ROOT_RIDGE = 1e-06
GRAFT_EPS = 1e-12
NORM_EPS = 1e-12
MOST = 3

ROOT_POLY = (
    25.0 / 16.0,
    -5.0 / 16.0 - 3125.0 / 4096.0,
    3125.0 / 4096.0,
    -1250.0 / 4096.0,
    250.0 / 4096.0,
    -25.0 / 4096.0,
    1.0 / 4096.0,
)

VMEM_LIMIT = 40 * 1024 * 1024
VMEM_MOST = 48 * 1024 * 1024
VMEM = pltpu.VMEM
HBM = pltpu.HBM
SMEM = pltpu.SMEM


def mul(left, right, dims=((1,), (0,))):
    return lax.dot_general(left, right, (dims, ((), ())), preferred_element_type=jnp.float32)


def blend(live, prev, gram):
    return jnp.where(live, DECAY_RATE * prev + (1.0 - DECAY_RATE) * gram, prev)


ROWS = 64
COLS = 128


def tiles(side):
    return [
        (slice(row, row + ROWS), slice(col, col + COLS))
        for row in range(0, side, ROWS)
        for col in range(0, side, COLS)
    ]


def plus_diag(tile, rows, cols, value):
    if rows.start // COLS != cols.start // COLS:
        return tile
    row_ids = lax.broadcasted_iota(jnp.int32, tile.shape, 0) + rows.start
    col_ids = lax.broadcasted_iota(jnp.int32, tile.shape, 1) + cols.start
    return tile + jnp.where(row_ids == col_ids, value, 0.0).astype(tile.dtype)


def total(parts):
    return jnp.sum(functools.reduce(lambda x, y: x + y, parts), keepdims=True)


def cost(matmuls, side, nbytes):
    return pl.CostEstimate(flops=matmuls * 2 * side**3, bytes_accessed=nbytes, transcendentals=0)


def place_kernel(place_ref, empty_ref, front_ref, up_ref, back_ref, down_ref, out_ref, sums, zeros, sem):
    half = front_ref.shape[0]
    zeros[...] = jnp.zeros_like(zeros)

    def blank(place, carry):
        @pl.when(empty_ref[place] > 0)
        def _():
            pltpu.make_async_copy(zeros, out_ref.at[place], sem).start()

        return carry

    def put(block):
        pltpu.make_async_copy(sums.at[block], out_ref.at[place_ref[block]], sem).start()

    def add(j, carry):
        sums[j] = (front_ref[j] + up_ref[j].astype(jnp.float32)).astype(jnp.bfloat16)
        put(j)
        sums[half + j] = (back_ref[j] + down_ref[j].astype(jnp.float32)).astype(jnp.bfloat16)
        put(half + j)
        return carry

    lax.fori_loop(0, half, add, 0, unroll=4)
    lax.fori_loop(0, out_ref.shape[0], blank, 0, unroll=4)
    pltpu.make_async_copy(out_ref, out_ref, sem).wait()


def place_blocks(place, empty, front, up, back, down):
    half, rows, cols = front.shape
    scalars = pl.BlockSpec(memory_space=SMEM)
    return pl.pallas_call(
        place_kernel,
        out_shape=jax.ShapeDtypeStruct((empty.shape[0], rows, cols), jnp.bfloat16),
        in_specs=[scalars] * 2 + [pl.BlockSpec(memory_space=VMEM)] * 4,
        out_specs=pl.BlockSpec(memory_space=HBM),
        scratch_shapes=[
            VMEM((2 * half, rows, cols), jnp.bfloat16),
            VMEM((rows, cols), jnp.bfloat16),
            pltpu.SemaphoreType.DMA(()),
        ],
        compiler_params=pltpu.CompilerParams(vmem_limit_bytes=VMEM_LIMIT),
        cost_estimate=cost(0, 0, 8 * half * rows * cols * 2),
        name="place_blocks",
    )(place, empty, front, up, back, down)


def precondition_kernel(
    live_ref, arrived, left_stats, right_stats, left_roots, right_roots, _, out, left_new, right_new,
    done_ref, stats, roots, results, wide, prod, raws, low, square, term, in_sems, out_sems,
):
    side = stats.shape[-1]
    entries = side * side
    f32, bf16 = jnp.float32, jnp.bfloat16
    c0, c1, c2, c3, c4, c5, c6 = ROOT_POLY
    grid = tiles(side)
    fetch = {}

    def get(name, source, target):
        fetch[name] = pltpu.make_async_copy(source, target, in_sems.at[len(fetch)])
        fetch[name].start()

    for slot in range(1, MOST):
        get("r%d" % slot, right_roots.at[0, 0, slot], roots.at[2 * slot - 1])
        get("l%d" % slot, left_roots.at[0, 0, slot], roots.at[2 * slot - 2])
    get("left", left_stats.at[0, 0, 0], stats.at[0])
    get("right", right_stats.at[0, 0, 0], stats.at[1])

    def block_of(slot):
        return arrived[:, slot].reshape(side, side)

    def give(number, target):
        copy = pltpu.make_async_copy(results.at[number], target, out_sems.at[number])
        copy.start()
        return copy

    def put(number, rows, cols, tile):
        slabs = slice(rows.start // 16, rows.stop // 16)
        results[number, slabs, :, cols] = tile.reshape(ROWS // 16, 16, COLS)

    def power(tile_of):
        return total([jnp.square(tile_of(rows, cols)) for rows, cols in grid]) * (1.0 / entries)

    def graft(slot, block, raw):
        grad_power = power(lambda rows, cols: block[rows, cols].astype(f32))
        scale = jnp.sqrt(grad_power) / jnp.sqrt(power(lambda rows, cols: raw[rows, cols]) + GRAFT_EPS)
        for rows, cols in grid:
            put(slot, rows, cols, (raw[rows, cols] * scale).astype(bf16))

    block = block_of(0)
    others = [block_of(slot) for slot in range(1, MOST)]
    wide[0] = mul(block, block, ((1,), (1,)))
    wide[1] = mul(block, block, ((0,), (0,)))
    for i in range(MOST - 1):
        fetch["r%d" % (i + 1)].wait()
        raws[i] = mul(others[i], roots[2 * i + 1])
    for i in range(MOST - 1):
        for rows, cols in grid:
            square[i, rows, cols] = raws[i, rows, cols].astype(bf16)
        fetch["l%d" % (i + 1)].wait()
        raws[i] = mul(roots[2 * i], square[i])
    sent = []
    live = live_ref[0] > 0
    keep = jnp.where(live, DECAY_RATE, 1.0)
    take = jnp.where(live, 1.0 - DECAY_RATE, 0.0)
    scales = []
    for i, name in enumerate(("left", "right")):
        fetch[name].wait()
        squares = []
        for rows, cols in grid:
            tile = keep * stats[i, rows, cols] + take * wide[i, rows, cols]
            tile = plus_diag(tile, rows, cols, ROOT_RIDGE)
            low[i, rows, cols] = tile.astype(bf16)
            squares.append(tile * tile)
        frob = side * jnp.sqrt(total(squares) * (1.0 / entries) + NORM_EPS)
        scales.append(2.5 / frob)
        prod[i] = mul(low[i], low[i])
        graft(i + 1, others[i], raws.at[i])
        sent.append(give(i + 1, out.at[:, i + 1]))
    for i in range(2):
        one, two = scales[i], scales[i] * scales[i]
        for rows, cols in grid:
            tile = prod[i, rows, cols].astype(bf16)
            square[i, rows, cols] = tile
            tile = (c5 * one).astype(bf16) * low[i, rows, cols] + (c6 * two).astype(bf16) * tile
            term[i, rows, cols] = plus_diag(tile, rows, cols, c4)
        prod[i] = mul(square[i], term[i])
    for i in range(2):
        one, two = scales[i], scales[i] * scales[i]
        for rows, cols in grid:
            tile = (two * prod[i, rows, cols]).astype(bf16) + (c3 * one).astype(bf16) * low[i, rows, cols]
            term[i, rows, cols] = plus_diag(tile, rows, cols, c2)
        prod[i] = mul(square[i], term[i])
    for i in (1, 0):
        one, two = scales[i], scales[i] * scales[i]
        for rows, cols in grid:
            tile = two * prod[i, rows, cols] + (c1 * one) * low[i, rows, cols].astype(f32)
            tile = plus_diag(tile, rows, cols, c0).astype(bf16)
            term[i, rows, cols] = tile
            put(MOST + i, rows, cols, tile)
    sent += [give(MOST, left_new), give(MOST + 1, right_new)]
    prod[0] = mul(block, term[1])
    for rows, cols in grid:
        low[0, rows, cols] = prod[0, rows, cols].astype(bf16)
    prod[1] = mul(term[0], low[0])
    graft(0, block, prod.at[1])
    sent.append(give(0, out.at[:, 0]))
    for copy in sent:
        copy.wait()
    done_ref[0] = 0


def precondition(live, arrived, left_stats, right_stats, left_roots, right_roots, spent):
    owners, _, rows, side = arrived.shape
    root = jax.ShapeDtypeStruct((owners, rows, side), jnp.bfloat16)
    far = pl.BlockSpec(memory_space=HBM)
    return pl.pallas_call(
        precondition_kernel,
        out_shape=[
            jax.ShapeDtypeStruct((owners, MOST, rows, side), jnp.bfloat16), root, root, token_shape(),
        ],
        in_specs=[pl.BlockSpec(memory_space=SMEM), pl.BlockSpec(memory_space=VMEM)] + [far] * 5,
        out_specs=[far] * 3 + [pl.BlockSpec(memory_space=SMEM)],
        scratch_shapes=[
            VMEM((2, side, side), jnp.float32),
            VMEM((2 * MOST - 2, side, side), jnp.bfloat16),
            VMEM((MOST + 2, owners, rows, side), jnp.bfloat16),
            VMEM((2, side, side), jnp.float32),
            VMEM((2, side, side), jnp.float32),
            VMEM((2, side, side), jnp.float32),
            VMEM((2, side, side), jnp.bfloat16),
            VMEM((2, side, side), jnp.bfloat16),
            VMEM((2, side, side), jnp.bfloat16),
            pltpu.SemaphoreType.DMA((2 * MOST,)),
            pltpu.SemaphoreType.DMA((MOST + 2,)),
        ],
        compiler_params=pltpu.CompilerParams(vmem_limit_bytes=VMEM_MOST),
        cost_estimate=cost(14, side, 9 * side * side * 4),
        input_output_aliases={6: 0},
        name="precondition",
    )(live, arrived, left_stats, right_stats, left_roots, right_roots, spent)


def stats_kernel(live_ref, block_ref, lprev_ref, rprev_ref, _, left_ref, right_ref):
    side = lprev_ref.shape[-1]
    block = block_ref[:, 0].reshape(side, side)
    live = live_ref[pl.program_id(0)] > 0
    left_ref[0, 0, 0] = blend(live, lprev_ref[0, 0, 0], mul(block, block, ((1,), (1,))))
    right_ref[0, 0, 0] = blend(live, rprev_ref[0, 0, 0], mul(block, block, ((0,), (0,))))


def update_stats(live, arrived, left_stats, right_stats, tied):
    owners, _, rows, side = arrived.shape
    at_slot = pl.BlockSpec((1, 1, 1, side, side), lambda s: (0, 0, s, 0, 0))
    shape = jax.ShapeDtypeStruct(left_stats.shape, jnp.float32)
    return pl.pallas_call(
        stats_kernel,
        grid=(MOST,),
        out_shape=[shape, shape],
        in_specs=[pl.BlockSpec(memory_space=SMEM)]
        + [pl.BlockSpec((owners, 1, rows, side), lambda s: (0, s, 0, 0))]
        + [at_slot, at_slot, pl.BlockSpec(memory_space=SMEM)],
        out_specs=[at_slot, at_slot],
        compiler_params=pltpu.CompilerParams(vmem_limit_bytes=VMEM_MOST),
        cost_estimate=cost(2 * MOST, side, 13 * side * side * 4),
        name="update_stats",
    )(live, arrived, left_stats, right_stats, tied)


def assemble_kernel(slot_ref, owner_ref, back_ref, out_ref, sem):
    count = out_ref.shape[0]

    def start(b, carry):
        pltpu.make_async_copy(back_ref.at[owner_ref[b], slot_ref[b]], out_ref.at[b], sem).start()
        return carry

    lax.fori_loop(0, count, start, 0, unroll=8)
    pltpu.make_async_copy(out_ref, out_ref, sem).wait()


def assemble(slot_of, owner_of, back):
    count = slot_of.shape[0]
    rows, cols = back.shape[2:]
    return pl.pallas_call(
        assemble_kernel,
        out_shape=jax.ShapeDtypeStruct((count, rows, cols), jnp.bfloat16),
        in_specs=[pl.BlockSpec(memory_space=SMEM)] * 2 + [pl.BlockSpec(memory_space=pl.ANY)],
        out_specs=pl.BlockSpec(memory_space=HBM),
        scratch_shapes=[pltpu.SemaphoreType.DMA(())],
        compiler_params=pltpu.CompilerParams(vmem_limit_bytes=VMEM_LIMIT),
        cost_estimate=cost(0, 0, 2 * count * rows * cols * 2),
        name="assemble",
    )(slot_of, owner_of, back)


def token_shape():
    return jax.ShapeDtypeStruct((1,), jnp.int32)


def routing(owner, owners):
    ids = jnp.arange(owner.shape[0], dtype=jnp.int32)
    same = owner[:, None] == owner[None, :]
    slot = jnp.sum((same & (ids[None, :] < ids[:, None])).astype(jnp.int32), axis=1)
    place = owner * MOST + slot
    taken = place[None, :] == jnp.arange(owners * MOST, dtype=jnp.int32)[:, None]
    return slot, place, 1 - jnp.sum(taken.astype(jnp.int32), axis=1)


def on_device(grads, owner_table, left_stats, right_stats, left_roots, right_roots):
    groups = lax.axis_size("rep")
    owners = lax.axis_size("fsdp")
    group_id = lax.axis_index("rep")
    owner_id = lax.axis_index("fsdp")
    local = grads[0]
    total_blocks, slab_rows, side = local.shape
    share = total_blocks // groups
    half = share // 2
    up = [(i, (i + 1) % groups) for i in range(groups)]
    down = [(i, (i - 1) % groups) for i in range(groups)]

    owner = lax.dynamic_slice_in_dim(owner_table[:, 0], group_id * share, share)
    slot, place, empty = routing(owner, owners)
    own_count = jnp.sum((owner == owner_id).astype(jnp.int32))
    live = (jnp.arange(MOST, dtype=jnp.int32) < own_count).astype(jnp.int32)

    def part(source, ahead, low):
        start = (group_id + ahead) % groups * share + low
        return lax.dynamic_slice_in_dim(source, start, half, 0)

    send_up1, send_down1 = part(local, 2, 0), part(local, 2, half)
    up1 = lax.ppermute(send_up1, "rep", up)
    down1 = lax.ppermute(send_down1, "rep", down)
    later, _, _ = lax.optimization_barrier((local, send_up1, send_down1))
    up2 = lax.ppermute(part(later, 1, half), "rep", up)
    down2 = lax.ppermute(part(later, 3, 0), "rep", down)
    up3 = lax.ppermute(part(local, 1, 0) + up1, "rep", up)
    down3 = lax.ppermute(part(local, 3, half) + down1, "rep", down)
    front = part(local, 0, 0).astype(jnp.float32) + down2.astype(jnp.float32)
    back = part(local, 0, half).astype(jnp.float32) + up2.astype(jnp.float32)

    outgoing = place_blocks(place, empty, front, up3, back, down3)
    outgoing = outgoing.reshape(owners, MOST, slab_rows, side)
    arrived = lax.all_to_all(outgoing, "fsdp", split_axis=0, concat_axis=0, tiled=True)
    results, left_new, right_new, done = precondition(
        live, arrived, left_stats, right_stats, left_roots, right_roots, outgoing
    )
    returned = lax.all_to_all(results, "fsdp", split_axis=0, concat_axis=0, tiled=True)
    left_out, right_out = update_stats(live, arrived, left_stats, right_stats, done)
    preconditioned = assemble(slot, owner, returned)
    return (
        preconditioned,
        left_out,
        right_out,
        left_new.reshape(1, 1, side, side),
        right_new.reshape(1, 1, side, side),
    )


def solution(mesh):
    in_specs = (
        P("rep", None, "fsdp", None),
        P(),
        P("rep", "fsdp", None, None, None),
        P("rep", "fsdp", None, None, None),
        P("rep", "fsdp", None, None, None),
        P("rep", "fsdp", None, None, None),
    )
    out_specs = (
        P("rep", "fsdp", None),
        P("rep", "fsdp", None, None, None),
        P("rep", "fsdp", None, None, None),
        P("rep", "fsdp", None, None),
        P("rep", "fsdp", None, None),
    )
    return jax.shard_map(
        on_device, mesh=mesh, in_specs=in_specs, out_specs=out_specs, check_vma=False
    )
```

time: 216 us -> 115 us (0.53)
  waiting for transfers between devices: 140 us -> 64.2 us
  matrix products: 27.4 us -> 0 us
  Pallas kernels: 0 us -> 19.1 us
  between operations: 14.3 us -> 0.79 us
  starting transfers between devices: 11.3 us -> 20.7 us
  other arithmetic: 11.6 us -> 4.55 us
  local copies, waits for them, and re-layouts: 11.4 us -> 5.41 us
    psum x1 -> x0, waiting for transfers between devices: 96.3 us -> none  [on_device(): lax.psum(local_grads.astype(jnp.float32).astype(jnp.bfloat16), 'rep')]
    dot_general x8 -> x0, matrix products: 27.4 us -> none  [the longest x5 19.3 us: batch_mul(): jnp.einsum('bij,bjk->bik', left_mat, right_mat, precision=lax.Precision.H...]
    ppermute x0 -> x6, waiting for transfers between devices: none -> 25.5 us  [the longest x1 7.81 us: on_device(): up2 = lax.ppermute(part(later, 1, half), 'rep', up)]
    pallas_call x0 -> x4, Pallas kernels: none -> 19.1 us  [the longest x1 9.27 us: precondition(): pl.pallas_call(precondition_kernel, out_shape=[jax.ShapeDtypeStruct((owne...]
    ppermute x0 -> x6, starting transfers between devices: none -> 8.23 us  [the longest x1 2.91 us: on_device(): down1 = lax.ppermute(send_down1, 'rep', down)]
    all_to_all x2, waiting for transfers between devices: 43.1 us -> 38.7 us  [the longest x1 23.3 us: on_device(): lax.all_to_all(outgoing, 'fsdp', split_axis=0, concat_axis=0, tiled=True)]
    convert_element_type x3 -> x1, other arithmetic: 4.76 us -> 0.65 us  [on_device(): live = (jnp.arange(MOST, dtype=jnp.int32) < own_count).astype(jnp.int32)]
    dynamic_slice x0 -> x2, local copies, waits for them, and re-layouts: none -> 3.51 us  [part(): return lax.dynamic_slice_in_dim(source, start, half, 0)]
  transfers between devices with their start and end apart: 3 -> 8, of which waited for: 3 -> 7; matrix products, arithmetic and copies ran while one was open for 3% -> 6% of each run, Pallas kernels for 0% -> 6%
where the time goes in v1:
time: 115 us
  waiting for transfers between devices  64.2 us (56%)
  starting transfers between devices  20.7 us (18%)
  Pallas kernels  19.1 us (17%)
  local copies, waits for them, and re-layouts  5.41 us (5%)
  other arithmetic  4.55 us (4%)
    all_to_all x1, waiting for transfers between devices, on_device(): lax.all_to_all(outgoing, 'fsdp', split_axis=0, concat_axis=0, tiled=True)  23.3 us
    all_to_all x1, waiting for transfers between devices, on_device(): lax.all_to_all(results, 'fsdp', split_axis=0, concat_axis=0, tiled=True)  15.4 us
    pallas_call x1, Pallas kernels, precondition(): pl.pallas_call(precondition_kernel, out_shape=[jax.ShapeDtypeStruct((owne...  9.27 us
    all_to_all x1, starting transfers between devices, on_device(): lax.all_to_all(outgoing, 'fsdp', split_axis=0, concat_axis=0, tiled=True)  8.48 us
    ppermute x1, waiting for transfers between devices, on_device(): up2 = lax.ppermute(part(later, 1, half), 'rep', up)  7.81 us
    pallas_call x1, Pallas kernels, update_stats(): pl.pallas_call(stats_kernel, grid=(MOST,), out_shape=[shape, shape], in_s...  6.63 us
    ppermute x1, waiting for transfers between devices, on_device(): down1 = lax.ppermute(send_down1, 'rep', down)  5.83 us
    ppermute x1, waiting for transfers between devices, on_device(): down3 = lax.ppermute(part(local, 3, half) + down1, 'rep', down)  4.76 us
  transfers between devices with their start and end apart: 8, of which 7 were waited for; matrix products, arithmetic and copies ran while one was open for 6% of the time, Pallas kernels for 6%

profile of v1, /device:TPU:0, one launch (start us, length us, event | category | flops | bytes accessed | tf_op | source)
XLA Modules:
  0.0 114.8 jit_solution(3474410766680314541)
XLA Ops:
  0.6 0.0 copy-start.2
  0.7 1.3 %dynamic-slice_bitcast_fusion = (bf16[32,16,512]{2,1,0:T(8,128)(2,1)S(1)}, bf16[32,16,512]{2,1,0:T(8,128)(2,1)S(1)}) fusion(bf16[1,256,16,512]{3,2,1,0:T(8,128)(2,1)} %param.6, s32[]{:T(128)S(6)} %select_n.59, s32[]{:T(128)S(6)} %select_n.58), kind=kLoop, calls=%fused_computation.4 | loop fusion | bytes 2097160 | tf_op jit(solution)/shard_map/dynamic_slice | solution.py:334
  1.9 2.9 %collective-permute-start.4 = (bf16[32,16,512]{2,1,0:T(8,128)(2,1)S(1)}, bf16[32,16,512]{2,1,0:T(8,128)(2,1)S(1)}, u32[]{:S(2)}, u32[]{:S(2)}) collective-permute-start(bf16[32,16,512]{2,1,0:T(8,128)(2,1)S(1)} %get-tuple-element.27), channel_id=1, source_target_pairs={{0,96},{32,0},{64,32},{96,64},{1,97},{33,1},{65,33},{97,65},{2,98}... | collective-permute-start | bytes 1572872 | tf_op jit(solution)/shard_map/ppermute | solution.py:338
  4.9 0.0 collective-permute-start.1
  4.9 2.2 %constant_dynamic-slice_fusion = (bf16[32,16,512]{2,1,0:T(8,128)(2,1)}, bf16[32,16,512]{2,1,0:T(8,128)(2,1)}) fusion(bf16[256,16,512]{2,1,0:T(8,128)(2,1)} %bitcast.21, s32[]{:T(128)S(6)} %select_n.65, s32[]{:T(128)S(6)} %select_n.61), kind=kLoop, calls=%fused_computation.11 | loop fusion | bytes 2097160 | tf_op jit(solution)/shard_map/dynamic_slice | solution.py:334
  7.1 0.8 collective-permute-start.3
  7.8 2.5 %collective-permute-start = (bf16[32,16,512]{2,1,0:T(8,128)(2,1)}, bf16[32,16,512]{2,1,0:T(8,128)(2,1)S(1)}, u32[]{:S(2)}, u32[]{:S(2)}) collective-permute-start(bf16[32,16,512]{2,1,0:T(8,128)(2,1)} %get-tuple-element.26), channel_id=1, source_target_pairs={{0,96},{32,0},{64,32},{96,64},{1,97},{33,1},{65,33},{97,65},{2,98}... | collective-permute-start | bytes 1572872 | tf_op jit(solution)/shard_map/ppermute | solution.py:341
  10.3 0.7 fusion.1
  11.0 0.2 convert_reduce_fusion.1.slot_ref
  11.2 0.1 convert_reduce_fusion
  11.4 5.8 %collective-permute-done.4 = bf16[32,16,512]{2,1,0:T(8,128)(2,1)S(1)} collective-permute-done((bf16[32,16,512]{2,1,0:T(8,128)(2,1)S(1)}, bf16[32,16,512]{2,1,0:T(8,128)(2,1)S(1)}, u32[]{:S(2)}, u32[]{:S(2)}) %collective-permute-start.4) | collective-permute-done | bytes 524320 | tf_op jit(solution)/shard_map/ppermute | solution.py:338
  17.2 3.7 %collective-permute-done.1 = bf16[32,16,512]{2,1,0:T(8,128)(2,1)S(1)} collective-permute-done((bf16[32,16,512]{2,1,0:T(8,128)(2,1)S(1)}, bf16[32,16,512]{2,1,0:T(8,128)(2,1)S(1)}, u32[]{:S(2)}, u32[]{:S(2)}) %collective-permute-start.1) | collective-permute-done | bytes 524320 | tf_op jit(solution)/shard_map/ppermute | solution.py:337
  20.9 1.3 %bitcast_add_fusion = (bf16[32,16,512]{2,1,0:T(8,128)(2,1)S(1)}, bf16[32,16,512]{2,1,0:T(8,128)(2,1)S(1)}) fusion(bf16[32,16,512]{2,1,0:T(8,128)(2,1)S(1)} %collective-permute-done.4, bf16[1,256,16,512]{3,2,1,0:T(8,128)(2,1)} %param.6, s32[]{:T(128)S(6)} %select_n.66, bf16[32,16,512]{2,1,0:T(8,128)(2,1)S(1)} %collective-permute-done.1, s32[]{:T(128)S(6)} %select_n.63), kind=kLoop, calls=%fused_computation.2 | loop fusion | flops 524288 | bytes 3145736 | tf_op jit(solution)/shard_map/add | solution.py:343
  22.2 0.1 collective-permute-start.5
  22.3 2.0 %collective-permute-start.2 = (bf16[32,16,512]{2,1,0:T(8,128)(2,1)S(1)}, bf16[32,16,512]{2,1,0:T(8,128)(2,1)S(1)}, u32[]{:S(2)}, u32[]{:S(2)}) collective-permute-start(bf16[32,16,512]{2,1,0:T(8,128)(2,1)S(1)} %get-tuple-element.22), channel_id=1, source_target_pairs={{0,32},{32,64},{64,96},{96,0},{1,33},{33,65},{65,97},{97,1},{2,34}... | collective-permute-start | bytes 1572872 | tf_op jit(solution)/shard_map/ppermute | solution.py:342
  24.3 7.8 %collective-permute-done.3 = bf16[32,16,512]{2,1,0:T(8,128)(2,1)S(1)} collective-permute-done((bf16[32,16,512]{2,1,0:T(8,128)(2,1)}, bf16[32,16,512]{2,1,0:T(8,128)(2,1)S(1)}, u32[]{:S(2)}, u32[]{:S(2)}) %collective-permute-start.3) | collective-permute-done | bytes 524320 | tf_op jit(solution)/shard_map/ppermute | solution.py:340
  32.1 0.0 collective-permute-done
  32.2 1.6 %convert_add_fusion = (f32[32,16,512]{2,1,0:T(8,128)S(1)}, f32[32,16,512]{2,1,0:T(8,128)S(1)}) fusion(bf16[32,16,512]{2,1,0:T(8,128)(2,1)S(1)} %collective-permute-done.3, bf16[1,256,16,512]{3,2,1,0:T(8,128)(2,1)} %param.6, s32[]{:T(128)S(6)} %select_n.64, bf16[32,16,512]{2,1,0:T(8,128)(2,1)S(1)} %collective-permute-done, s32[]{:T(128)S(6)} %select_n.56), kind=kLoop, calls=%fused_computation | loop fusion | flops 1572864 | bytes 4194312 | tf_op jit(solution)/shard_map/add | solution.py:345
  33.7 4.8 %collective-permute-done.5.down_ref = bf16[32,16,512]{2,1,0:T(8,128)(2,1)S(1)} collective-permute-done((bf16[32,16,512]{2,1,0:T(8,128)(2,1)S(1)}, bf16[32,16,512]{2,1,0:T(8,128)(2,1)S(1)}, u32[]{:S(2)}, u32[]{:S(2)}) %collective-permute-start.5) | collective-permute-done | bytes 524320 | tf_op jit(solution)/shard_map/ppermute | solution.py:343
  38.5 3.4 %collective-permute-done.2.up_ref = bf16[32,16,512]{2,1,0:T(8,128)(2,1)S(1)} collective-permute-done((bf16[32,16,512]{2,1,0:T(8,128)(2,1)S(1)}, bf16[32,16,512]{2,1,0:T(8,128)(2,1)S(1)}, u32[]{:S(2)}, u32[]{:S(2)}) %collective-permute-start.2) | collective-permute-done | bytes 524320 | tf_op jit(solution)/shard_map/ppermute | solution.py:342
  41.9 1.7 %place_blocks.1 = bf16[96,16,512]{2,1,0:T(8,128)(2,1)} custom-call(s32[64]{0:T(128)S(1)} %multiply_add_fusion.place_ref, s32[96]{0:T(128)S(1)} %broadcast_subtract_fusion.empty_ref, f32[32,16,512]{2,1,0:T(8,128)S(1)} %get-tuple-element.24.front_ref, bf16[32,16,512]{2,1,0:T(8,128)(2,1)S(1)} %collective-permute-done.2.up_ref, ...), custom_call_target="tpu_custom_call" | custom-call | bytes 4194304 | tf_op jit(solution)/shard_map/place_blocks/pallas_call | solution.py:98
  43.7 0.0 copy-start.1
  43.7 8.5 %all-to-all-start = ((bf16[32,3,16,512]{3,2,1,0:T(8,128)(2,1)}), bf16[32,3,16,512]{3,2,1,0:T(8,128)(2,1)S(1)}, u32[]{:S(2)}, u32[]{:S(2)}) async-start(bf16[32,3,16,512]{3,2,1,0:T(8,128)(2,1)} %bitcast.8._), calls=%async_computation | async-start | bytes 3145728 | tf_op jit(solution)/shard_map/all_to_all | solution.py:349
  52.2 0.7 compare_convert_fusion.live_ref
  52.8 23.3 %all-to-all-done.arrived.block_ref = bf16[32,3,16,512]{3,2,1,0:T(8,128)(2,1)S(1)} async-done(((bf16[32,3,16,512]{3,2,1,0:T(8,128)(2,1)}), bf16[32,3,16,512]{3,2,1,0:T(8,128)(2,1)S(1)}, u32[]{:S(2)}, u32[]{:S(2)}) %all-to-all-start) | async-done | bytes 1572896 | tf_op jit(solution)/shard_map/all_to_all | solution.py:349
  76.1 9.3 %precondition.1 = (bf16[32,3,16,512]{3,2,1,0:T(8,128)(2,1)}, bf16[32,16,512]{2,1,0:T(8,128)(2,1)}, bf16[32,16,512]{2,1,0:T(8,128)(2,1)}, s32[1]{0:T(128)}) custom-call(s32[3]{0:T(128)S(1)} %compare_convert_fusion.live_ref, bf16[32,3,16,512]{3,2,1,0:T(8,128)(2,1)S(1)} %all-to-all-done.arrived.block_ref, ...), custom_call_target="tpu_custom_call", output_to_operand_aliasing={{0}: (6, {})} | custom-call | flops 3758096384 | bytes 9437184 | tf_op jit(solution)/shard_map/precondition/pallas_call | solution.py:223
  85.4 4.0 %all-to-all-start.1 = ((bf16[32,3,16,512]{3,2,1,0:T(8,128)(2,1)}), bf16[32,3,16,512]{3,2,1,0:T(8,128)(2,1)S(1)}, u32[]{:S(2)}, u32[]{:S(2)}) async-start(bf16[32,3,16,512]{3,2,1,0:T(8,128)(2,1)} %get-tuple-element.13), calls=%async_computation.1 | async-start | bytes 3145728 | tf_op jit(solution)/shard_map/all_to_all | solution.py:353
  89.4 0.0 copy-start
  89.4 1.9 %copy-done = f32[1,1,3,512,512]{4,3,2,1,0:T(8,128)S(1)} copy-done((f32[1,1,3,512,512]{4,3,2,1,0:T(8,128)S(1)}, f32[1,1,3,512,512]{4,3,2,1,0:T(8,128)}, u32[]{:S(2)}) %copy-start) | copy-done | bytes 3145752
  91.2 6.6 %update_stats.1 = (f32[1,1,3,512,512]{4,3,2,1,0:T(8,128)}, f32[1,1,3,512,512]{4,3,2,1,0:T(8,128)}) custom-call(s32[3]{0:T(128)S(1)} %compare_convert_fusion.live_ref, bf16[32,3,16,512]{3,2,1,0:T(8,128)(2,1)S(1)} %all-to-all-done.arrived.block_ref, f32[1,1,3,512,512]{4,3,2,1,0:T(8,128)S(1)} %copy-done, f32[1,1,3,512,512]{4,3,2,1,0:T(8,128)} %rprev_ref.1, ...), custom_call_target="tpu_custom_call" | custom-call | flops 1610612736 | bytes 13631488 | tf_op jit(solution)/shard_map/update_stats/pallas_call | solution.py:262
  97.9 15.4 %all-to-all-done.1.back_ref = bf16[32,3,16,512]{3,2,1,0:T(8,128)(2,1)S(1)} async-done(((bf16[32,3,16,512]{3,2,1,0:T(8,128)(2,1)}), bf16[32,3,16,512]{3,2,1,0:T(8,128)(2,1)S(1)}, u32[]{:S(2)}, u32[]{:S(2)}) %all-to-all-start.1) | async-done | bytes 1572896 | tf_op jit(solution)/shard_map/all_to_all | solution.py:353
  113.3 1.5 %assemble.1 = bf16[64,16,512]{2,1,0:T(8,128)(2,1)} custom-call(s32[64]{0:T(128)S(1)} %convert_reduce_fusion.1.slot_ref, s32[64]{0:T(128)S(1)} %get-tuple-element.20.owner_ref, bf16[32,3,16,512]{3,2,1,0:T(8,128)(2,1)S(1)} %all-to-all-done.1.back_ref), custom_call_target="tpu_custom_call" | custom-call | bytes 2097152 | tf_op jit(solution)/shard_map/assemble/pallas_call | solution.py:290
  (4 shorter events, 0.0 us)
Async XLA Ops:
  0.6 9.7 %copy-start.2 = (s32[256,1]{0,1:T(1,128)S(1)}, s32[256,1]{0,1:T(1,128)}, u32[]{:S(2)}) copy-start(s32[256,1]{0,1:T(1,128)} %param.7) | copy-start | bytes 3076
  1.9 15.2 %collective-permute-start.4 = (bf16[32,16,512]{2,1,0:T(8,128)(2,1)S(1)}, bf16[32,16,512]{2,1,0:T(8,128)(2,1)S(1)}, u32[]{:S(2)}, u32[]{:S(2)}) collective-permute-start(bf16[32,16,512]{2,1,0:T(8,128)(2,1)S(1)} %get-tuple-element.27), channel_id=1, source_target_pairs={{0,96},{32,0},{64,32},{96,64},{1,97},{33,1},{65,33},{97,65},{2,98}... | collective-permute-start | bytes 1572872 | tf_op jit(solution)/shard_map/ppermute | solution.py:338
  4.9 16.1 %collective-permute-start.1 = (bf16[32,16,512]{2,1,0:T(8,128)(2,1)S(1)}, bf16[32,16,512]{2,1,0:T(8,128)(2,1)S(1)}, u32[]{:S(2)}, u32[]{:S(2)}) collective-permute-start(bf16[32,16,512]{2,1,0:T(8,128)(2,1)S(1)} %get-tuple-element.28), channel_id=1, source_target_pairs={{0,32},{32,64},{64,96},{96,0},{1,33},{33,65},{65,97},{97,1},{2,34}... | collective-permute-start | bytes 1572872 | tf_op jit(solution)/shard_map/ppermute | solution.py:337
  7.1 25.1 %collective-permute-start.3 = (bf16[32,16,512]{2,1,0:T(8,128)(2,1)}, bf16[32,16,512]{2,1,0:T(8,128)(2,1)S(1)}, u32[]{:S(2)}, u32[]{:S(2)}) collective-permute-start(bf16[32,16,512]{2,1,0:T(8,128)(2,1)} %get-tuple-element.25), channel_id=1, source_target_pairs={{0,32},{32,64},{64,96},{96,0},{1,33},{33,65},{65,97},{97,1},{2,34}... | collective-permute-start | bytes 1572872 | tf_op jit(solution)/shard_map/ppermute | solution.py:340
  7.8 24.3 %collective-permute-start = (bf16[32,16,512]{2,1,0:T(8,128)(2,1)}, bf16[32,16,512]{2,1,0:T(8,128)(2,1)S(1)}, u32[]{:S(2)}, u32[]{:S(2)}) collective-permute-start(bf16[32,16,512]{2,1,0:T(8,128)(2,1)} %get-tuple-element.26), channel_id=1, source_target_pairs={{0,96},{32,0},{64,32},{96,64},{1,97},{33,1},{65,33},{97,65},{2,98}... | collective-permute-start | bytes 1572872 | tf_op jit(solution)/shard_map/ppermute | solution.py:341
  22.2 16.3 %collective-permute-start.5 = (bf16[32,16,512]{2,1,0:T(8,128)(2,1)S(1)}, bf16[32,16,512]{2,1,0:T(8,128)(2,1)S(1)}, u32[]{:S(2)}, u32[]{:S(2)}) collective-permute-start(bf16[32,16,512]{2,1,0:T(8,128)(2,1)S(1)} %get-tuple-element.21), channel_id=1, source_target_pairs={{0,96},{32,0},{64,32},{96,64},{1,97},{33,1},{65,33},{97,65},{2,98}... | collective-permute-start | bytes 1572872 | tf_op jit(solution)/shard_map/ppermute | solution.py:343
  22.3 19.6 %collective-permute-start.2 = (bf16[32,16,512]{2,1,0:T(8,128)(2,1)S(1)}, bf16[32,16,512]{2,1,0:T(8,128)(2,1)S(1)}, u32[]{:S(2)}, u32[]{:S(2)}) collective-permute-start(bf16[32,16,512]{2,1,0:T(8,128)(2,1)S(1)} %get-tuple-element.22), channel_id=1, source_target_pairs={{0,32},{32,64},{64,96},{96,0},{1,33},{33,65},{65,97},{97,1},{2,34}... | collective-permute-start | bytes 1572872 | tf_op jit(solution)/shard_map/ppermute | solution.py:342
  43.7 32.4 %copy-start.1 = (bf16[1,1,3,512,512]{4,3,2,1,0:T(8,128)(2,1)S(1)}, bf16[1,1,3,512,512]{4,3,2,1,0:T(8,128)(2,1)}, u32[]{:S(2)}) copy-start(bf16[1,1,3,512,512]{4,3,2,1,0:T(8,128)(2,1)} %left_roots.1) | copy-start | bytes 4718596
  43.7 32.4 %all-to-all-start = ((bf16[32,3,16,512]{3,2,1,0:T(8,128)(2,1)}), bf16[32,3,16,512]{3,2,1,0:T(8,128)(2,1)S(1)}, u32[]{:S(2)}, u32[]{:S(2)}) async-start(bf16[32,3,16,512]{3,2,1,0:T(8,128)(2,1)} %bitcast.8._), calls=%async_computation | async-start | bytes 3145728 | tf_op jit(solution)/shard_map/all_to_all | solution.py:349
  85.4 27.9 %all-to-all-start.1 = ((bf16[32,3,16,512]{3,2,1,0:T(8,128)(2,1)}), bf16[32,3,16,512]{3,2,1,0:T(8,128)(2,1)S(1)}, u32[]{:S(2)}, u32[]{:S(2)}) async-start(bf16[32,3,16,512]{3,2,1,0:T(8,128)(2,1)} %get-tuple-element.13), calls=%async_computation.1 | async-start | bytes 3145728 | tf_op jit(solution)/shard_map/all_to_all | solution.py:353
  89.4 1.9 %copy-start = (f32[1,1,3,512,512]{4,3,2,1,0:T(8,128)S(1)}, f32[1,1,3,512,512]{4,3,2,1,0:T(8,128)}, u32[]{:S(2)}) copy-start(f32[1,1,3,512,512]{4,3,2,1,0:T(8,128)} %lprev_ref.1) | copy-start | bytes 9437188

commit v2 on v1

--- a/solution.py
+++ b/solution.py
@@ -24,7 +24,8 @@
 )
 
 VMEM_LIMIT = 40 * 1024 * 1024
-VMEM_MOST = 48 * 1024 * 1024
+VMEM_MOST = 52 * 1024 * 1024
+VMEM_SMALL = 16 * 1024 * 1024
 VMEM = pltpu.VMEM
 HBM = pltpu.HBM
 SMEM = pltpu.SMEM
@@ -66,7 +67,8 @@
     return pl.CostEstimate(flops=matmuls * 2 * side**3, bytes_accessed=nbytes, transcendentals=0)
 
 
-def place_kernel(place_ref, empty_ref, front_ref, up_ref, back_ref, down_ref, out_ref, sums, zeros, sem):
+def place_kernel(after, place_ref, empty_ref, front_ref, up_ref, back_ref, down_ref, *rest):
+    out_ref, sums, zeros, sem = rest[after], *rest[-3:]
     half = front_ref.shape[0]
     zeros[...] = jnp.zeros_like(zeros)
 
@@ -92,14 +94,19 @@
     pltpu.make_async_copy(out_ref, out_ref, sem).wait()
 
 
-def place_blocks(place, empty, front, up, back, down):
+def place_blocks(place, empty, front, up, back, down, *after, room=None):
     half, rows, cols = front.shape
     scalars = pl.BlockSpec(memory_space=SMEM)
     return pl.pallas_call(
-        place_kernel,
-        out_shape=jax.ShapeDtypeStruct((empty.shape[0], rows, cols), jnp.bfloat16),
-        in_specs=[scalars] * 2 + [pl.BlockSpec(memory_space=VMEM)] * 4,
-        out_specs=pl.BlockSpec(memory_space=HBM),
+        functools.partial(place_kernel, len(after)),
+        out_shape=[
+            jax.ShapeDtypeStruct((empty.shape[0], rows, cols), jnp.bfloat16),
+            *([jax.ShapeDtypeStruct(room, jnp.bfloat16)] if room else []),
+        ],
+        in_specs=[scalars] * 2
+        + [pl.BlockSpec(memory_space=VMEM)] * 4
+        + [pl.BlockSpec(memory_space=pl.ANY)] * len(after),
+        out_specs=[pl.BlockSpec(memory_space=HBM)] * (2 if room else 1),
         scratch_shapes=[
             VMEM((2 * half, rows, cols), jnp.bfloat16),
             VMEM((rows, cols), jnp.bfloat16),
@@ -108,11 +115,36 @@
         compiler_params=pltpu.CompilerParams(vmem_limit_bytes=VMEM_LIMIT),
         cost_estimate=cost(0, 0, 8 * half * rows * cols * 2),
         name="place_blocks",
-    )(place, empty, front, up, back, down)
+    )(place, empty, front, up, back, down, *after)
+
+
+def add_kernel(one_ref, two_ref, three_ref, four_ref, *rest):
+    first_ref, second_ref = rest[-2:]
+
+    def add(j, carry):
+        first_ref[j] = one_ref[j] + two_ref[j]
+        second_ref[j] = three_ref[j] + four_ref[j]
+        return carry
+
+    lax.fori_loop(0, first_ref.shape[0], add, 0, unroll=8)
+
+
+def add_pairs(one, two, three, four, *after):
+    near = pl.BlockSpec(memory_space=VMEM)
+    shape = jax.ShapeDtypeStruct(one.shape, one.dtype)
+    return pl.pallas_call(
+        add_kernel,
+        out_shape=[shape, shape],
+        in_specs=[near] * 4 + [pl.BlockSpec(memory_space=pl.ANY)] * len(after),
+        out_specs=[near, near],
+        compiler_params=pltpu.CompilerParams(vmem_limit_bytes=VMEM_SMALL),
+        cost_estimate=cost(800, 512, 2 * one.size),
+        name="add_pairs",
+    )(one, two, three, four, *after)
 
 
 def precondition_kernel(
-    live_ref, arrived, left_stats, right_stats, left_roots, right_roots, _, out, left_new, right_new,
+    live_ref, arrived_a, arrived_b, left_stats, right_stats, left_roots, right_roots, _, out, left_new, right_new,
     done_ref, stats, roots, results, wide, prod, raws, low, square, term, in_sems, out_sems,
 ):
     side = stats.shape[-1]
@@ -133,7 +165,8 @@
     get("right", right_stats.at[0, 0, 0], stats.at[1])
 
     def block_of(slot):
-        return arrived[:, slot].reshape(side, side)
+        halves = [half[:, slot].reshape(side, side // 2) for half in (arrived_a, arrived_b)]
+        return jnp.concatenate(halves, axis=1)
 
     def give(number, target):
         copy = pltpu.make_async_copy(results.at[number], target, out_sems.at[number])
@@ -217,7 +250,8 @@
 
 
 def precondition(live, arrived, left_stats, right_stats, left_roots, right_roots, spent):
-    owners, _, rows, side = arrived.shape
+    owners, _, rows, width = arrived[0].shape
+    side = left_stats.shape[-1]
     root = jax.ShapeDtypeStruct((owners, rows, side), jnp.bfloat16)
     far = pl.BlockSpec(memory_space=HBM)
     return pl.pallas_call(
@@ -225,7 +259,7 @@
         out_shape=[
             jax.ShapeDtypeStruct((owners, MOST, rows, side), jnp.bfloat16), root, root, token_shape(),
         ],
-        in_specs=[pl.BlockSpec(memory_space=SMEM), pl.BlockSpec(memory_space=VMEM)] + [far] * 5,
+        in_specs=[pl.BlockSpec(memory_space=SMEM)] + [pl.BlockSpec(memory_space=VMEM)] * 2 + [far] * 5,
         out_specs=[far] * 3 + [pl.BlockSpec(memory_space=SMEM)],
         scratch_shapes=[
             VMEM((2, side, side), jnp.float32),
@@ -242,21 +276,22 @@
         ],
         compiler_params=pltpu.CompilerParams(vmem_limit_bytes=VMEM_MOST),
         cost_estimate=cost(14, side, 9 * side * side * 4),
-        input_output_aliases={6: 0},
+        input_output_aliases={7: 0},
         name="precondition",
-    )(live, arrived, left_stats, right_stats, left_roots, right_roots, spent)
-
-
-def stats_kernel(live_ref, block_ref, lprev_ref, rprev_ref, _, left_ref, right_ref):
+    )(live, *arrived, left_stats, right_stats, left_roots, right_roots, spent)
+
+
+def stats_kernel(live_ref, front_ref, back_ref, lprev_ref, rprev_ref, _, left_ref, right_ref):
     side = lprev_ref.shape[-1]
-    block = block_ref[:, 0].reshape(side, side)
+    block = jnp.concatenate([front_ref[:, 0], back_ref[:, 0]], axis=-1).reshape(side, side)
     live = live_ref[pl.program_id(0)] > 0
     left_ref[0, 0, 0] = blend(live, lprev_ref[0, 0, 0], mul(block, block, ((1,), (1,))))
     right_ref[0, 0, 0] = blend(live, rprev_ref[0, 0, 0], mul(block, block, ((0,), (0,))))
 
 
 def update_stats(live, arrived, left_stats, right_stats, tied):
-    owners, _, rows, side = arrived.shape
+    owners, _, rows, width = arrived[0].shape
+    side = left_stats.shape[-1]
     at_slot = pl.BlockSpec((1, 1, 1, side, side), lambda s: (0, 0, s, 0, 0))
     shape = jax.ShapeDtypeStruct(left_stats.shape, jnp.float32)
     return pl.pallas_call(
@@ -264,13 +299,13 @@
         grid=(MOST,),
         out_shape=[shape, shape],
         in_specs=[pl.BlockSpec(memory_space=SMEM)]
-        + [pl.BlockSpec((owners, 1, rows, side), lambda s: (0, s, 0, 0))]
+        + [pl.BlockSpec((owners, 1, rows, width), lambda s: (0, s, 0, 0))] * 2
         + [at_slot, at_slot, pl.BlockSpec(memory_space=SMEM)],
         out_specs=[at_slot, at_slot],
         compiler_params=pltpu.CompilerParams(vmem_limit_bytes=VMEM_MOST),
         cost_estimate=cost(2 * MOST, side, 13 * side * side * 4),
         name="update_stats",
-    )(live, arrived, left_stats, right_stats, tied)
+    )(live, *arrived, left_stats, right_stats, tied)
 
 
 def assemble_kernel(slot_ref, owner_ref, back_ref, out_ref, sem):
@@ -329,26 +364,59 @@
     own_count = jnp.sum((owner == owner_id).astype(jnp.int32))
     live = (jnp.arange(MOST, dtype=jnp.int32) < own_count).astype(jnp.int32)
 
-    def part(source, ahead, low):
+    width = side // 2
+
+    def part(source, ahead, low, column):
         start = (group_id + ahead) % groups * share + low
-        return lax.dynamic_slice_in_dim(source, start, half, 0)
-
-    send_up1, send_down1 = part(local, 2, 0), part(local, 2, half)
-    up1 = lax.ppermute(send_up1, "rep", up)
-    down1 = lax.ppermute(send_down1, "rep", down)
-    later, _, _ = lax.optimization_barrier((local, send_up1, send_down1))
-    up2 = lax.ppermute(part(later, 1, half), "rep", up)
-    down2 = lax.ppermute(part(later, 3, 0), "rep", down)
-    up3 = lax.ppermute(part(local, 1, 0) + up1, "rep", up)
-    down3 = lax.ppermute(part(local, 3, half) + down1, "rep", down)
-    front = part(local, 0, 0).astype(jnp.float32) + down2.astype(jnp.float32)
-    back = part(local, 0, half).astype(jnp.float32) + up2.astype(jnp.float32)
-
-    outgoing = place_blocks(place, empty, front, up3, back, down3)
-    outgoing = outgoing.reshape(owners, MOST, slab_rows, side)
-    arrived = lax.all_to_all(outgoing, "fsdp", split_axis=0, concat_axis=0, tiled=True)
+        return lax.dynamic_slice(source, (start, 0, column), (half, slab_rows, width))
+
+    def send(pair):
+        return lax.ppermute(pair[0], "rep", up), lax.ppermute(pair[1], "rep", down)
+
+    def firsts(source, column):
+        return part(source, 2, 0, column), part(source, 2, half, column)
+
+    def seconds(source, column):
+        return part(source, 1, half, column), part(source, 3, 0, column)
+
+    def mids(source, column):
+        return part(source, 1, 0, column), part(source, 3, half, column)
+
+    def own_sums(source, column, up2, down2):
+        front = part(source, 0, 0, column).astype(jnp.float32) + down2.astype(jnp.float32)
+        return front, part(source, 0, half, column).astype(jnp.float32) + up2.astype(jnp.float32)
+
+    first = firsts(local, 0)
+    up1, down1 = send(first)
+    later, _ = lax.optimization_barrier((local, first))
+    second = seconds(later, 0)
+    up2, down2 = send(second)
+    later, _ = lax.optimization_barrier((later, second))
+    mid = mids(later, 0)
+    third = mid[0] + up1, mid[1] + down1
+    up3, down3 = send(third)
+    later, _ = lax.optimization_barrier((later, third))
+    firsts_b, seconds_b = firsts(later, width), seconds(later, width)
+    sums = own_sums(local, 0, up2, down2)
+    up1, down1 = send(firsts_b)
+    up2, down2 = send(seconds_b)
+    (outgoing_a,) = place_blocks(place, empty, sums[0], up3, sums[1], down3, *firsts_b, *seconds_b)
+    mid = mids(later, width)
+    third = add_pairs(mid[0], up1, mid[1], down1, outgoing_a)
+    up3, down3 = send(third)
+    later, _ = lax.optimization_barrier((later, third))
+    sums = own_sums(later, width, up2, down2)
+    outgoing_b, spent = place_blocks(
+        place, empty, sums[0], up3, sums[1], down3, room=(owners, MOST, slab_rows, side)
+    )
+    arrived = [
+        lax.all_to_all(
+            outgoing.reshape(owners, MOST, slab_rows, width), "fsdp", split_axis=0, concat_axis=0, tiled=True
+        )
+        for outgoing in (outgoing_a, outgoing_b)
+    ]
     results, left_new, right_new, done = precondition(
-        live, arrived, left_stats, right_stats, left_roots, right_roots, outgoing
+        live, arrived, left_stats, right_stats, left_roots, right_roots, spent
     )
     returned = lax.all_to_all(results, "fsdp", split_axis=0, concat_axis=0, tiled=True)
     left_out, right_out = update_stats(live, arrived, left_stats, right_stats, done)

time: 115 us -> 111 us (0.965)
  waiting for transfers between devices: 64.2 us -> 41.6 us
  starting transfers between devices: 20.7 us -> 33.3 us
  Pallas kernels: 19.1 us -> 22.2 us
  other arithmetic: 4.55 us -> 5.92 us
    ppermute x6 -> x12, waiting for transfers between devices: 25.5 us -> 9.7 us  [the longest x6 9.41 us: send(): lax.ppermute(pair[0], 'rep', up)]
    all_to_all x1 -> x2, waiting for transfers between devices: 23.3 us -> 15.9 us  [on_device(): lax.all_to_all(outgoing.reshape(owners, MOST, slab_rows, width), 'fsdp',...]
    ppermute x6 -> x12, starting transfers between devices: 8.23 us -> 15.5 us  [the longest x6 10.1 us: send(): lax.ppermute(pair[1], 'rep', down)]
    all_to_all x1 -> x2, starting transfers between devices: 8.48 us -> 13.7 us  [on_device(): lax.all_to_all(outgoing.reshape(owners, MOST, slab_rows, width), 'fsdp',...]
    pallas_call x1 -> x3, Pallas kernels: 1.73 us -> 3.22 us  [the longest x2 3.15 us: place_blocks(): pl.pallas_call(functools.partial(place_kernel, len(after)), out_shape=[ja...]
    pallas_call x1, Pallas kernels: 6.63 us -> 7.88 us  [update_stats(): pl.pallas_call(stats_kernel, grid=(MOST,), out_shape=[shape, shape], in_s...]
    dynamic_slice x2 -> x3, local copies, waits for them, and re-layouts: 3.51 us -> 4.37 us  [part(): lax.dynamic_slice(source, (start, 0, column), (half, slab_rows, width))]
    add x2 -> x3, other arithmetic: 2.92 us -> 3.64 us  [the longest x2 2.53 us: own_sums(): part(source, 0, half, column).astype(jnp.float32) + up2.astype(jnp.float32)]
  transfers between devices with their start and end apart: 8 -> 15, of which waited for: 7 -> 7; matrix products, arithmetic and copies ran while one was open for 6% -> 8% of each run, Pallas kernels for 6% -> 10%
where the time goes in v2:
time: 111 us; the launch traced here: 110 us
  waiting for transfers between devices  41.6 us (37%)
  starting transfers between devices  33.3 us (30%)
  Pallas kernels  22.2 us (20%)
  local copies, waits for them, and re-layouts  6.42 us (6%)
  other arithmetic  5.92 us (5%)
    all_to_all x1, waiting for transfers between devices, on_device(): lax.all_to_all(results, 'fsdp', split_axis=0, concat_axis=0, tiled=True)  16 us
    all_to_all x2, waiting for transfers between devices, on_device(): lax.all_to_all(outgoing.reshape(owners, MOST, slab_rows, width), 'fsdp',...  15.9 us
    all_to_all x2, starting transfers between devices, on_device(): lax.all_to_all(outgoing.reshape(owners, MOST, slab_rows, width), 'fsdp',...  13.7 us
    ppermute x6, starting transfers between devices, send(): lax.ppermute(pair[1], 'rep', down)  10.1 us
    pallas_call x1, Pallas kernels, precondition(): pl.pallas_call(precondition_kernel, out_shape=[jax.ShapeDtypeStruct((owne...  9.61 us
    ppermute x6, waiting for transfers between devices, send(): lax.ppermute(pair[0], 'rep', up)  9.41 us
    pallas_call x1, Pallas kernels, update_stats(): pl.pallas_call(stats_kernel, grid=(MOST,), out_shape=[shape, shape], in_s...  7.88 us
    ppermute x6, starting transfers between devices, send(): lax.ppermute(pair[0], 'rep', up)  5.4 us
  transfers between devices with their start and end apart: 15, of which 7 were waited for; matrix products, arithmetic and copies ran while one was open for 8% of the time, Pallas kernels for 10%

profile of v2, /device:TPU:0, one launch (start us, length us, event | category | flops | bytes accessed | tf_op | source)
XLA Modules:
  0.0 110.3 jit_solution(12783866334232882174)
XLA Ops:
  0.7 1.1 dynamic-slice_bitcast_fusion
  1.7 2.9 %collective-permute-start.4 = (bf16[32,16,256]{2,1,0:T(8,128)(2,1)S(1)}, bf16[32,16,256]{2,1,0:T(8,128)(2,1)S(1)}, u32[]{:S(2)}, u32[]{:S(2)}) collective-permute-start(bf16[32,16,256]{2,1,0:T(8,128)(2,1)S(1)} %get-tuple-element.49), channel_id=1, source_target_pairs={{0,96},{32,0},{64,32},{96,64},{1,97},{33,1},{65,33},{97,65},{2,98}... | collective-permute-start | bytes 786440 | tf_op jit(solution)/shard_map/ppermute | solution.py:374
  4.6 1.1 constant_dynamic-slice_fusion.6
  5.7 0.8 collective-permute-start.3
  6.5 2.6 %collective-permute-start = (bf16[32,16,256]{2,1,0:T(8,128)(2,1)S(1)}, bf16[32,16,256]{2,1,0:T(8,128)(2,1)S(1)}, u32[]{:S(2)}, u32[]{:S(2)}) collective-permute-start(bf16[32,16,256]{2,1,0:T(8,128)(2,1)S(1)} %get-tuple-element.48), channel_id=1, source_target_pairs={{0,96},{32,0},{64,32},{96,64},{1,97},{33,1},{65,33},{97,65},{2,98}... | collective-permute-start | bytes 786440 | tf_op jit(solution)/shard_map/ppermute | solution.py:374
  9.1 1.4 %fusion.1 = (s32[]{:T(128)}, s32[64]{0:T(128)S(1)}) fusion(s32[]{:T(128)S(6)} %axis_index.25, s32[256,1]{0,1:T(1,128)} %param.7, s32[]{:T(128)S(6)} %select_n.78), kind=kLoop, calls=%fused_computation.24 | loop fusion | flops 191 | bytes 524 | tf_op jit(solution)/shard_map/reduce_sum | solution.py:364
  11.0 0.5 copy-done.5
  11.7 3.4 %collective-permute-done.1 = bf16[32,16,256]{2,1,0:T(8,128)(2,1)S(1)} collective-permute-done((bf16[32,16,256]{2,1,0:T(8,128)(2,1)S(1)}, bf16[32,16,256]{2,1,0:T(8,128)(2,1)S(1)}, u32[]{:S(2)}, u32[]{:S(2)}) %collective-permute-start.1) | collective-permute-done | bytes 262176 | tf_op jit(solution)/shard_map/ppermute | solution.py:374
  15.1 1.1 %dynamic-slice_add_fusion = (bf16[32,16,256]{2,1,0:T(8,128)(2,1)S(1)}, bf16[32,16,256]{2,1,0:T(8,128)(2,1)S(1)}) fusion(bf16[32,16,256]{2,1,0:T(8,128)(2,1)S(1)} %collective-permute-done.4, bf16[256,16,512]{2,1,0:T(8,128)(2,1)} %bitcast.19, s32[]{:T(128)S(6)} %select_n.90, bf16[32,16,256]{2,1,0:T(8,128)(2,1)S(1)} %collective-permute-done.1, s32[]{:T(128)S(6)} %select_n.88), kind=kLoop, calls=%fused_computation.4 | loop fusion | flops 262144 | bytes 1572872 | tf_op jit(solution)/shard_map/add | solution.py:396
  16.3 2.0 %collective-permute-start.2 = (bf16[32,16,256]{2,1,0:T(8,128)(2,1)S(1)}, bf16[32,16,256]{2,1,0:T(8,128)(2,1)S(1)}, u32[]{:S(2)}, u32[]{:S(2)}) collective-permute-start(bf16[32,16,256]{2,1,0:T(8,128)(2,1)S(1)} %get-tuple-element.44), channel_id=1, source_target_pairs={{0,32},{32,64},{64,96},{96,0},{1,33},{33,65},{65,97},{97,1},{2,34}... | collective-permute-start | bytes 786440 | tf_op jit(solution)/shard_map/ppermute | solution.py:374
  18.3 2.2 %constant_dynamic-slice_fusion = (bf16[32,16,256]{2,1,0:T(8,128)(2,1)S(1)}, bf16[32,16,256]{2,1,0:T(8,128)(2,1)S(1)}, bf16[32,16,256]{2,1,0:T(8,128)(2,1)}, bf16...) fusion(bf16[256,16,512]{2,1,0:T(8,128)(2,1)} %bitcast.20, ...), kind=kLoop, calls=%fused_computation.13 | loop fusion | bytes 3145752 | tf_op jit(solution)/shard_map/dynamic_slice | solution.py:371
  20.5 1.3 %collective-permute-start.8 = (bf16[32,16,256]{2,1,0:T(8,128)(2,1)}, bf16[32,16,256]{2,1,0:T(8,128)(2,1)}, u32[]{:S(2)}, u32[]{:S(2)}) collective-permute-start(bf16[32,16,256]{2,1,0:T(8,128)(2,1)} %get-tuple-element.39.rest_3_), channel_id=1, source_target_pairs={{0,96},{32,0},{64,32},{96,64},{1,97},{33,1},{65,33},{97,65},{2,98}... | collective-permute-start | bytes 786440 | tf_op jit(solution)/shard_map/ppermute | solution.py:374
  21.9 2.0 %collective-permute-start.6 = (bf16[32,16,256]{2,1,0:T(8,128)(2,1)S(1)}, bf16[32,16,256]{2,1,0:T(8,128)(2,1)S(1)}, u32[]{:S(2)}, u32[]{:S(2)}) collective-permute-start(bf16[32,16,256]{2,1,0:T(8,128)(2,1)S(1)} %get-tuple-element.42.rest_0_), channel_id=1, source_target_pairs={{0,32},{32,64},{64,96},{96,0},{1,33},{33,65},{65,97},{97,1},{2,34}... | collective-permute-start | bytes 786440 | tf_op jit(solution)/shard_map/ppermute | solution.py:374
  23.9 1.2 %convert_add_fusion = (f32[32,16,256]{2,1,0:T(8,128)S(1)}, f32[32,16,256]{2,1,0:T(8,128)S(1)}) fusion(bf16[32,16,256]{2,1,0:T(8,128)(2,1)S(1)} %collective-permute-done.3, bf16[1,256,16,512]{3,2,1,0:T(8,128)(2,1)} %param.6, s32[]{:T(128)S(6)} %select_n.89, bf16[32,16,256]{2,1,0:T(8,128)(2,1)S(1)} %collective-permute-done, s32[]{:T(128)S(6)} %select_n.80), kind=kLoop, calls=%fused_computation | loop fusion | flops 786432 | bytes 2097160 | tf_op jit(solution)/shard_map/add | solution.py:387
  25.3 0.5 collective-permute-start.10
  25.9 0.9 collective-permute-done.2.up_ref
  26.8 1.6 %place_blocks.2.rest_0_ = bf16[96,16,256]{2,1,0:T(8,128)(2,1)} custom-call(s32[64]{0:T(128)S(1)} %multiply_add_fusion.place_ref, s32[96]{0:T(128)S(1)} %broadcast_subtract_fusion.empty_ref, f32[32,16,256]{2,1,0:T(8,128)S(1)} %get-tuple-element.46.front_ref, bf16[32,16,256]{2,1,0:T(8,128)(2,1)S(1)} %collective-permute-done.2.up_ref, ...), custom_call_target="tpu_custom_call" | custom-call | bytes 2097152 | tf_op jit(solution)/shard_map/place_blocks/pallas_call | solution.py:100
  28.4 8.5 %all-to-all-start = ((bf16[32,3,16,256]{3,2,1,0:T(8,128)(2,1)}), bf16[32,3,16,256]{3,2,1,0:T(8,128)(2,1)}, u32[]{:S(2)}, u32[]{:S(2)}) async-start(bf16[32,3,16,256]{3,2,1,0:T(8,128)(2,1)} %bitcast.6), calls=%async_computation | async-start | bytes 1572864 | tf_op jit(solution)/shard_map/all_to_all | solution.py:413
  37.0 3.2 %collective-permute-start.11 = (bf16[32,16,256]{2,1,0:T(8,128)(2,1)S(1)}, bf16[32,16,256]{2,1,0:T(8,128)(2,1)S(1)}, u32[]{:S(2)}, u32[]{:S(2)}) collective-permute-start(bf16[32,16,256]{2,1,0:T(8,128)(2,1)S(1)} %get-tuple-element.23), channel_id=1, source_target_pairs={{0,96},{32,0},{64,32},{96,64},{1,97},{33,1},{65,33},{97,65},{2,98}... | collective-permute-start | bytes 786440 | tf_op jit(solution)/shard_map/ppermute | solution.py:374
  40.3 1.3 %convert_add_fusion.2 = (f32[32,16,256]{2,1,0:T(8,128)S(1)}, f32[32,16,256]{2,1,0:T(8,128)S(1)}) fusion(bf16[32,16,256]{2,1,0:T(8,128)(2,1)} %collective-permute-done.10, bf16[256,16,512]{2,1,0:T(8,128)(2,1)} %bitcast.21, s32[]{:T(128)S(6)} %select_n.89, bf16[32,16,256]{2,1,0:T(8,128)(2,1)} %collective-permute-done.8, s32[]{:T(128)S(6)} %select_n.80), kind=kLoop, calls=%fused_computation.2 | loop fusion | flops 786432 | bytes 2097160 | tf_op jit(solution)/shard_map/add | solution.py:387
  41.6 5.0 %collective-permute-done.9.up_ref = bf16[32,16,256]{2,1,0:T(8,128)(2,1)S(1)} collective-permute-done((bf16[32,16,256]{2,1,0:T(8,128)(2,1)S(1)}, bf16[32,16,256]{2,1,0:T(8,128)(2,1)S(1)}, u32[]{:S(2)}, u32[]{:S(2)}) %collective-permute-start.9) | collective-permute-done | bytes 262176 | tf_op jit(solution)/shard_map/ppermute | solution.py:374
  46.7 1.6 %place_blocks.3 = (bf16[96,16,256]{2,1,0:T(8,128)(2,1)}, bf16[32,3,16,512]{3,2,1,0:T(8,128)(2,1)S(1)}) custom-call(s32[64]{0:T(128)S(1)} %multiply_add_fusion.place_ref, s32[96]{0:T(128)S(1)} %copy-done.2, f32[32,16,256]{2,1,0:T(8,128)S(1)} %get-tuple-element.36.front_ref, bf16[32,16,256]{2,1,0:T(8,128)(2,1)S(1)} %collective-permute-done.9.up_ref, ...), custom_call_target="tpu_custom_call" | custom-call | bytes 2097152 | tf_op jit(solution)/shard_map/place_blocks/pallas_call | solution.py:100
  48.3 1.2 %copy-done = bf16[32,3,16,512]{3,2,1,0:T(8,128)(2,1)} copy-done((bf16[32,3,16,512]{3,2,1,0:T(8,128)(2,1)}, bf16[32,3,16,512]{3,2,1,0:T(8,128)(2,1)S(1)}, u32[]{:S(2)}) %copy-start) | copy-done | bytes 1572888
  49.4 2.0 %all-to-all-done.arrived_a.front_ref = bf16[32,3,16,256]{3,2,1,0:T(8,128)(2,1)} async-done(((bf16[32,3,16,256]{3,2,1,0:T(8,128)(2,1)}), bf16[32,3,16,256]{3,2,1,0:T(8,128)(2,1)}, u32[]{:S(2)}, u32[]{:S(2)}) %all-to-all-start) | async-done | bytes 786464 | tf_op jit(solution)/shard_map/all_to_all | solution.py:413
  51.4 5.3 %all-to-all-start.1 = ((bf16[32,3,16,256]{3,2,1,0:T(8,128)(2,1)}), bf16[32,3,16,256]{3,2,1,0:T(8,128)(2,1)S(1)}, u32[]{:S(2)}, u32[]{:S(2)}) async-start(bf16[32,3,16,256]{3,2,1,0:T(8,128)(2,1)} %bitcast.7), calls=%async_computation.1 | async-start | bytes 1572864 | tf_op jit(solution)/shard_map/all_to_all | solution.py:413
  56.7 0.7 compare_convert_fusion.live_ref
  57.4 13.9 %all-to-all-done.1.arrived_b.back_ref = bf16[32,3,16,256]{3,2,1,0:T(8,128)(2,1)S(1)} async-done(((bf16[32,3,16,256]{3,2,1,0:T(8,128)(2,1)}), bf16[32,3,16,256]{3,2,1,0:T(8,128)(2,1)S(1)}, u32[]{:S(2)}, u32[]{:S(2)}) %all-to-all-start.1) | async-done | bytes 786464 | tf_op jit(solution)/shard_map/all_to_all | solution.py:413
  71.3 9.6 %precondition.1 = (bf16[32,3,16,512]{3,2,1,0:T(8,128)(2,1)}, bf16[32,16,512]{2,1,0:T(8,128)(2,1)}, bf16[32,16,512]{2,1,0:T(8,128)(2,1)}, s32[1]{0:T(128)}) custom-call(s32[3]{0:T(128)S(1)} %compare_convert_fusion.live_ref, bf16[32,3,16,256]{3,2,1,0:T(8,128)(2,1)} %all-to-all-done.arrived_a.front_ref, ...), custom_call_target="tpu_custom_call", output_to_operand_aliasing={{0}: (7, {})} | custom-call | flops 3758096384 | bytes 9437184 | tf_op jit(solution)/shard_map/precondition/pallas_call | solution.py:257
  80.9 4.0 %all-to-all-start.2 = ((bf16[32,3,16,512]{3,2,1,0:T(8,128)(2,1)}), bf16[32,3,16,512]{3,2,1,0:T(8,128)(2,1)S(1)}, u32[]{:S(2)}, u32[]{:S(2)}) async-start(bf16[32,3,16,512]{3,2,1,0:T(8,128)(2,1)} %get-tuple-element.27), calls=%async_computation.2 | async-start | bytes 3145728 | tf_op jit(solution)/shard_map/all_to_all | solution.py:421
  84.9 7.9 %update_stats.1 = (f32[1,1,3,512,512]{4,3,2,1,0:T(8,128)}, f32[1,1,3,512,512]{4,3,2,1,0:T(8,128)}) custom-call(s32[3]{0:T(128)S(1)} %compare_convert_fusion.live_ref, bf16[32,3,16,256]{3,2,1,0:T(8,128)(2,1)} %all-to-all-done.arrived_a.front_ref, bf16[32,3,16,256]{3,2,1,0:T(8,128)(2,1)S(1)} %all-to-all-done.1.arrived_b.back_ref, ...), custom_call_target="tpu_custom_call" | custom-call | flops 1610612736 | bytes 13631488 | tf_op jit(solution)/shard_map/update_stats/pallas_call | solution.py:297
  92.8 16.0 %all-to-all-done.2.back_ref = bf16[32,3,16,512]{3,2,1,0:T(8,128)(2,1)S(1)} async-done(((bf16[32,3,16,512]{3,2,1,0:T(8,128)(2,1)}), bf16[32,3,16,512]{3,2,1,0:T(8,128)(2,1)S(1)}, u32[]{:S(2)}, u32[]{:S(2)}) %all-to-all-start.2) | async-done | bytes 1572896 | tf_op jit(solution)/shard_map/all_to_all | solution.py:421
  108.8 1.5 %assemble.1 = bf16[64,16,512]{2,1,0:T(8,128)(2,1)} custom-call(s32[64]{0:T(128)S(1)} %copy-done.6, s32[64]{0:T(128)S(1)} %copy-done.4, bf16[32,3,16,512]{3,2,1,0:T(8,128)(2,1)S(1)} %all-to-all-done.2.back_ref), custom_call_target="tpu_custom_call" | custom-call | bytes 2097152 | tf_op jit(solution)/shard_map/assemble/pallas_call | solution.py:325
  (30 shorter events, 1.2 us)
Async XLA Ops:
  1.7 9.9 %collective-permute-start.4 = (bf16[32,16,256]{2,1,0:T(8,128)(2,1)S(1)}, bf16[32,16,256]{2,1,0:T(8,128)(2,1)S(1)}, u32[]{:S(2)}, u32[]{:S(2)}) collective-permute-start(bf16[32,16,256]{2,1,0:T(8,128)(2,1)S(1)} %get-tuple-element.49), channel_id=1, source_target_pairs={{0,96},{32,0},{64,32},{96,64},{1,97},{33,1},{65,33},{97,65},{2,98}... | collective-permute-start | bytes 786440 | tf_op jit(solution)/shard_map/ppermute | solution.py:374
  4.6 10.4 %collective-permute-start.1 = (bf16[32,16,256]{2,1,0:T(8,128)(2,1)S(1)}, bf16[32,16,256]{2,1,0:T(8,128)(2,1)S(1)}, u32[]{:S(2)}, u32[]{:S(2)}) collective-permute-start(bf16[32,16,256]{2,1,0:T(8,128)(2,1)S(1)} %get-tuple-element.50), channel_id=1, source_target_pairs={{0,32},{32,64},{64,96},{96,0},{1,33},{33,65},{65,97},{97,1},{2,34}... | collective-permute-start | bytes 786440 | tf_op jit(solution)/shard_map/ppermute | solution.py:374
  5.7 16.1 %collective-permute-start.3 = (bf16[32,16,256]{2,1,0:T(8,128)(2,1)S(1)}, bf16[32,16,256]{2,1,0:T(8,128)(2,1)S(1)}, u32[]{:S(2)}, u32[]{:S(2)}) collective-permute-start(bf16[32,16,256]{2,1,0:T(8,128)(2,1)S(1)} %get-tuple-element.47), channel_id=1, source_target_pairs={{0,32},{32,64},{64,96},{96,0},{1,33},{33,65},{65,97},{97,1},{2,34}... | collective-permute-start | bytes 786440 | tf_op jit(solution)/shard_map/ppermute | solution.py:374
  6.5 15.4 %collective-permute-start = (bf16[32,16,256]{2,1,0:T(8,128)(2,1)S(1)}, bf16[32,16,256]{2,1,0:T(8,128)(2,1)S(1)}, u32[]{:S(2)}, u32[]{:S(2)}) collective-permute-start(bf16[32,16,256]{2,1,0:T(8,128)(2,1)S(1)} %get-tuple-element.48), channel_id=1, source_target_pairs={{0,96},{32,0},{64,32},{96,64},{1,97},{33,1},{65,33},{97,65},{2,98}... | collective-permute-start | bytes 786440 | tf_op jit(solution)/shard_map/ppermute | solution.py:374
  10.5 0.5 copy-start.3
  11.0 0.5 copy-start.5
  11.6 15.2 %copy-start.1 = (s32[96]{0:T(128)}, s32[96]{0:T(128)S(1)}, u32[]{:S(2)}) copy-start(s32[96]{0:T(128)S(1)} %broadcast_subtract_fusion.empty_ref) | copy-start | bytes 1156
  16.2 9.1 %collective-permute-start.5 = (bf16[32,16,256]{2,1,0:T(8,128)(2,1)S(1)}, bf16[32,16,256]{2,1,0:T(8,128)(2,1)S(1)}, u32[]{:S(2)}, u32[]{:S(2)}) collective-permute-start(bf16[32,16,256]{2,1,0:T(8,128)(2,1)S(1)} %get-tuple-element.43), channel_id=1, source_target_pairs={{0,96},{32,0},{64,32},{96,64},{1,97},{33,1},{65,33},{97,65},{2,98}... | collective-permute-start | bytes 786440 | tf_op jit(solution)/shard_map/ppermute | solution.py:374
  16.3 10.5 %collective-permute-start.2 = (bf16[32,16,256]{2,1,0:T(8,128)(2,1)S(1)}, bf16[32,16,256]{2,1,0:T(8,128)(2,1)S(1)}, u32[]{:S(2)}, u32[]{:S(2)}) collective-permute-start(bf16[32,16,256]{2,1,0:T(8,128)(2,1)S(1)} %get-tuple-element.44), channel_id=1, source_target_pairs={{0,32},{32,64},{64,96},{96,0},{1,33},{33,65},{65,97},{97,1},{2,34}... | collective-permute-start | bytes 786440 | tf_op jit(solution)/shard_map/ppermute | solution.py:374
  20.5 19.7 %collective-permute-start.8 = (bf16[32,16,256]{2,1,0:T(8,128)(2,1)}, bf16[32,16,256]{2,1,0:T(8,128)(2,1)}, u32[]{:S(2)}, u32[]{:S(2)}) collective-permute-start(bf16[32,16,256]{2,1,0:T(8,128)(2,1)} %get-tuple-element.39.rest_3_), channel_id=1, source_target_pairs={{0,96},{32,0},{64,32},{96,64},{1,97},{33,1},{65,33},{97,65},{2,98}... | collective-permute-start | bytes 786440 | tf_op jit(solution)/shard_map/ppermute | solution.py:374
  21.8 15.0 %collective-permute-start.7 = (bf16[32,16,256]{2,1,0:T(8,128)(2,1)S(1)}, bf16[32,16,256]{2,1,0:T(8,128)(2,1)S(1)}, u32[]{:S(2)}, u32[]{:S(2)}) collective-permute-start(bf16[32,16,256]{2,1,0:T(8,128)(2,1)S(1)} %get-tuple-element.41.rest_1_), channel_id=1, source_target_pairs={{0,96},{32,0},{64,32},{96,64},{1,97},{33,1},{65,33},{97,65},{2,98}... | collective-permute-start | bytes 786440 | tf_op jit(solution)/shard_map/ppermute | solution.py:374
  21.9 15.0 %collective-permute-start.6 = (bf16[32,16,256]{2,1,0:T(8,128)(2,1)S(1)}, bf16[32,16,256]{2,1,0:T(8,128)(2,1)S(1)}, u32[]{:S(2)}, u32[]{:S(2)}) collective-permute-start(bf16[32,16,256]{2,1,0:T(8,128)(2,1)S(1)} %get-tuple-element.42.rest_0_), channel_id=1, source_target_pairs={{0,32},{32,64},{64,96},{96,0},{1,33},{33,65},{65,97},{97,1},{2,34}... | collective-permute-start | bytes 786440 | tf_op jit(solution)/shard_map/ppermute | solution.py:374
  25.3 15.0 %collective-permute-start.10 = (bf16[32,16,256]{2,1,0:T(8,128)(2,1)}, bf16[32,16,256]{2,1,0:T(8,128)(2,1)}, u32[]{:S(2)}, u32[]{:S(2)}) collective-permute-start(bf16[32,16,256]{2,1,0:T(8,128)(2,1)} %get-tuple-element.40.rest_2_), channel_id=1, source_target_pairs={{0,32},{32,64},{64,96},{96,0},{1,33},{33,65},{65,97},{97,1},{2,34}... | collective-permute-start | bytes 786440 | tf_op jit(solution)/shard_map/ppermute | solution.py:374
  28.4 23.0 %all-to-all-start = ((bf16[32,3,16,256]{3,2,1,0:T(8,128)(2,1)}), bf16[32,3,16,256]{3,2,1,0:T(8,128)(2,1)}, u32[]{:S(2)}, u32[]{:S(2)}) async-start(bf16[32,3,16,256]{3,2,1,0:T(8,128)(2,1)} %bitcast.6), calls=%async_computation | async-start | bytes 1572864 | tf_op jit(solution)/shard_map/all_to_all | solution.py:413
  36.9 9.8 %copy-start.2 = (s32[96]{0:T(128)S(1)}, s32[96]{0:T(128)}, u32[]{:S(2)}) copy-start(s32[96]{0:T(128)} %copy-done.1) | copy-start | bytes 1156
  37.0 9.7 %collective-permute-start.9 = (bf16[32,16,256]{2,1,0:T(8,128)(2,1)S(1)}, bf16[32,16,256]{2,1,0:T(8,128)(2,1)S(1)}, u32[]{:S(2)}, u32[]{:S(2)}) collective-permute-start(bf16[32,16,256]{2,1,0:T(8,128)(2,1)S(1)} %get-tuple-element.22), channel_id=1, source_target_pairs={{0,32},{32,64},{64,96},{96,0},{1,33},{33,65},{65,97},{97,1},{2,34}... | collective-permute-start | bytes 786440 | tf_op jit(solution)/shard_map/ppermute | solution.py:374
  37.0 9.6 %collective-permute-start.11 = (bf16[32,16,256]{2,1,0:T(8,128)(2,1)S(1)}, bf16[32,16,256]{2,1,0:T(8,128)(2,1)S(1)}, u32[]{:S(2)}, u32[]{:S(2)}) collective-permute-start(bf16[32,16,256]{2,1,0:T(8,128)(2,1)S(1)} %get-tuple-element.23), channel_id=1, source_target_pairs={{0,96},{32,0},{64,32},{96,64},{1,97},{33,1},{65,33},{97,65},{2,98}... | collective-permute-start | bytes 786440 | tf_op jit(solution)/shard_map/ppermute | solution.py:374
  48.2 1.2 %copy-start = (bf16[32,3,16,512]{3,2,1,0:T(8,128)(2,1)}, bf16[32,3,16,512]{3,2,1,0:T(8,128)(2,1)S(1)}, u32[]{:S(2)}) copy-start(bf16[32,3,16,512]{3,2,1,0:T(8,128)(2,1)S(1)} %get-tuple-element.26._) | copy-start | bytes 4718596
  51.4 19.9 %all-to-all-start.1 = ((bf16[32,3,16,256]{3,2,1,0:T(8,128)(2,1)}), bf16[32,3,16,256]{3,2,1,0:T(8,128)(2,1)S(1)}, u32[]{:S(2)}, u32[]{:S(2)}) async-start(bf16[32,3,16,256]{3,2,1,0:T(8,128)(2,1)} %bitcast.7), calls=%async_computation.1 | async-start | bytes 1572864 | tf_op jit(solution)/shard_map/all_to_all | solution.py:413
  80.9 27.9 %all-to-all-start.2 = ((bf16[32,3,16,512]{3,2,1,0:T(8,128)(2,1)}), bf16[32,3,16,512]{3,2,1,0:T(8,128)(2,1)S(1)}, u32[]{:S(2)}, u32[]{:S(2)}) async-start(bf16[32,3,16,512]{3,2,1,0:T(8,128)(2,1)} %get-tuple-element.27), calls=%async_computation.2 | async-start | bytes 3145728 | tf_op jit(solution)/shard_map/all_to_all | solution.py:421
  84.9 23.9 %copy-start.4 = (s32[64]{0:T(128)S(1)}, s32[64]{0:T(128)}, u32[]{:S(2)}) copy-start(s32[64]{0:T(128)} %copy-done.3) | copy-start | bytes 772
  84.9 23.9 %copy-start.6 = (s32[64]{0:T(128)S(1)}, s32[64]{0:T(128)}, u32[]{:S(2)}) copy-start(s32[64]{0:T(128)} %copy-done.5) | copy-start | bytes 772

commit v3 on v2

--- a/solution.py
+++ b/solution.py
@@ -25,6 +25,7 @@
 
 VMEM_LIMIT = 40 * 1024 * 1024
 VMEM_MOST = 52 * 1024 * 1024
+VMEM_ALL = 60 * 1024 * 1024
 VMEM_SMALL = 16 * 1024 * 1024
 VMEM = pltpu.VMEM
 HBM = pltpu.HBM
@@ -41,6 +42,7 @@
 
 ROWS = 64
 COLS = 128
+PARTS = 4
 
 
 def tiles(side):
@@ -67,6 +69,22 @@
     return pl.CostEstimate(flops=matmuls * 2 * side**3, bytes_accessed=nbytes, transcendentals=0)
 
 
+def spare_kernel(_, room_ref, done_ref):
+    done_ref[0] = 0
+
+
+def spare_room(after, shape):
+    scalars = pl.BlockSpec(memory_space=SMEM)
+    return pl.pallas_call(
+        spare_kernel,
+        out_shape=[jax.ShapeDtypeStruct(shape, jnp.bfloat16), token_shape()],
+        in_specs=[scalars],
+        out_specs=[pl.BlockSpec(memory_space=pl.ANY), scalars],
+        compiler_params=pltpu.CompilerParams(vmem_limit_bytes=VMEM_ALL),
+        name="spare_room",
+    )(after)
+
+
 def place_kernel(after, place_ref, empty_ref, front_ref, up_ref, back_ref, down_ref, *rest):
     out_ref, sums, zeros, sem = rest[after], *rest[-3:]
     half = front_ref.shape[0]
@@ -94,19 +112,16 @@
     pltpu.make_async_copy(out_ref, out_ref, sem).wait()
 
 
-def place_blocks(place, empty, front, up, back, down, *after, room=None):
+def place_blocks(place, empty, front, up, back, down, *after):
     half, rows, cols = front.shape
     scalars = pl.BlockSpec(memory_space=SMEM)
     return pl.pallas_call(
         functools.partial(place_kernel, len(after)),
-        out_shape=[
-            jax.ShapeDtypeStruct((empty.shape[0], rows, cols), jnp.bfloat16),
-            *([jax.ShapeDtypeStruct(room, jnp.bfloat16)] if room else []),
-        ],
+        out_shape=jax.ShapeDtypeStruct((empty.shape[0], rows, cols), jnp.bfloat16),
         in_specs=[scalars] * 2
         + [pl.BlockSpec(memory_space=VMEM)] * 4
         + [pl.BlockSpec(memory_space=pl.ANY)] * len(after),
-        out_specs=[pl.BlockSpec(memory_space=HBM)] * (2 if room else 1),
+        out_specs=pl.BlockSpec(memory_space=HBM),
         scratch_shapes=[
             VMEM((2 * half, rows, cols), jnp.bfloat16),
             VMEM((rows, cols), jnp.bfloat16),
@@ -143,79 +158,25 @@
     )(one, two, three, four, *after)
 
 
-def precondition_kernel(
-    live_ref, arrived_a, arrived_b, left_stats, right_stats, left_roots, right_roots, _, out, left_new, right_new,
-    done_ref, stats, roots, results, wide, prod, raws, low, square, term, in_sems, out_sems,
-):
+def new_roots(live, stats, grams, low, square, term, prod, between):
     side = stats.shape[-1]
-    entries = side * side
     f32, bf16 = jnp.float32, jnp.bfloat16
     c0, c1, c2, c3, c4, c5, c6 = ROOT_POLY
     grid = tiles(side)
-    fetch = {}
-
-    def get(name, source, target):
-        fetch[name] = pltpu.make_async_copy(source, target, in_sems.at[len(fetch)])
-        fetch[name].start()
-
-    for slot in range(1, MOST):
-        get("r%d" % slot, right_roots.at[0, 0, slot], roots.at[2 * slot - 1])
-        get("l%d" % slot, left_roots.at[0, 0, slot], roots.at[2 * slot - 2])
-    get("left", left_stats.at[0, 0, 0], stats.at[0])
-    get("right", right_stats.at[0, 0, 0], stats.at[1])
-
-    def block_of(slot):
-        halves = [half[:, slot].reshape(side, side // 2) for half in (arrived_a, arrived_b)]
-        return jnp.concatenate(halves, axis=1)
-
-    def give(number, target):
-        copy = pltpu.make_async_copy(results.at[number], target, out_sems.at[number])
-        copy.start()
-        return copy
-
-    def put(number, rows, cols, tile):
-        slabs = slice(rows.start // 16, rows.stop // 16)
-        results[number, slabs, :, cols] = tile.reshape(ROWS // 16, 16, COLS)
-
-    def power(tile_of):
-        return total([jnp.square(tile_of(rows, cols)) for rows, cols in grid]) * (1.0 / entries)
-
-    def graft(slot, block, raw):
-        grad_power = power(lambda rows, cols: block[rows, cols].astype(f32))
-        scale = jnp.sqrt(grad_power) / jnp.sqrt(power(lambda rows, cols: raw[rows, cols]) + GRAFT_EPS)
-        for rows, cols in grid:
-            put(slot, rows, cols, (raw[rows, cols] * scale).astype(bf16))
-
-    block = block_of(0)
-    others = [block_of(slot) for slot in range(1, MOST)]
-    wide[0] = mul(block, block, ((1,), (1,)))
-    wide[1] = mul(block, block, ((0,), (0,)))
-    for i in range(MOST - 1):
-        fetch["r%d" % (i + 1)].wait()
-        raws[i] = mul(others[i], roots[2 * i + 1])
-    for i in range(MOST - 1):
-        for rows, cols in grid:
-            square[i, rows, cols] = raws[i, rows, cols].astype(bf16)
-        fetch["l%d" % (i + 1)].wait()
-        raws[i] = mul(roots[2 * i], square[i])
-    sent = []
-    live = live_ref[0] > 0
     keep = jnp.where(live, DECAY_RATE, 1.0)
     take = jnp.where(live, 1.0 - DECAY_RATE, 0.0)
     scales = []
-    for i, name in enumerate(("left", "right")):
-        fetch[name].wait()
+    for i in range(2):
         squares = []
         for rows, cols in grid:
-            tile = keep * stats[i, rows, cols] + take * wide[i, rows, cols]
+            tile = keep * stats[i, rows, cols] + take * grams[i, rows, cols]
             tile = plus_diag(tile, rows, cols, ROOT_RIDGE)
             low[i, rows, cols] = tile.astype(bf16)
             squares.append(tile * tile)
-        frob = side * jnp.sqrt(total(squares) * (1.0 / entries) + NORM_EPS)
+        frob = side * jnp.sqrt(total(squares) * (1.0 / (side * side)) + NORM_EPS)
         scales.append(2.5 / frob)
         prod[i] = mul(low[i], low[i])
-        graft(i + 1, others[i], raws.at[i])
-        sent.append(give(i + 1, out.at[:, i + 1]))
+        between()
     for i in range(2):
         one, two = scales[i], scales[i] * scales[i]
         for rows, cols in grid:
@@ -234,37 +195,102 @@
         one, two = scales[i], scales[i] * scales[i]
         for rows, cols in grid:
             tile = two * prod[i, rows, cols] + (c1 * one) * low[i, rows, cols].astype(f32)
-            tile = plus_diag(tile, rows, cols, c0).astype(bf16)
-            term[i, rows, cols] = tile
-            put(MOST + i, rows, cols, tile)
-    sent += [give(MOST, left_new), give(MOST + 1, right_new)]
+            term[i, rows, cols] = plus_diag(tile, rows, cols, c0).astype(bf16)
+
+
+def precondition_kernel(
+    live_ref, arrived_a, arrived_b, left_stats, right_stats, left_roots, right_roots, _, out,
+    done_ref, stats, roots, results, wide, prod, raws, low, square, term, in_sems, out_sems,
+):
+    side = stats.shape[-1]
+    entries = side * side
+    f32, bf16 = jnp.float32, jnp.bfloat16
+    grid = tiles(side)
+    fetch = {}
+
+    def get(name, source, target):
+        fetch[name] = pltpu.make_async_copy(source, target, in_sems.at[len(fetch)])
+        fetch[name].start()
+
+    for slot in range(1, MOST):
+        get("r%d" % slot, right_roots.at[0, 0, slot], roots.at[2 * slot - 1])
+        get("l%d" % slot, left_roots.at[0, 0, slot], roots.at[2 * slot - 2])
+    get("left", left_stats.at[0, 0, 0], stats.at[0])
+    get("right", right_stats.at[0, 0, 0], stats.at[1])
+
+    def block_of(slot):
+        halves = [half[:, slot].reshape(side, side // 2) for half in (arrived_a, arrived_b)]
+        return jnp.concatenate(halves, axis=1)
+
+    def give(slot, low=0, high=arrived_a.shape[0], part=0):
+        slabs = pl.ds(low, high - low)
+        copy = pltpu.make_async_copy(results.at[slot, slabs], out.at[slabs, slot], out_sems.at[slot + part])
+        copy.start()
+        sent.append(copy)
+
+    def put(number, rows, cols, tile):
+        slabs = slice(rows.start // 16, rows.stop // 16)
+        results[number, slabs, :, cols] = tile.reshape(ROWS // 16, 16, COLS)
+
+    def power(tile_of):
+        return total([jnp.square(tile_of(rows, cols)) for rows, cols in grid]) * (1.0 / entries)
+
+    def graft(slot, block, raw, parts=1):
+        grad_power = power(lambda rows, cols: block[rows, cols].astype(f32))
+        scale = jnp.sqrt(grad_power) / jnp.sqrt(power(lambda rows, cols: raw[rows, cols]) + GRAFT_EPS)
+        share = results.shape[1] // parts
+        for part in range(parts):
+            for rows, cols in grid:
+                if rows.start // 16 // share == part:
+                    put(slot, rows, cols, (raw[rows, cols] * scale).astype(bf16))
+            give(slot, part * share, (part + 1) * share, MOST * (part > 0) + max(part - 1, 0))
+
+    block = block_of(0)
+    others = [block_of(slot) for slot in range(1, MOST)]
+    wide[0] = mul(block, block, ((1,), (1,)))
+    wide[1] = mul(block, block, ((0,), (0,)))
+    for i in range(MOST - 1):
+        fetch["r%d" % (i + 1)].wait()
+        raws[i] = mul(others[i], roots[2 * i + 1])
+    for i in range(MOST - 1):
+        for rows, cols in grid:
+            square[i, rows, cols] = raws[i, rows, cols].astype(bf16)
+        fetch["l%d" % (i + 1)].wait()
+        raws[i] = mul(roots[2 * i], square[i])
+    sent = []
+    for i, name in enumerate(("left", "right")):
+        fetch[name].wait()
+    fill = iter(range(MOST - 1))
+
+    def between():
+        for i in fill:
+            graft(i + 1, others[i], raws.at[i])
+            break
+
+    new_roots(live_ref[0] > 0, stats, wide, low, square, term, prod, between)
     prod[0] = mul(block, term[1])
     for rows, cols in grid:
         low[0, rows, cols] = prod[0, rows, cols].astype(bf16)
     prod[1] = mul(term[0], low[0])
-    graft(0, block, prod.at[1])
-    sent.append(give(0, out.at[:, 0]))
+    graft(0, block, prod.at[1], PARTS)
     for copy in sent:
         copy.wait()
     done_ref[0] = 0
 
 
-def precondition(live, arrived, left_stats, right_stats, left_roots, right_roots, spent):
+def precondition(live, arrived, left_stats, right_stats, left_roots, right_roots, spare):
     owners, _, rows, width = arrived[0].shape
     side = left_stats.shape[-1]
-    root = jax.ShapeDtypeStruct((owners, rows, side), jnp.bfloat16)
     far = pl.BlockSpec(memory_space=HBM)
     return pl.pallas_call(
         precondition_kernel,
-        out_shape=[
-            jax.ShapeDtypeStruct((owners, MOST, rows, side), jnp.bfloat16), root, root, token_shape(),
-        ],
+        out_shape=[jax.ShapeDtypeStruct((owners, MOST, rows, side), jnp.bfloat16), token_shape()],
         in_specs=[pl.BlockSpec(memory_space=SMEM)] + [pl.BlockSpec(memory_space=VMEM)] * 2 + [far] * 5,
-        out_specs=[far] * 3 + [pl.BlockSpec(memory_space=SMEM)],
+        out_specs=[far, pl.BlockSpec(memory_space=SMEM)],
         scratch_shapes=[
             VMEM((2, side, side), jnp.float32),
             VMEM((2 * MOST - 2, side, side), jnp.bfloat16),
-            VMEM((MOST + 2, owners, rows, side), jnp.bfloat16),
+            VMEM((MOST, owners, rows, side), jnp.bfloat16),
             VMEM((2, side, side), jnp.float32),
             VMEM((2, side, side), jnp.float32),
             VMEM((2, side, side), jnp.float32),
@@ -272,38 +298,62 @@
             VMEM((2, side, side), jnp.bfloat16),
             VMEM((2, side, side), jnp.bfloat16),
             pltpu.SemaphoreType.DMA((2 * MOST,)),
-            pltpu.SemaphoreType.DMA((MOST + 2,)),
+            pltpu.SemaphoreType.DMA((MOST + PARTS - 1,)),
         ],
         compiler_params=pltpu.CompilerParams(vmem_limit_bytes=VMEM_MOST),
         cost_estimate=cost(14, side, 9 * side * side * 4),
         input_output_aliases={7: 0},
         name="precondition",
-    )(live, *arrived, left_stats, right_stats, left_roots, right_roots, spent)
-
-
-def stats_kernel(live_ref, front_ref, back_ref, lprev_ref, rprev_ref, _, left_ref, right_ref):
+    )(live, *arrived, left_stats, right_stats, left_roots, right_roots, spare)
+
+
+def stats_kernel(
+    live_ref, front_ref, back_ref, lprev_ref, rprev_ref, _, left_ref, right_ref, lroot_ref, rroot_ref,
+    stats, grams, low, square, term, prod,
+):
     side = lprev_ref.shape[-1]
     block = jnp.concatenate([front_ref[:, 0], back_ref[:, 0]], axis=-1).reshape(side, side)
     live = live_ref[pl.program_id(0)] > 0
-    left_ref[0, 0, 0] = blend(live, lprev_ref[0, 0, 0], mul(block, block, ((1,), (1,))))
-    right_ref[0, 0, 0] = blend(live, rprev_ref[0, 0, 0], mul(block, block, ((0,), (0,))))
+    grams[0] = mul(block, block, ((1,), (1,)))
+    grams[1] = mul(block, block, ((0,), (0,)))
+    for rows, cols in tiles(side):
+        left_ref[0, 0, 0, rows, cols] = blend(live, lprev_ref[0, 0, 0, rows, cols], grams[0, rows, cols])
+        right_ref[0, 0, 0, rows, cols] = blend(live, rprev_ref[0, 0, 0, rows, cols], grams[1, rows, cols])
+
+    @pl.when(pl.program_id(0) == 0)
+    def _():
+        stats[0] = lprev_ref[0, 0, 0]
+        stats[1] = rprev_ref[0, 0, 0]
+        new_roots(live, stats, grams, low, square, term, prod, lambda: None)
+        lroot_ref[0, 0] = term[0]
+        rroot_ref[0, 0] = term[1]
 
 
 def update_stats(live, arrived, left_stats, right_stats, tied):
     owners, _, rows, width = arrived[0].shape
     side = left_stats.shape[-1]
     at_slot = pl.BlockSpec((1, 1, 1, side, side), lambda s: (0, 0, s, 0, 0))
+    of_first = pl.BlockSpec((1, 1, side, side), lambda s: (0, 0, 0, 0))
     shape = jax.ShapeDtypeStruct(left_stats.shape, jnp.float32)
+    root = jax.ShapeDtypeStruct((1, 1, side, side), jnp.bfloat16)
     return pl.pallas_call(
         stats_kernel,
         grid=(MOST,),
-        out_shape=[shape, shape],
+        out_shape=[shape, shape, root, root],
         in_specs=[pl.BlockSpec(memory_space=SMEM)]
         + [pl.BlockSpec((owners, 1, rows, width), lambda s: (0, s, 0, 0))] * 2
         + [at_slot, at_slot, pl.BlockSpec(memory_space=SMEM)],
-        out_specs=[at_slot, at_slot],
+        out_specs=[at_slot, at_slot, of_first, of_first],
+        scratch_shapes=[
+            VMEM((2, side, side), jnp.float32),
+            VMEM((2, side, side), jnp.float32),
+            VMEM((2, side, side), jnp.bfloat16),
+            VMEM((2, side, side), jnp.bfloat16),
+            VMEM((2, side, side), jnp.bfloat16),
+            VMEM((2, side, side), jnp.float32),
+        ],
         compiler_params=pltpu.CompilerParams(vmem_limit_bytes=VMEM_MOST),
-        cost_estimate=cost(2 * MOST, side, 13 * side * side * 4),
+        cost_estimate=cost(2 * MOST + 6, side, 13 * side * side * 4),
         name="update_stats",
     )(live, *arrived, left_stats, right_stats, tied)
 
@@ -359,7 +409,7 @@
     up = [(i, (i + 1) % groups) for i in range(groups)]
     down = [(i, (i - 1) % groups) for i in range(groups)]
 
-    owner = lax.dynamic_slice_in_dim(owner_table[:, 0], group_id * share, share)
+    owner = lax.dynamic_slice(owner_table[:, 0], (group_id * share,), (share,), allow_negative_indices=False)
     slot, place, empty = routing(owner, owners)
     own_count = jnp.sum((owner == owner_id).astype(jnp.int32))
     live = (jnp.arange(MOST, dtype=jnp.int32) < own_count).astype(jnp.int32)
@@ -367,8 +417,10 @@
     width = side // 2
 
     def part(source, ahead, low, column):
-        start = (group_id + ahead) % groups * share + low
-        return lax.dynamic_slice(source, (start, 0, column), (half, slab_rows, width))
+        start = ((group_id + ahead) & (groups - 1)) * share + low
+        return lax.dynamic_slice(
+            source, (start, 0, column), (half, slab_rows, width), allow_negative_indices=False
+        )
 
     def send(pair):
         return lax.ppermute(pair[0], "rep", up), lax.ppermute(pair[1], "rep", down)
@@ -400,33 +452,32 @@
     sums = own_sums(local, 0, up2, down2)
     up1, down1 = send(firsts_b)
     up2, down2 = send(seconds_b)
-    (outgoing_a,) = place_blocks(place, empty, sums[0], up3, sums[1], down3, *firsts_b, *seconds_b)
+    spare, made = spare_room(empty, (owners, MOST, slab_rows, side))
+    outgoing_a = place_blocks(place, empty, sums[0], up3, sums[1], down3, *firsts_b, *seconds_b, made)
     mid = mids(later, width)
     third = add_pairs(mid[0], up1, mid[1], down1, outgoing_a)
     up3, down3 = send(third)
     later, _ = lax.optimization_barrier((later, third))
     sums = own_sums(later, width, up2, down2)
-    outgoing_b, spent = place_blocks(
-        place, empty, sums[0], up3, sums[1], down3, room=(owners, MOST, slab_rows, side)
-    )
+    outgoing_b = place_blocks(place, empty, sums[0], up3, sums[1], down3)
     arrived = [
         lax.all_to_all(
             outgoing.reshape(owners, MOST, slab_rows, width), "fsdp", split_axis=0, concat_axis=0, tiled=True
         )
         for outgoing in (outgoing_a, outgoing_b)
     ]
-    results, left_new, right_new, done = precondition(
-        live, arrived, left_stats, right_stats, left_roots, right_roots, spent
+    results, done = precondition(
+        live, arrived, left_stats, right_stats, left_roots, right_roots, spare
     )
     returned = lax.all_to_all(results, "fsdp", split_axis=0, concat_axis=0, tiled=True)
-    left_out, right_out = update_stats(live, arrived, left_stats, right_stats, done)
+    left_out, right_out, left_new, right_new = update_stats(live, arrived, left_stats, right_stats, done)
     preconditioned = assemble(slot, owner, returned)
     return (
         preconditioned,
         left_out,
         right_out,
-        left_new.reshape(1, 1, side, side),
-        right_new.reshape(1, 1, side, side),
+        left_new,
+        right_new,
     )
 
 

time: 111 us -> 110 us (level)
  waiting for transfers between devices: 41.6 us -> 36.2 us
  Pallas kernels: 22.2 us -> 27.4 us
  local copies, waits for them, and re-layouts: 6.42 us -> 5.29 us
    pallas_call x3 -> x4, Pallas kernels: 11 us -> 16.4 us  [the longest x1 11.5 us: update_stats(): pl.pallas_call(stats_kernel, grid=(MOST,), out_shape=[shape, shape, root,...]
    all_to_all x1, waiting for transfers between devices: 16 us -> 12.3 us  [on_device(): lax.all_to_all(results, 'fsdp', split_axis=0, concat_axis=0, tiled=True)]
    ppermute x6, waiting for transfers between devices: 9.41 us -> 6.81 us  [send(): lax.ppermute(pair[0], 'rep', up)]
    all_to_all x2, waiting for transfers between devices: 15.9 us -> 17 us  [on_device(): lax.all_to_all(outgoing.reshape(owners, MOST, slab_rows, width), 'fsdp',...]
    all_to_all x2, starting transfers between devices: 13.7 us -> 12.6 us  [on_device(): lax.all_to_all(outgoing.reshape(owners, MOST, slab_rows, width), 'fsdp',...]
    unnamed x14 -> x12, local copies, waits for them, and re-layouts: 2.06 us -> 0.92 us
  transfers between devices with their start and end apart: 15 -> 15, of which waited for: 7 -> 5; matrix products, arithmetic and copies ran while one was open for 8% -> 9% of each run, Pallas kernels for 10% -> 15%
where the time goes in v3:
time: 110 us; the launch traced here: 109 us
  waiting for transfers between devices  36.2 us (33%)
  starting transfers between devices  32.6 us (30%)
  Pallas kernels  27.4 us (25%)
  other arithmetic  6.44 us (6%)
  local copies, waits for them, and re-layouts  5.29 us (5%)
    all_to_all x2, waiting for transfers between devices, on_device(): lax.all_to_all(outgoing.reshape(owners, MOST, slab_rows, width), 'fsdp',...  17 us
    all_to_all x2, starting transfers between devices, on_device(): lax.all_to_all(outgoing.reshape(owners, MOST, slab_rows, width), 'fsdp',...  12.6 us
    all_to_all x1, waiting for transfers between devices, on_device(): lax.all_to_all(results, 'fsdp', split_axis=0, concat_axis=0, tiled=True)  12.3 us
    pallas_call x1, Pallas kernels, update_stats(): pl.pallas_call(stats_kernel, grid=(MOST,), out_shape=[shape, shape, root,...  11.5 us
    ppermute x6, starting transfers between devices, send(): lax.ppermute(pair[1], 'rep', down)  10.5 us
    pallas_call x1, Pallas kernels, precondition(): pl.pallas_call(precondition_kernel, out_shape=[jax.ShapeDtypeStruct((owne...  9.41 us
    ppermute x6, waiting for transfers between devices, send(): lax.ppermute(pair[0], 'rep', up)  6.81 us
    ppermute x6, starting transfers between devices, send(): lax.ppermute(pair[0], 'rep', up)  5.29 us
  transfers between devices with their start and end apart: 15, of which 5 were waited for; matrix products, arithmetic and copies ran while one was open for 9% of the time, Pallas kernels for 15%

profile of v3, /device:TPU:0, one launch (start us, length us, event | category | flops | bytes accessed | tf_op | source)
XLA Modules:
  0.0 108.8 jit_solution(17418230152466052617)
XLA Ops:
  0.6 1.1 dynamic-slice_bitcast_fusion
  1.7 2.9 %collective-permute-start.4 = (bf16[32,16,256]{2,1,0:T(8,128)(2,1)S(1)}, bf16[32,16,256]{2,1,0:T(8,128)(2,1)S(1)}, u32[]{:S(2)}, u32[]{:S(2)}) collective-permute-start(bf16[32,16,256]{2,1,0:T(8,128)(2,1)S(1)} %get-tuple-element.49), channel_id=1, source_target_pairs={{0,96},{32,0},{64,32},{96,64},{1,97},{33,1},{65,33},{97,65},{2,98}... | collective-permute-start | bytes 786440 | tf_op jit(solution)/shard_map/ppermute | solution.py:426
  4.6 1.1 constant_dynamic-slice_fusion.6
  5.7 0.8 collective-permute-start.3
  6.5 2.6 %collective-permute-start = (bf16[32,16,256]{2,1,0:T(8,128)(2,1)S(1)}, bf16[32,16,256]{2,1,0:T(8,128)(2,1)S(1)}, u32[]{:S(2)}, u32[]{:S(2)}) collective-permute-start(bf16[32,16,256]{2,1,0:T(8,128)(2,1)S(1)} %get-tuple-element.48), channel_id=1, source_target_pairs={{0,96},{32,0},{64,32},{96,64},{1,97},{33,1},{65,33},{97,65},{2,98}... | collective-permute-start | bytes 786440 | tf_op jit(solution)/shard_map/ppermute | solution.py:426
  9.1 1.4 %fusion.1 = (s32[]{:T(128)}, s32[64]{0:T(128)S(1)}) fusion(s32[]{:T(128)S(6)} %axis_index.25, s32[256,1]{0,1:T(1,128)} %param.7, s32[]{:T(128)S(6)} %mul.18), kind=kLoop, calls=%fused_computation.24 | loop fusion | flops 191 | bytes 524 | tf_op jit(solution)/shard_map/reduce_sum | solution.py:414
  11.0 0.5 copy-done.4
  11.6 0.5 broadcast_subtract_fusion._.empty_ref
  12.1 1.2 %spare_room.1 = (bf16[32,3,16,512]{3,2,1,0:T(8,128)(2,1)}, s32[1]{0:T(128)}) custom-call(s32[96]{0:T(128)} %broadcast_subtract_fusion._.empty_ref), custom_call_target="tpu_custom_call" | custom-call | tf_op jit(solution)/shard_map/spare_room/pallas_call | solution.py:78
  13.3 1.7 %collective-permute-done.1 = bf16[32,16,256]{2,1,0:T(8,128)(2,1)S(1)} collective-permute-done((bf16[32,16,256]{2,1,0:T(8,128)(2,1)S(1)}, bf16[32,16,256]{2,1,0:T(8,128)(2,1)S(1)}, u32[]{:S(2)}, u32[]{:S(2)}) %collective-permute-start.1) | collective-permute-done | bytes 262176 | tf_op jit(solution)/shard_map/ppermute | solution.py:426
  15.1 1.1 %dynamic-slice_add_fusion = (bf16[32,16,256]{2,1,0:T(8,128)(2,1)S(1)}, bf16[32,16,256]{2,1,0:T(8,128)(2,1)S(1)}) fusion(bf16[32,16,256]{2,1,0:T(8,128)(2,1)S(1)} %collective-permute-done.4, bf16[256,16,512]{2,1,0:T(8,128)(2,1)} %bitcast.17, s32[]{:T(128)S(6)} %add.65, bf16[32,16,256]{2,1,0:T(8,128)(2,1)S(1)} %collective-permute-done.1, s32[]{:T(128)S(6)} %mul.43), kind=kLoop, calls=%fused_computation.4 | loop fusion | flops 262144 | bytes 1572872 | tf_op jit(solution)/shard_map/add | solution.py:448
  16.5 1.8 %collective-permute-start.2 = (bf16[32,16,256]{2,1,0:T(8,128)(2,1)S(1)}, bf16[32,16,256]{2,1,0:T(8,128)(2,1)S(1)}, u32[]{:S(2)}, u32[]{:S(2)}) collective-permute-start(bf16[32,16,256]{2,1,0:T(8,128)(2,1)S(1)} %get-tuple-element.44), channel_id=1, source_target_pairs={{0,32},{32,64},{64,96},{96,0},{1,33},{33,65},{65,97},{97,1},{2,34}... | collective-permute-start | bytes 786440 | tf_op jit(solution)/shard_map/ppermute | solution.py:426
  18.3 2.2 %constant_dynamic-slice_fusion = (bf16[32,16,256]{2,1,0:T(8,128)(2,1)S(1)}, bf16[32,16,256]{2,1,0:T(8,128)(2,1)S(1)}, bf16[32,16,256]{2,1,0:T(8,128)(2,1)}, bf16...) fusion(bf16[256,16,512]{2,1,0:T(8,128)(2,1)} %bitcast.18, ...), kind=kLoop, calls=%fused_computation.13 | loop fusion | bytes 3145752 | tf_op jit(solution)/shard_map/dynamic_slice | solution.py:421
  20.5 1.4 %collective-permute-start.8 = (bf16[32,16,256]{2,1,0:T(8,128)(2,1)}, bf16[32,16,256]{2,1,0:T(8,128)(2,1)}, u32[]{:S(2)}, u32[]{:S(2)}) collective-permute-start(bf16[32,16,256]{2,1,0:T(8,128)(2,1)} %get-tuple-element.39.rest_3_), channel_id=1, source_target_pairs={{0,96},{32,0},{64,32},{96,64},{1,97},{33,1},{65,33},{97,65},{2,98}... | collective-permute-start | bytes 786440 | tf_op jit(solution)/shard_map/ppermute | solution.py:426
  22.0 2.0 %collective-permute-start.6 = (bf16[32,16,256]{2,1,0:T(8,128)(2,1)S(1)}, bf16[32,16,256]{2,1,0:T(8,128)(2,1)S(1)}, u32[]{:S(2)}, u32[]{:S(2)}) collective-permute-start(bf16[32,16,256]{2,1,0:T(8,128)(2,1)S(1)} %get-tuple-element.42.rest_0_), channel_id=1, source_target_pairs={{0,32},{32,64},{64,96},{96,0},{1,33},{33,65},{65,97},{97,1},{2,34}... | collective-permute-start | bytes 786440 | tf_op jit(solution)/shard_map/ppermute | solution.py:426
  24.0 1.2 %convert_add_fusion = (f32[32,16,256]{2,1,0:T(8,128)S(1)}, f32[32,16,256]{2,1,0:T(8,128)S(1)}) fusion(bf16[32,16,256]{2,1,0:T(8,128)(2,1)S(1)} %collective-permute-done.3, bf16[1,256,16,512]{3,2,1,0:T(8,128)(2,1)} %param.6, s32[]{:T(128)S(6)} %add.63, bf16[32,16,256]{2,1,0:T(8,128)(2,1)S(1)} %collective-permute-done, s32[]{:T(128)S(6)} %mul.40), kind=kLoop, calls=%fused_computation | loop fusion | flops 786432 | bytes 2097160 | tf_op jit(solution)/shard_map/add | solution.py:439
  25.2 0.6 collective-permute-start.10
  25.9 2.2 %place_blocks.2.rest_0_ = bf16[96,16,256]{2,1,0:T(8,128)(2,1)} custom-call(s32[64]{0:T(128)S(1)} %multiply_add_fusion.place_ref, s32[96]{0:T(128)S(1)} %copy-done.2, f32[32,16,256]{2,1,0:T(8,128)S(1)} %get-tuple-element.46.front_ref, bf16[32,16,256]{2,1,0:T(8,128)(2,1)S(1)} %collective-permute-done.2.up_ref, f32[32,16,256]{2,1,0:T(8,128)S(1)} %get-tuple-element.45.back_ref, ...), custom_call_target="tpu_custom_call" | custom-call | bytes 2097152 | tf_op jit(solution)/shard_map/place_blocks/pallas_call | solution.py:118
  28.1 8.5 %all-to-all-start = ((bf16[32,3,16,256]{3,2,1,0:T(8,128)(2,1)}), bf16[32,3,16,256]{3,2,1,0:T(8,128)(2,1)}, u32[]{:S(2)}, u32[]{:S(2)}) async-start(bf16[32,3,16,256]{3,2,1,0:T(8,128)(2,1)} %bitcast.6), calls=%async_computation | async-start | bytes 1572864 | tf_op jit(solution)/shard_map/all_to_all | solution.py:464
  36.8 3.2 %collective-permute-start.11 = (bf16[32,16,256]{2,1,0:T(8,128)(2,1)S(1)}, bf16[32,16,256]{2,1,0:T(8,128)(2,1)S(1)}, u32[]{:S(2)}, u32[]{:S(2)}) collective-permute-start(bf16[32,16,256]{2,1,0:T(8,128)(2,1)S(1)} %get-tuple-element.24), channel_id=1, source_target_pairs={{0,96},{32,0},{64,32},{96,64},{1,97},{33,1},{65,33},{97,65},{2,98}... | collective-permute-start | bytes 786440 | tf_op jit(solution)/shard_map/ppermute | solution.py:426
  40.0 1.3 %convert_add_fusion.2 = (f32[32,16,256]{2,1,0:T(8,128)S(1)}, f32[32,16,256]{2,1,0:T(8,128)S(1)}) fusion(bf16[32,16,256]{2,1,0:T(8,128)(2,1)} %collective-permute-done.10, bf16[256,16,512]{2,1,0:T(8,128)(2,1)} %bitcast.19, s32[]{:T(128)S(6)} %add.63, bf16[32,16,256]{2,1,0:T(8,128)(2,1)} %collective-permute-done.8, s32[]{:T(128)S(6)} %mul.40), kind=kLoop, calls=%fused_computation.2 | loop fusion | flops 786432 | bytes 2097160 | tf_op jit(solution)/shard_map/add | solution.py:439
  41.3 5.0 %collective-permute-done.9.up_ref = bf16[32,16,256]{2,1,0:T(8,128)(2,1)S(1)} collective-permute-done((bf16[32,16,256]{2,1,0:T(8,128)(2,1)S(1)}, bf16[32,16,256]{2,1,0:T(8,128)(2,1)S(1)}, u32[]{:S(2)}, u32[]{:S(2)}) %collective-permute-start.9) | collective-permute-done | bytes 262176 | tf_op jit(solution)/shard_map/ppermute | solution.py:426
  46.4 1.6 %place_blocks.3 = bf16[96,16,256]{2,1,0:T(8,128)(2,1)} custom-call(s32[64]{0:T(128)S(1)} %multiply_add_fusion.place_ref, s32[96]{0:T(128)S(1)} %copy-done.3, f32[32,16,256]{2,1,0:T(8,128)S(1)} %get-tuple-element.36.front_ref, bf16[32,16,256]{2,1,0:T(8,128)(2,1)S(1)} %collective-permute-done.9.up_ref, f32[32,16,256]{2,1,0:T(8,128)S(1)} %get-tuple-element.35.back_ref, ...), custom_call_target="tpu_custom_call" | custom-call | bytes 2097152 | tf_op jit(solution)/shard_map/place_blocks/pallas_call | solution.py:118
  48.0 3.2 %all-to-all-done.arrived_a.front_ref = bf16[32,3,16,256]{3,2,1,0:T(8,128)(2,1)} async-done(((bf16[32,3,16,256]{3,2,1,0:T(8,128)(2,1)}), bf16[32,3,16,256]{3,2,1,0:T(8,128)(2,1)}, u32[]{:S(2)}, u32[]{:S(2)}) %all-to-all-start) | async-done | bytes 786464 | tf_op jit(solution)/shard_map/all_to_all | solution.py:464
  51.1 4.1 %all-to-all-start.1 = ((bf16[32,3,16,256]{3,2,1,0:T(8,128)(2,1)}), bf16[32,3,16,256]{3,2,1,0:T(8,128)(2,1)S(1)}, u32[]{:S(2)}, u32[]{:S(2)}) async-start(bf16[32,3,16,256]{3,2,1,0:T(8,128)(2,1)} %bitcast.7), calls=%async_computation.1 | async-start | bytes 1572864 | tf_op jit(solution)/shard_map/all_to_all | solution.py:464
  55.3 0.7 compare_convert_fusion.live_ref
  55.9 13.9 %all-to-all-done.1.arrived_b.back_ref = bf16[32,3,16,256]{3,2,1,0:T(8,128)(2,1)S(1)} async-done(((bf16[32,3,16,256]{3,2,1,0:T(8,128)(2,1)}), bf16[32,3,16,256]{3,2,1,0:T(8,128)(2,1)S(1)}, u32[]{:S(2)}, u32[]{:S(2)}) %all-to-all-start.1) | async-done | bytes 786464 | tf_op jit(solution)/shard_map/all_to_all | solution.py:464
  69.8 9.4 %precondition.1 = (bf16[32,3,16,512]{3,2,1,0:T(8,128)(2,1)}, s32[1]{0:T(128)}) custom-call(s32[3]{0:T(128)S(1)} %compare_convert_fusion.live_ref, bf16[32,3,16,256]{3,2,1,0:T(8,128)(2,1)} %all-to-all-done.arrived_a.front_ref, bf16[32,3,16,256]{3,2,1,0:T(8,128)(2,1)S(1)} %all-to-all-done.1.arrived_b.back_ref, ...), custom_call_target="tpu_custom_call", output_to_operand_aliasing={{0}: (7, {})} | custom-call | flops 3758096384 | bytes 9437184 | tf_op jit(solution)/shard_map/precondition/pallas_call | solution.py:285
  79.2 4.2 %all-to-all-start.2 = ((bf16[32,3,16,512]{3,2,1,0:T(8,128)(2,1)}), bf16[32,3,16,512]{3,2,1,0:T(8,128)(2,1)S(1)}, u32[]{:S(2)}, u32[]{:S(2)}) async-start(bf16[32,3,16,512]{3,2,1,0:T(8,128)(2,1)} %get-tuple-element.27), calls=%async_computation.2 | async-start | bytes 3145728 | tf_op jit(solution)/shard_map/all_to_all | solution.py:472
  83.4 11.5 %update_stats.1 = (f32[1,1,3,512,512]{4,3,2,1,0:T(8,128)}, f32[1,1,3,512,512]{4,3,2,1,0:T(8,128)}, bf16[1,1,512,512]{3,2,1,0:T(8,128)(2,1)}, bf16[1,1,512,512]{3,2,1,0:T(8,128)(2,1)}) custom-call(s32[3]{0:T(128)S(1)} %compare_convert_fusion.live_ref, bf16[32,3,16,256]{3,2,1,0:T(8,128)(2,1)} %all-to-all-done.arrived_a.front_ref, ...), custom_call_target="tpu_custom_call" | custom-call | flops 3221225472 | bytes 13631488 | tf_op jit(solution)/shard_map/update_stats/pallas_call | solution.py:339
  94.9 12.3 %all-to-all-done.2.back_ref = bf16[32,3,16,512]{3,2,1,0:T(8,128)(2,1)S(1)} async-done(((bf16[32,3,16,512]{3,2,1,0:T(8,128)(2,1)}), bf16[32,3,16,512]{3,2,1,0:T(8,128)(2,1)S(1)}, u32[]{:S(2)}, u32[]{:S(2)}) %all-to-all-start.2) | async-done | bytes 1572896 | tf_op jit(solution)/shard_map/all_to_all | solution.py:472
  107.2 1.5 %assemble.1 = bf16[64,16,512]{2,1,0:T(8,128)(2,1)} custom-call(s32[64]{0:T(128)S(1)} %copy-done.5, s32[64]{0:T(128)S(1)} %copy-done.1, bf16[32,3,16,512]{3,2,1,0:T(8,128)(2,1)S(1)} %all-to-all-done.2.back_ref), custom_call_target="tpu_custom_call" | custom-call | bytes 2097152 | tf_op jit(solution)/shard_map/assemble/pallas_call | solution.py:375
  (29 shorter events, 1.3 us)
Async XLA Ops:
  1.7 11.6 %collective-permute-start.4 = (bf16[32,16,256]{2,1,0:T(8,128)(2,1)S(1)}, bf16[32,16,256]{2,1,0:T(8,128)(2,1)S(1)}, u32[]{:S(2)}, u32[]{:S(2)}) collective-permute-start(bf16[32,16,256]{2,1,0:T(8,128)(2,1)S(1)} %get-tuple-element.49), channel_id=1, source_target_pairs={{0,96},{32,0},{64,32},{96,64},{1,97},{33,1},{65,33},{97,65},{2,98}... | collective-permute-start | bytes 786440 | tf_op jit(solution)/shard_map/ppermute | solution.py:426
  4.6 10.4 %collective-permute-start.1 = (bf16[32,16,256]{2,1,0:T(8,128)(2,1)S(1)}, bf16[32,16,256]{2,1,0:T(8,128)(2,1)S(1)}, u32[]{:S(2)}, u32[]{:S(2)}) collective-permute-start(bf16[32,16,256]{2,1,0:T(8,128)(2,1)S(1)} %get-tuple-element.50), channel_id=1, source_target_pairs={{0,32},{32,64},{64,96},{96,0},{1,33},{33,65},{65,97},{97,1},{2,34}... | collective-permute-start | bytes 786440 | tf_op jit(solution)/shard_map/ppermute | solution.py:426
  5.7 16.3 %collective-permute-start.3 = (bf16[32,16,256]{2,1,0:T(8,128)(2,1)S(1)}, bf16[32,16,256]{2,1,0:T(8,128)(2,1)S(1)}, u32[]{:S(2)}, u32[]{:S(2)}) collective-permute-start(bf16[32,16,256]{2,1,0:T(8,128)(2,1)S(1)} %get-tuple-element.47), channel_id=1, source_target_pairs={{0,32},{32,64},{64,96},{96,0},{1,33},{33,65},{65,97},{97,1},{2,34}... | collective-permute-start | bytes 786440 | tf_op jit(solution)/shard_map/ppermute | solution.py:426
  6.5 15.5 %collective-permute-start = (bf16[32,16,256]{2,1,0:T(8,128)(2,1)S(1)}, bf16[32,16,256]{2,1,0:T(8,128)(2,1)S(1)}, u32[]{:S(2)}, u32[]{:S(2)}) collective-permute-start(bf16[32,16,256]{2,1,0:T(8,128)(2,1)S(1)} %get-tuple-element.48), channel_id=1, source_target_pairs={{0,96},{32,0},{64,32},{96,64},{1,97},{33,1},{65,33},{97,65},{2,98}... | collective-permute-start | bytes 786440 | tf_op jit(solution)/shard_map/ppermute | solution.py:426
  10.4 0.6 copy-start
  11.0 0.5 copy-start.4
  13.3 12.6 %copy-start.2 = (s32[96]{0:T(128)S(1)}, s32[96]{0:T(128)}, u32[]{:S(2)}) copy-start(s32[96]{0:T(128)} %broadcast_subtract_fusion._.empty_ref) | copy-start | bytes 1156
  16.2 9.0 %collective-permute-start.5 = (bf16[32,16,256]{2,1,0:T(8,128)(2,1)S(1)}, bf16[32,16,256]{2,1,0:T(8,128)(2,1)S(1)}, u32[]{:S(2)}, u32[]{:S(2)}) collective-permute-start(bf16[32,16,256]{2,1,0:T(8,128)(2,1)S(1)} %get-tuple-element.43), channel_id=1, source_target_pairs={{0,96},{32,0},{64,32},{96,64},{1,97},{33,1},{65,33},{97,65},{2,98}... | collective-permute-start | bytes 786440 | tf_op jit(solution)/shard_map/ppermute | solution.py:426
  16.5 9.4 %collective-permute-start.2 = (bf16[32,16,256]{2,1,0:T(8,128)(2,1)S(1)}, bf16[32,16,256]{2,1,0:T(8,128)(2,1)S(1)}, u32[]{:S(2)}, u32[]{:S(2)}) collective-permute-start(bf16[32,16,256]{2,1,0:T(8,128)(2,1)S(1)} %get-tuple-element.44), channel_id=1, source_target_pairs={{0,32},{32,64},{64,96},{96,0},{1,33},{33,65},{65,97},{97,1},{2,34}... | collective-permute-start | bytes 786440 | tf_op jit(solution)/shard_map/ppermute | solution.py:426
  20.5 19.5 %collective-permute-start.8 = (bf16[32,16,256]{2,1,0:T(8,128)(2,1)}, bf16[32,16,256]{2,1,0:T(8,128)(2,1)}, u32[]{:S(2)}, u32[]{:S(2)}) collective-permute-start(bf16[32,16,256]{2,1,0:T(8,128)(2,1)} %get-tuple-element.39.rest_3_), channel_id=1, source_target_pairs={{0,96},{32,0},{64,32},{96,64},{1,97},{33,1},{65,33},{97,65},{2,98}... | collective-permute-start | bytes 786440 | tf_op jit(solution)/shard_map/ppermute | solution.py:426
  22.0 14.6 %collective-permute-start.7 = (bf16[32,16,256]{2,1,0:T(8,128)(2,1)S(1)}, bf16[32,16,256]{2,1,0:T(8,128)(2,1)S(1)}, u32[]{:S(2)}, u32[]{:S(2)}) collective-permute-start(bf16[32,16,256]{2,1,0:T(8,128)(2,1)S(1)} %get-tuple-element.41.rest_1_), channel_id=1, source_target_pairs={{0,96},{32,0},{64,32},{96,64},{1,97},{33,1},{65,33},{97,65},{2,98}... | collective-permute-start | bytes 786440 | tf_op jit(solution)/shard_map/ppermute | solution.py:426
  22.0 14.6 %collective-permute-start.6 = (bf16[32,16,256]{2,1,0:T(8,128)(2,1)S(1)}, bf16[32,16,256]{2,1,0:T(8,128)(2,1)S(1)}, u32[]{:S(2)}, u32[]{:S(2)}) collective-permute-start(bf16[32,16,256]{2,1,0:T(8,128)(2,1)S(1)} %get-tuple-element.42.rest_0_), channel_id=1, source_target_pairs={{0,32},{32,64},{64,96},{96,0},{1,33},{33,65},{65,97},{97,1},{2,34}... | collective-permute-start | bytes 786440 | tf_op jit(solution)/shard_map/ppermute | solution.py:426
  25.2 14.8 %collective-permute-start.10 = (bf16[32,16,256]{2,1,0:T(8,128)(2,1)}, bf16[32,16,256]{2,1,0:T(8,128)(2,1)}, u32[]{:S(2)}, u32[]{:S(2)}) collective-permute-start(bf16[32,16,256]{2,1,0:T(8,128)(2,1)} %get-tuple-element.40.rest_2_), channel_id=1, source_target_pairs={{0,32},{32,64},{64,96},{96,0},{1,33},{33,65},{65,97},{97,1},{2,34}... | collective-permute-start | bytes 786440 | tf_op jit(solution)/shard_map/ppermute | solution.py:426
  28.1 23.0 %all-to-all-start = ((bf16[32,3,16,256]{3,2,1,0:T(8,128)(2,1)}), bf16[32,3,16,256]{3,2,1,0:T(8,128)(2,1)}, u32[]{:S(2)}, u32[]{:S(2)}) async-start(bf16[32,3,16,256]{3,2,1,0:T(8,128)(2,1)} %bitcast.6), calls=%async_computation | async-start | bytes 1572864 | tf_op jit(solution)/shard_map/all_to_all | solution.py:464
  36.6 9.8 %copy-start.3 = (s32[96]{0:T(128)S(1)}, s32[96]{0:T(128)}, u32[]{:S(2)}) copy-start(s32[96]{0:T(128)} %broadcast_subtract_fusion._.empty_ref) | copy-start | bytes 1156
  36.7 9.7 %collective-permute-start.9 = (bf16[32,16,256]{2,1,0:T(8,128)(2,1)S(1)}, bf16[32,16,256]{2,1,0:T(8,128)(2,1)S(1)}, u32[]{:S(2)}, u32[]{:S(2)}) collective-permute-start(bf16[32,16,256]{2,1,0:T(8,128)(2,1)S(1)} %get-tuple-element.23), channel_id=1, source_target_pairs={{0,32},{32,64},{64,96},{96,0},{1,33},{33,65},{65,97},{97,1},{2,34}... | collective-permute-start | bytes 786440 | tf_op jit(solution)/shard_map/ppermute | solution.py:426
  36.8 9.6 %collective-permute-start.11 = (bf16[32,16,256]{2,1,0:T(8,128)(2,1)S(1)}, bf16[32,16,256]{2,1,0:T(8,128)(2,1)S(1)}, u32[]{:S(2)}, u32[]{:S(2)}) collective-permute-start(bf16[32,16,256]{2,1,0:T(8,128)(2,1)S(1)} %get-tuple-element.24), channel_id=1, source_target_pairs={{0,96},{32,0},{64,32},{96,64},{1,97},{33,1},{65,33},{97,65},{2,98}... | collective-permute-start | bytes 786440 | tf_op jit(solution)/shard_map/ppermute | solution.py:426
  51.1 18.7 %all-to-all-start.1 = ((bf16[32,3,16,256]{3,2,1,0:T(8,128)(2,1)}), bf16[32,3,16,256]{3,2,1,0:T(8,128)(2,1)S(1)}, u32[]{:S(2)}, u32[]{:S(2)}) async-start(bf16[32,3,16,256]{3,2,1,0:T(8,128)(2,1)} %bitcast.7), calls=%async_computation.1 | async-start | bytes 1572864 | tf_op jit(solution)/shard_map/all_to_all | solution.py:464
  79.2 27.9 %all-to-all-start.2 = ((bf16[32,3,16,512]{3,2,1,0:T(8,128)(2,1)}), bf16[32,3,16,512]{3,2,1,0:T(8,128)(2,1)S(1)}, u32[]{:S(2)}, u32[]{:S(2)}) async-start(bf16[32,3,16,512]{3,2,1,0:T(8,128)(2,1)} %get-tuple-element.27), calls=%async_computation.2 | async-start | bytes 3145728 | tf_op jit(solution)/shard_map/all_to_all | solution.py:472
  83.4 23.8 %copy-start.1 = (s32[64]{0:T(128)S(1)}, s32[64]{0:T(128)}, u32[]{:S(2)}) copy-start(s32[64]{0:T(128)} %copy-done) | copy-start | bytes 772
  83.4 23.7 %copy-start.5 = (s32[64]{0:T(128)S(1)}, s32[64]{0:T(128)}, u32[]{:S(2)}) copy-start(s32[64]{0:T(128)} %copy-done.4) | copy-start | bytes 772

commit v4 on v3

--- a/solution.py
+++ b/solution.py
@@ -40,6 +40,7 @@
     return jnp.where(live, DECAY_RATE * prev + (1.0 - DECAY_RATE) * gram, prev)
 
 
+PIECE = 256
 ROWS = 64
 COLS = 128
 PARTS = 4
@@ -51,6 +52,17 @@
         for row in range(0, side, ROWS)
         for col in range(0, side, COLS)
     ]
+
+
+def product(left, right, use):
+    side = left.shape[0]
+    for row in range(0, side, PIECE):
+        for col in range(0, side, PIECE):
+            piece = mul(left[row : row + PIECE, :], right[:, col : col + PIECE])
+            for r in range(0, PIECE, ROWS):
+                for c in range(0, PIECE, COLS):
+                    rows, cols = slice(row + r, row + r + ROWS), slice(col + c, col + c + COLS)
+                    use(piece[r : r + ROWS, c : c + COLS], rows, cols)
 
 
 def plus_diag(tile, rows, cols, value):
@@ -158,49 +170,54 @@
     )(one, two, three, four, *after)
 
 
-def new_roots(live, stats, grams, low, square, term, prod, between):
+def new_roots(live, stats, grams, low, square, inner, outer, between):
     side = stats.shape[-1]
     f32, bf16 = jnp.float32, jnp.bfloat16
     c0, c1, c2, c3, c4, c5, c6 = ROOT_POLY
-    grid = tiles(side)
     keep = jnp.where(live, DECAY_RATE, 1.0)
     take = jnp.where(live, 1.0 - DECAY_RATE, 0.0)
     scales = []
     for i in range(2):
         squares = []
-        for rows, cols in grid:
+        for rows, cols in tiles(side):
             tile = keep * stats[i, rows, cols] + take * grams[i, rows, cols]
             tile = plus_diag(tile, rows, cols, ROOT_RIDGE)
             low[i, rows, cols] = tile.astype(bf16)
             squares.append(tile * tile)
         frob = side * jnp.sqrt(total(squares) * (1.0 / (side * side)) + NORM_EPS)
         scales.append(2.5 / frob)
-        prod[i] = mul(low[i], low[i])
+
+    for i in range(2):
+        near, far = (c5 * scales[i]).astype(bf16), (c6 * scales[i] * scales[i]).astype(bf16)
+
+        def first(tile, rows, cols):
+            tile = tile.astype(bf16)
+            square[i, rows, cols] = tile
+            inner[i, rows, cols] = plus_diag(near * low[i, rows, cols] + far * tile, rows, cols, c4)
+
+        product(low[i], low[i], first)
         between()
     for i in range(2):
-        one, two = scales[i], scales[i] * scales[i]
-        for rows, cols in grid:
-            tile = prod[i, rows, cols].astype(bf16)
-            square[i, rows, cols] = tile
-            tile = (c5 * one).astype(bf16) * low[i, rows, cols] + (c6 * two).astype(bf16) * tile
-            term[i, rows, cols] = plus_diag(tile, rows, cols, c4)
-        prod[i] = mul(square[i], term[i])
-    for i in range(2):
-        one, two = scales[i], scales[i] * scales[i]
-        for rows, cols in grid:
-            tile = (two * prod[i, rows, cols]).astype(bf16) + (c3 * one).astype(bf16) * low[i, rows, cols]
-            term[i, rows, cols] = plus_diag(tile, rows, cols, c2)
-        prod[i] = mul(square[i], term[i])
+        near, far = (c3 * scales[i]).astype(bf16), scales[i] * scales[i]
+
+        def second(tile, rows, cols):
+            tile = (far * tile).astype(bf16) + near * low[i, rows, cols]
+            outer[i, rows, cols] = plus_diag(tile, rows, cols, c2)
+
+        product(square[i], inner[i], second)
     for i in (1, 0):
-        one, two = scales[i], scales[i] * scales[i]
-        for rows, cols in grid:
-            tile = two * prod[i, rows, cols] + (c1 * one) * low[i, rows, cols].astype(f32)
-            term[i, rows, cols] = plus_diag(tile, rows, cols, c0).astype(bf16)
+        near, far = c1 * scales[i], scales[i] * scales[i]
+
+        def third(tile, rows, cols):
+            tile = far * tile + near * low[i, rows, cols].astype(f32)
+            inner[i, rows, cols] = plus_diag(tile, rows, cols, c0).astype(bf16)
+
+        product(square[i], outer[i], third)
 
 
 def precondition_kernel(
     live_ref, arrived_a, arrived_b, left_stats, right_stats, left_roots, right_roots, _, out,
-    done_ref, stats, roots, results, wide, prod, raws, low, square, term, in_sems, out_sems,
+    done_ref, halves, stats, roots, results, grams, raws, applied, low, square, inner, outer, in_sems, out_sems,
 ):
     side = stats.shape[-1]
     entries = side * side
@@ -212,15 +229,19 @@
         fetch[name] = pltpu.make_async_copy(source, target, in_sems.at[len(fetch)])
         fetch[name].start()
 
+    get("a0", arrived_a.at[:, 0], halves.at[0])
     for slot in range(1, MOST):
+        get("a%d" % slot, arrived_a.at[:, slot], halves.at[slot])
         get("r%d" % slot, right_roots.at[0, 0, slot], roots.at[2 * slot - 1])
+    for slot in range(1, MOST):
         get("l%d" % slot, left_roots.at[0, 0, slot], roots.at[2 * slot - 2])
     get("left", left_stats.at[0, 0, 0], stats.at[0])
     get("right", right_stats.at[0, 0, 0], stats.at[1])
 
     def block_of(slot):
-        halves = [half[:, slot].reshape(side, side // 2) for half in (arrived_a, arrived_b)]
-        return jnp.concatenate(halves, axis=1)
+        fetch["a%d" % slot].wait()
+        front, back = halves[slot], arrived_b[:, slot]
+        return jnp.concatenate([half.reshape(side, side // 2) for half in (front, back)], axis=1)
 
     def give(slot, low=0, high=arrived_a.shape[0], part=0):
         slabs = pl.ds(low, high - low)
@@ -235,44 +256,56 @@
     def power(tile_of):
         return total([jnp.square(tile_of(rows, cols)) for rows, cols in grid]) * (1.0 / entries)
 
-    def graft(slot, block, raw, parts=1):
-        grad_power = power(lambda rows, cols: block[rows, cols].astype(f32))
-        scale = jnp.sqrt(grad_power) / jnp.sqrt(power(lambda rows, cols: raw[rows, cols]) + GRAFT_EPS)
+    def graft(slot, out_power, parts=1):
+        grad_power = power(lambda rows, cols: blocks[slot][rows, cols].astype(f32))
+        scale = jnp.sqrt(grad_power) / jnp.sqrt(out_power + GRAFT_EPS)
         share = results.shape[1] // parts
         for part in range(parts):
             for rows, cols in grid:
                 if rows.start // 16 // share == part:
-                    put(slot, rows, cols, (raw[rows, cols] * scale).astype(bf16))
+                    put(slot, rows, cols, (raws[slot, rows, cols] * scale).astype(bf16))
             give(slot, part * share, (part + 1) * share, MOST * (part > 0) + max(part - 1, 0))
 
-    block = block_of(0)
-    others = [block_of(slot) for slot in range(1, MOST)]
-    wide[0] = mul(block, block, ((1,), (1,)))
-    wide[1] = mul(block, block, ((0,), (0,)))
-    for i in range(MOST - 1):
-        fetch["r%d" % (i + 1)].wait()
-        raws[i] = mul(others[i], roots[2 * i + 1])
-    for i in range(MOST - 1):
-        for rows, cols in grid:
-            square[i, rows, cols] = raws[i, rows, cols].astype(bf16)
-        fetch["l%d" % (i + 1)].wait()
-        raws[i] = mul(roots[2 * i], square[i])
+    def apply_right(slot, root):
+        def use(tile, rows, cols):
+            applied[slot, rows, cols] = tile.astype(bf16)
+
+        product(blocks[slot], root, use)
+
+    def apply_left(slot, root):
+        squares = []
+
+        def use(tile, rows, cols):
+            raws[slot, rows, cols] = tile
+            squares.append(tile * tile)
+
+        product(root, applied[slot], use)
+        return total(squares) * (1.0 / entries)
+
+    blocks = [block_of(0)]
+    grams[0] = mul(blocks[0], blocks[0], ((1,), (1,)))
+    grams[1] = mul(blocks[0], blocks[0], ((0,), (0,)))
+    for slot in range(1, MOST):
+        blocks.append(block_of(slot))
+        fetch["r%d" % slot].wait()
+    for slot in range(1, MOST):
+        apply_right(slot, roots[2 * slot - 1])
+    for slot in range(1, MOST):
+        fetch["l%d" % slot].wait()
+    powers = [apply_left(slot, roots[2 * slot - 2]) for slot in range(1, MOST)]
     sent = []
-    for i, name in enumerate(("left", "right")):
-        fetch[name].wait()
-    fill = iter(range(MOST - 1))
+    fetch["left"].wait()
+    fetch["right"].wait()
+    fill = iter(range(1, MOST))
 
     def between():
-        for i in fill:
-            graft(i + 1, others[i], raws.at[i])
+        for slot in fill:
+            graft(slot, powers[slot - 1])
             break
 
-    new_roots(live_ref[0] > 0, stats, wide, low, square, term, prod, between)
-    prod[0] = mul(block, term[1])
-    for rows, cols in grid:
-        low[0, rows, cols] = prod[0, rows, cols].astype(bf16)
-    prod[1] = mul(term[0], low[0])
-    graft(0, block, prod.at[1], PARTS)
+    new_roots(live_ref[0] > 0, stats, grams, low, square, inner, outer, between)
+    apply_right(0, inner[1])
+    graft(0, apply_left(0, inner[0]), PARTS)
     for copy in sent:
         copy.wait()
     done_ref[0] = 0
@@ -285,19 +318,21 @@
     return pl.pallas_call(
         precondition_kernel,
         out_shape=[jax.ShapeDtypeStruct((owners, MOST, rows, side), jnp.bfloat16), token_shape()],
-        in_specs=[pl.BlockSpec(memory_space=SMEM)] + [pl.BlockSpec(memory_space=VMEM)] * 2 + [far] * 5,
+        in_specs=[pl.BlockSpec(memory_space=SMEM), far, pl.BlockSpec(memory_space=VMEM)] + [far] * 5,
         out_specs=[far, pl.BlockSpec(memory_space=SMEM)],
         scratch_shapes=[
+            VMEM((MOST, owners, rows, width), jnp.bfloat16),
             VMEM((2, side, side), jnp.float32),
             VMEM((2 * MOST - 2, side, side), jnp.bfloat16),
             VMEM((MOST, owners, rows, side), jnp.bfloat16),
             VMEM((2, side, side), jnp.float32),
-            VMEM((2, side, side), jnp.float32),
-            VMEM((2, side, side), jnp.float32),
-            VMEM((2, side, side), jnp.bfloat16),
-            VMEM((2, side, side), jnp.bfloat16),
-            VMEM((2, side, side), jnp.bfloat16),
-            pltpu.SemaphoreType.DMA((2 * MOST,)),
+            VMEM((MOST, side, side), jnp.float32),
+            VMEM((MOST, side, side), jnp.bfloat16),
+            VMEM((2, side, side), jnp.bfloat16),
+            VMEM((2, side, side), jnp.bfloat16),
+            VMEM((2, side, side), jnp.bfloat16),
+            VMEM((2, side, side), jnp.bfloat16),
+            pltpu.SemaphoreType.DMA((3 * MOST,)),
             pltpu.SemaphoreType.DMA((MOST + PARTS - 1,)),
         ],
         compiler_params=pltpu.CompilerParams(vmem_limit_bytes=VMEM_MOST),
@@ -309,7 +344,7 @@
 
 def stats_kernel(
     live_ref, front_ref, back_ref, lprev_ref, rprev_ref, _, left_ref, right_ref, lroot_ref, rroot_ref,
-    stats, grams, low, square, term, prod,
+    stats, grams, low, square, inner, outer,
 ):
     side = lprev_ref.shape[-1]
     block = jnp.concatenate([front_ref[:, 0], back_ref[:, 0]], axis=-1).reshape(side, side)
@@ -324,9 +359,9 @@
     def _():
         stats[0] = lprev_ref[0, 0, 0]
         stats[1] = rprev_ref[0, 0, 0]
-        new_roots(live, stats, grams, low, square, term, prod, lambda: None)
-        lroot_ref[0, 0] = term[0]
-        rroot_ref[0, 0] = term[1]
+        new_roots(live, stats, grams, low, square, inner, outer, lambda: None)
+        lroot_ref[0, 0] = inner[0]
+        rroot_ref[0, 0] = inner[1]
 
 
 def update_stats(live, arrived, left_stats, right_stats, tied):
@@ -350,7 +385,7 @@
             VMEM((2, side, side), jnp.bfloat16),
             VMEM((2, side, side), jnp.bfloat16),
             VMEM((2, side, side), jnp.bfloat16),
-            VMEM((2, side, side), jnp.float32),
+            VMEM((2, side, side), jnp.bfloat16),
         ],
         compiler_params=pltpu.CompilerParams(vmem_limit_bytes=VMEM_MOST),
         cost_estimate=cost(2 * MOST + 6, side, 13 * side * side * 4),
@@ -409,11 +444,6 @@
     up = [(i, (i + 1) % groups) for i in range(groups)]
     down = [(i, (i - 1) % groups) for i in range(groups)]
 
-    owner = lax.dynamic_slice(owner_table[:, 0], (group_id * share,), (share,), allow_negative_indices=False)
-    slot, place, empty = routing(owner, owners)
-    own_count = jnp.sum((owner == owner_id).astype(jnp.int32))
-    live = (jnp.arange(MOST, dtype=jnp.int32) < own_count).astype(jnp.int32)
-
     width = side // 2
 
     def part(source, ahead, low, column):
@@ -447,19 +477,23 @@
     mid = mids(later, 0)
     third = mid[0] + up1, mid[1] + down1
     up3, down3 = send(third)
-    later, _ = lax.optimization_barrier((later, third))
+    later, table, _ = lax.optimization_barrier((later, owner_table, third))
+    owner = lax.dynamic_slice(table[:, 0], (group_id * share,), (share,), allow_negative_indices=False)
+    slot, place, empty = routing(owner, owners)
+    own_count = jnp.sum((owner == owner_id).astype(jnp.int32))
+    live = (jnp.arange(MOST, dtype=jnp.int32) < own_count).astype(jnp.int32)
     firsts_b, seconds_b = firsts(later, width), seconds(later, width)
     sums = own_sums(local, 0, up2, down2)
     up1, down1 = send(firsts_b)
     up2, down2 = send(seconds_b)
+    outgoing_a = place_blocks(place, empty, sums[0], up3, sums[1], down3)
     spare, made = spare_room(empty, (owners, MOST, slab_rows, side))
-    outgoing_a = place_blocks(place, empty, sums[0], up3, sums[1], down3, *firsts_b, *seconds_b, made)
     mid = mids(later, width)
     third = add_pairs(mid[0], up1, mid[1], down1, outgoing_a)
     up3, down3 = send(third)
     later, _ = lax.optimization_barrier((later, third))
     sums = own_sums(later, width, up2, down2)
-    outgoing_b = place_blocks(place, empty, sums[0], up3, sums[1], down3)
+    outgoing_b = place_blocks(place, empty, sums[0], up3, sums[1], down3, made)
     arrived = [
         lax.all_to_all(
             outgoing.reshape(owners, MOST, slab_rows, width), "fsdp", split_axis=0, concat_axis=0, tiled=True

time: 110 us -> 116 us (1.055)
  waiting for transfers between devices: 36.2 us -> 39.5 us
  starting transfers between devices: 32.6 us -> 35.7 us
    ppermute x6, starting transfers between devices: 10.5 us -> 16.1 us  [send(): lax.ppermute(pair[1], 'rep', down)]
    ppermute x6, starting transfers between devices: 5.29 us -> 2.17 us  [send(): lax.ppermute(pair[0], 'rep', up)]
    ppermute x6, waiting for transfers between devices: 0.03 us -> 2.35 us  [send(): lax.ppermute(pair[1], 'rep', down)]
    ppermute x6, waiting for transfers between devices: 6.81 us -> 8.78 us  [send(): lax.ppermute(pair[0], 'rep', up)]
  transfers between devices with their start and end apart: 15 -> 15, of which waited for: 5 -> 6; matrix products, arithmetic and copies ran while one was open for 9% -> 8% of each run, Pallas kernels for 15% -> 15%
where the time goes in v4:
time: 116 us; the launch traced here: 115 us
  waiting for transfers between devices  39.5 us (34%)
  starting transfers between devices  35.7 us (31%)
  Pallas kernels  27.5 us (24%)
  local copies, waits for them, and re-layouts  5.96 us (5%)
  other arithmetic  5.73 us (5%)
    all_to_all x2, waiting for transfers between devices, on_device(): lax.all_to_all(outgoing.reshape(owners, MOST, slab_rows, width), 'fsdp',...  16.3 us
    ppermute x6, starting transfers between devices, send(): lax.ppermute(pair[1], 'rep', down)  16.1 us
    all_to_all x2, starting transfers between devices, on_device(): lax.all_to_all(outgoing.reshape(owners, MOST, slab_rows, width), 'fsdp',...  13.3 us
    all_to_all x1, waiting for transfers between devices, on_device(): lax.all_to_all(results, 'fsdp', split_axis=0, concat_axis=0, tiled=True)  12.1 us
    pallas_call x1, Pallas kernels, update_stats(): pl.pallas_call(stats_kernel, grid=(MOST,), out_shape=[shape, shape, root,...  11.7 us
    pallas_call x1, Pallas kernels, precondition(): pl.pallas_call(precondition_kernel, out_shape=[jax.ShapeDtypeStruct((owne...  9.24 us
    ppermute x6, waiting for transfers between devices, send(): lax.ppermute(pair[0], 'rep', up)  8.78 us
    dynamic_slice x3, local copies, waits for them, and re-layouts, part(): lax.dynamic_slice(source, (start, 0, column), (half, slab_rows, width), a...  4.37 us
  transfers between devices with their start and end apart: 15, of which 6 were waited for; matrix products, arithmetic and copies ran while one was open for 8% of the time, Pallas kernels for 15%

profile of v4, /device:TPU:0, one launch (start us, length us, event | category | flops | bytes accessed | tf_op | source)
XLA Modules:
  0.0 115.4 jit_solution(3551745927327738983)
XLA Ops:
  0.6 1.1 dynamic-slice_bitcast_fusion
  1.7 2.9 %collective-permute-start.1 = (bf16[32,16,256]{2,1,0:T(8,128)(2,1)S(1)}, bf16[32,16,256]{2,1,0:T(8,128)(2,1)S(1)}, u32[]{:S(2)}, u32[]{:S(2)}) collective-permute-start(bf16[32,16,256]{2,1,0:T(8,128)(2,1)S(1)} %get-tuple-element.51), channel_id=1, source_target_pairs={{0,96},{32,0},{64,32},{96,64},{1,97},{33,1},{65,33},{97,65},{2,98}... | collective-permute-start | bytes 786440 | tf_op jit(solution)/shard_map/ppermute | solution.py:456
  4.6 1.1 constant_dynamic-slice_fusion.7
  5.7 3.3 %collective-permute-start.2 = (bf16[32,16,256]{2,1,0:T(8,128)(2,1)S(1)}, bf16[32,16,256]{2,1,0:T(8,128)(2,1)S(1)}, u32[]{:S(2)}, u32[]{:S(2)}) collective-permute-start(bf16[32,16,256]{2,1,0:T(8,128)(2,1)S(1)} %get-tuple-element.49), channel_id=1, source_target_pairs={{0,96},{32,0},{64,32},{96,64},{1,97},{33,1},{65,33},{97,65},{2,98}... | collective-permute-start | bytes 786440 | tf_op jit(solution)/shard_map/ppermute | solution.py:456
  9.0 2.3 %collective-permute-done.1 = bf16[32,16,256]{2,1,0:T(8,128)(2,1)S(1)} collective-permute-done((bf16[32,16,256]{2,1,0:T(8,128)(2,1)S(1)}, bf16[32,16,256]{2,1,0:T(8,128)(2,1)S(1)}, u32[]{:S(2)}, u32[]{:S(2)}) %collective-permute-start.1) | collective-permute-done | bytes 262176 | tf_op jit(solution)/shard_map/ppermute | solution.py:456
  11.3 3.7 %collective-permute-done = bf16[32,16,256]{2,1,0:T(8,128)(2,1)S(1)} collective-permute-done((bf16[32,16,256]{2,1,0:T(8,128)(2,1)S(1)}, bf16[32,16,256]{2,1,0:T(8,128)(2,1)S(1)}, u32[]{:S(2)}, u32[]{:S(2)}) %collective-permute-start) | collective-permute-done | bytes 262176 | tf_op jit(solution)/shard_map/ppermute | solution.py:456
  15.1 1.1 dynamic-slice_add_fusion
  16.2 2.0 %collective-permute-start.3 = (bf16[32,16,256]{2,1,0:T(8,128)(2,1)S(1)}, bf16[32,16,256]{2,1,0:T(8,128)(2,1)S(1)}, u32[]{:S(2)}, u32[]{:S(2)}) collective-permute-start(bf16[32,16,256]{2,1,0:T(8,128)(2,1)S(1)} %get-tuple-element.48), channel_id=1, source_target_pairs={{0,32},{32,64},{64,96},{96,0},{1,33},{33,65},{65,97},{97,1},{2,34}... | collective-permute-start | bytes 786440 | tf_op jit(solution)/shard_map/ppermute | solution.py:456
  18.3 0.7 fusion.1
  19.5 0.5 copy-done.6
  20.1 2.2 %constant_dynamic-slice_fusion = (bf16[32,16,256]{2,1,0:T(8,128)(2,1)}, bf16[32,16,256]{2,1,0:T(8,128)(2,1)}, bf16[32,16,256]{2,1,0:T(8,128)(2,1)S(1)}, bf16[32,...) fusion(bf16[256,16,512]{2,1,0:T(8,128)(2,1)} %bitcast.18, ...), kind=kLoop, calls=%fused_computation.13 | loop fusion | bytes 3145752 | tf_op jit(solution)/shard_map/dynamic_slice | solution.py:451
  22.5 0.5 broadcast_subtract_fusion.empty_ref._
  23.0 1.2 %spare_room.1 = (bf16[32,3,16,512]{3,2,1,0:T(8,128)(2,1)}, s32[1]{0:T(128)}) custom-call(s32[96]{0:T(128)} %broadcast_subtract_fusion.empty_ref._), custom_call_target="tpu_custom_call" | custom-call | tf_op jit(solution)/shard_map/spare_room/pallas_call | solution.py:90
  24.2 3.3 %collective-permute-start.7 = (bf16[32,16,256]{2,1,0:T(8,128)(2,1)S(1)}, bf16[32,16,256]{2,1,0:T(8,128)(2,1)S(1)}, u32[]{:S(2)}, u32[]{:S(2)}) collective-permute-start(bf16[32,16,256]{2,1,0:T(8,128)(2,1)S(1)} %get-tuple-element.41), channel_id=1, source_target_pairs={{0,96},{32,0},{64,32},{96,64},{1,97},{33,1},{65,33},{97,65},{2,98}... | collective-permute-start | bytes 786440 | tf_op jit(solution)/shard_map/ppermute | solution.py:456
  27.5 1.2 %convert_add_fusion = (f32[32,16,256]{2,1,0:T(8,128)S(1)}, f32[32,16,256]{2,1,0:T(8,128)S(1)}) fusion(bf16[32,16,256]{2,1,0:T(8,128)(2,1)S(1)} %collective-permute-done.4, bf16[1,256,16,512]{3,2,1,0:T(8,128)(2,1)} %param.6, s32[]{:T(128)S(6)} %add.65, bf16[32,16,256]{2,1,0:T(8,128)(2,1)S(1)} %collective-permute-done.2, s32[]{:T(128)S(6)} %mul.43), kind=kLoop, calls=%fused_computation | loop fusion | flops 786432 | bytes 2097160 | tf_op jit(solution)/shard_map/add | solution.py:469
  28.7 3.3 %collective-permute-start.8 = (bf16[32,16,256]{2,1,0:T(8,128)(2,1)}, bf16[32,16,256]{2,1,0:T(8,128)(2,1)}, u32[]{:S(2)}, u32[]{:S(2)}) collective-permute-start(bf16[32,16,256]{2,1,0:T(8,128)(2,1)} %get-tuple-element.40), channel_id=1, source_target_pairs={{0,96},{32,0},{64,32},{96,64},{1,97},{33,1},{65,33},{97,65},{2,98}... | collective-permute-start | bytes 786440 | tf_op jit(solution)/shard_map/ppermute | solution.py:456
  32.0 0.7 copy-done.4
  32.6 1.6 %place_blocks.2.rest_0_ = bf16[96,16,256]{2,1,0:T(8,128)(2,1)} custom-call(s32[64]{0:T(128)S(1)} %multiply_add_fusion.place_ref, s32[96]{0:T(128)S(1)} %copy-done.4, f32[32,16,256]{2,1,0:T(8,128)S(1)} %get-tuple-element.46.front_ref, bf16[32,16,256]{2,1,0:T(8,128)(2,1)S(1)} %collective-permute-done.3.up_ref, f32[32,16,256]{2,1,0:T(8,128)S(1)} %get-tuple-element.45.back_ref, ...), custom_call_target="tpu_custom_call" | custom-call | bytes 2097152 | tf_op jit(solution)/shard_map/place_blocks/pallas_call | solution.py:130
  34.2 8.5 %all-to-all-start = ((bf16[32,3,16,256]{3,2,1,0:T(8,128)(2,1)}), bf16[32,3,16,256]{3,2,1,0:T(8,128)(2,1)}, u32[]{:S(2)}, u32[]{:S(2)}) async-start(bf16[32,3,16,256]{3,2,1,0:T(8,128)(2,1)} %bitcast.6), calls=%async_computation | async-start | bytes 1572864 | tf_op jit(solution)/shard_map/all_to_all | solution.py:498
  42.9 3.2 %collective-permute-start.11 = (bf16[32,16,256]{2,1,0:T(8,128)(2,1)S(1)}, bf16[32,16,256]{2,1,0:T(8,128)(2,1)S(1)}, u32[]{:S(2)}, u32[]{:S(2)}) collective-permute-start(bf16[32,16,256]{2,1,0:T(8,128)(2,1)S(1)} %get-tuple-element.25), channel_id=1, source_target_pairs={{0,96},{32,0},{64,32},{96,64},{1,97},{33,1},{65,33},{97,65},{2,98}... | collective-permute-start | bytes 786440 | tf_op jit(solution)/shard_map/ppermute | solution.py:456
  46.1 1.3 %convert_add_fusion.2 = (f32[32,16,256]{2,1,0:T(8,128)S(1)}, f32[32,16,256]{2,1,0:T(8,128)S(1)}) fusion(bf16[32,16,256]{2,1,0:T(8,128)(2,1)} %collective-permute-done.10, bf16[256,16,512]{2,1,0:T(8,128)(2,1)} %bitcast.19, s32[]{:T(128)S(6)} %add.65, bf16[32,16,256]{2,1,0:T(8,128)(2,1)} %collective-permute-done.8, s32[]{:T(128)S(6)} %mul.43), kind=kLoop, calls=%fused_computation.2 | loop fusion | flops 786432 | bytes 2097160 | tf_op jit(solution)/shard_map/add | solution.py:469
  47.5 5.0 %collective-permute-done.9.up_ref = bf16[32,16,256]{2,1,0:T(8,128)(2,1)S(1)} collective-permute-done((bf16[32,16,256]{2,1,0:T(8,128)(2,1)S(1)}, bf16[32,16,256]{2,1,0:T(8,128)(2,1)S(1)}, u32[]{:S(2)}, u32[]{:S(2)}) %collective-permute-start.9) | collective-permute-done | bytes 262176 | tf_op jit(solution)/shard_map/ppermute | solution.py:456
  52.5 2.3 %place_blocks.3 = bf16[96,16,256]{2,1,0:T(8,128)(2,1)} custom-call(s32[64]{0:T(128)S(1)} %copy-done.3, s32[96]{0:T(128)S(1)} %copy-done.5, f32[32,16,256]{2,1,0:T(8,128)S(1)} %get-tuple-element.38.front_ref, bf16[32,16,256]{2,1,0:T(8,128)(2,1)S(1)} %collective-permute-done.9.up_ref, f32[32,16,256]{2,1,0:T(8,128)S(1)} %get-tuple-element.37.back_ref, ...), custom_call_target="tpu_custom_call" | custom-call | bytes 2097152 | tf_op jit(solution)/shard_map/place_blocks/pallas_call | solution.py:130
  54.8 2.4 %all-to-all-done.arrived_a.front_ref = bf16[32,3,16,256]{3,2,1,0:T(8,128)(2,1)} async-done(((bf16[32,3,16,256]{3,2,1,0:T(8,128)(2,1)}), bf16[32,3,16,256]{3,2,1,0:T(8,128)(2,1)}, u32[]{:S(2)}, u32[]{:S(2)}) %all-to-all-start) | async-done | bytes 786464 | tf_op jit(solution)/shard_map/all_to_all | solution.py:498
  57.2 4.8 %all-to-all-start.1 = ((bf16[32,3,16,256]{3,2,1,0:T(8,128)(2,1)}), bf16[32,3,16,256]{3,2,1,0:T(8,128)(2,1)S(1)}, u32[]{:S(2)}, u32[]{:S(2)}) async-start(bf16[32,3,16,256]{3,2,1,0:T(8,128)(2,1)} %bitcast.7), calls=%async_computation.1 | async-start | bytes 1572864 | tf_op jit(solution)/shard_map/all_to_all | solution.py:498
  62.1 0.7 compare_convert_fusion.live_ref
  62.7 13.9 %all-to-all-done.1.arrived_b.back_ref = bf16[32,3,16,256]{3,2,1,0:T(8,128)(2,1)S(1)} async-done(((bf16[32,3,16,256]{3,2,1,0:T(8,128)(2,1)}), bf16[32,3,16,256]{3,2,1,0:T(8,128)(2,1)S(1)}, u32[]{:S(2)}, u32[]{:S(2)}) %all-to-all-start.1) | async-done | bytes 786464 | tf_op jit(solution)/shard_map/all_to_all | solution.py:498
  76.6 9.2 %precondition.1 = (bf16[32,3,16,512]{3,2,1,0:T(8,128)(2,1)}, s32[1]{0:T(128)}) custom-call(s32[3]{0:T(128)S(1)} %compare_convert_fusion.live_ref, bf16[32,3,16,256]{3,2,1,0:T(8,128)(2,1)} %all-to-all-done.arrived_a.front_ref, bf16[32,3,16,256]{3,2,1,0:T(8,128)(2,1)S(1)} %all-to-all-done.1.arrived_b.back_ref, ...), custom_call_target="tpu_custom_call", output_to_operand_aliasing={{0}: (7, {})} | custom-call | flops 3758096384 | bytes 9437184 | tf_op jit(solution)/shard_map/precondition/pallas_call | solution.py:318
  85.9 4.2 %all-to-all-start.2 = ((bf16[32,3,16,512]{3,2,1,0:T(8,128)(2,1)}), bf16[32,3,16,512]{3,2,1,0:T(8,128)(2,1)S(1)}, u32[]{:S(2)}, u32[]{:S(2)}) async-start(bf16[32,3,16,512]{3,2,1,0:T(8,128)(2,1)} %get-tuple-element.29), calls=%async_computation.2 | async-start | bytes 3145728 | tf_op jit(solution)/shard_map/all_to_all | solution.py:506
  90.1 11.7 %update_stats.1 = (f32[1,1,3,512,512]{4,3,2,1,0:T(8,128)}, f32[1,1,3,512,512]{4,3,2,1,0:T(8,128)}, bf16[1,1,512,512]{3,2,1,0:T(8,128)(2,1)}, bf16[1,1,512,512]{3,2,1,0:T(8,128)(2,1)}) custom-call(s32[3]{0:T(128)S(1)} %compare_convert_fusion.live_ref, bf16[32,3,16,256]{3,2,1,0:T(8,128)(2,1)} %all-to-all-done.arrived_a.front_ref, ...), custom_call_target="tpu_custom_call" | custom-call | flops 3221225472 | bytes 13631488 | tf_op jit(solution)/shard_map/update_stats/pallas_call | solution.py:374
  101.7 12.1 %all-to-all-done.2.back_ref = bf16[32,3,16,512]{3,2,1,0:T(8,128)(2,1)S(1)} async-done(((bf16[32,3,16,512]{3,2,1,0:T(8,128)(2,1)}), bf16[32,3,16,512]{3,2,1,0:T(8,128)(2,1)S(1)}, u32[]{:S(2)}, u32[]{:S(2)}) %all-to-all-start.2) | async-done | bytes 1572896 | tf_op jit(solution)/shard_map/all_to_all | solution.py:506
  113.8 1.5 %assemble.1 = bf16[64,16,512]{2,1,0:T(8,128)(2,1)} custom-call(s32[64]{0:T(128)S(1)} %copy-done.7, s32[64]{0:T(128)S(1)} %copy-done.1, bf16[32,3,16,512]{3,2,1,0:T(8,128)(2,1)S(1)} %all-to-all-done.2.back_ref), custom_call_target="tpu_custom_call" | custom-call | bytes 2097152 | tf_op jit(solution)/shard_map/assemble/pallas_call | solution.py:410
  (35 shorter events, 1.0 us)
Async XLA Ops:
  0.6 17.6 %copy-start.8 = (s32[256,1]{0,1:T(1,128)S(1)}, s32[256,1]{0,1:T(1,128)}, u32[]{:S(2)}) copy-start(s32[256,1]{0,1:T(1,128)} %param.7) | copy-start | bytes 3076
  1.7 9.6 %collective-permute-start.1 = (bf16[32,16,256]{2,1,0:T(8,128)(2,1)S(1)}, bf16[32,16,256]{2,1,0:T(8,128)(2,1)S(1)}, u32[]{:S(2)}, u32[]{:S(2)}) collective-permute-start(bf16[32,16,256]{2,1,0:T(8,128)(2,1)S(1)} %get-tuple-element.51), channel_id=1, source_target_pairs={{0,96},{32,0},{64,32},{96,64},{1,97},{33,1},{65,33},{97,65},{2,98}... | collective-permute-start | bytes 786440 | tf_op jit(solution)/shard_map/ppermute | solution.py:456
  4.6 10.4 %collective-permute-start = (bf16[32,16,256]{2,1,0:T(8,128)(2,1)S(1)}, bf16[32,16,256]{2,1,0:T(8,128)(2,1)S(1)}, u32[]{:S(2)}, u32[]{:S(2)}) collective-permute-start(bf16[32,16,256]{2,1,0:T(8,128)(2,1)S(1)} %get-tuple-element.52), channel_id=1, source_target_pairs={{0,32},{32,64},{64,96},{96,0},{1,33},{33,65},{65,97},{97,1},{2,34}... | collective-permute-start | bytes 786440 | tf_op jit(solution)/shard_map/ppermute | solution.py:456
  5.7 18.5 %collective-permute-start.2 = (bf16[32,16,256]{2,1,0:T(8,128)(2,1)S(1)}, bf16[32,16,256]{2,1,0:T(8,128)(2,1)S(1)}, u32[]{:S(2)}, u32[]{:S(2)}) collective-permute-start(bf16[32,16,256]{2,1,0:T(8,128)(2,1)S(1)} %get-tuple-element.49), channel_id=1, source_target_pairs={{0,96},{32,0},{64,32},{96,64},{1,97},{33,1},{65,33},{97,65},{2,98}... | collective-permute-start | bytes 786440 | tf_op jit(solution)/shard_map/ppermute | solution.py:456
  9.0 18.5 %collective-permute-start.4 = (bf16[32,16,256]{2,1,0:T(8,128)(2,1)S(1)}, bf16[32,16,256]{2,1,0:T(8,128)(2,1)S(1)}, u32[]{:S(2)}, u32[]{:S(2)}) collective-permute-start(bf16[32,16,256]{2,1,0:T(8,128)(2,1)S(1)} %get-tuple-element.50), channel_id=1, source_target_pairs={{0,32},{32,64},{64,96},{96,0},{1,33},{33,65},{65,97},{97,1},{2,34}... | collective-permute-start | bytes 786440 | tf_op jit(solution)/shard_map/ppermute | solution.py:456
  16.2 12.5 %collective-permute-start.5 = (bf16[32,16,256]{2,1,0:T(8,128)(2,1)S(1)}, bf16[32,16,256]{2,1,0:T(8,128)(2,1)S(1)}, u32[]{:S(2)}, u32[]{:S(2)}) collective-permute-start(bf16[32,16,256]{2,1,0:T(8,128)(2,1)S(1)} %get-tuple-element.47), channel_id=1, source_target_pairs={{0,96},{32,0},{64,32},{96,64},{1,97},{33,1},{65,33},{97,65},{2,98}... | collective-permute-start | bytes 786440 | tf_op jit(solution)/shard_map/ppermute | solution.py:456
  16.2 15.7 %collective-permute-start.3 = (bf16[32,16,256]{2,1,0:T(8,128)(2,1)S(1)}, bf16[32,16,256]{2,1,0:T(8,128)(2,1)S(1)}, u32[]{:S(2)}, u32[]{:S(2)}) collective-permute-start(bf16[32,16,256]{2,1,0:T(8,128)(2,1)S(1)} %get-tuple-element.48), channel_id=1, source_target_pairs={{0,32},{32,64},{64,96},{96,0},{1,33},{33,65},{65,97},{97,1},{2,34}... | collective-permute-start | bytes 786440 | tf_op jit(solution)/shard_map/ppermute | solution.py:456
  19.0 0.6 copy-start
  19.5 0.5 copy-start.6
  20.1 14.1 %copy-start.2 = (s32[64]{0:T(128)}, s32[64]{0:T(128)S(1)}, u32[]{:S(2)}) copy-start(s32[64]{0:T(128)S(1)} %multiply_add_fusion.place_ref) | copy-start | bytes 772
  22.4 23.7 %collective-permute-start.10 = (bf16[32,16,256]{2,1,0:T(8,128)(2,1)}, bf16[32,16,256]{2,1,0:T(8,128)(2,1)}, u32[]{:S(2)}, u32[]{:S(2)}) collective-permute-start(bf16[32,16,256]{2,1,0:T(8,128)(2,1)} %get-tuple-element.39), channel_id=1, source_target_pairs={{0,32},{32,64},{64,96},{96,0},{1,33},{33,65},{65,97},{97,1},{2,34}... | collective-permute-start | bytes 786440 | tf_op jit(solution)/shard_map/ppermute | solution.py:456
  24.2 18.5 %collective-permute-start.7 = (bf16[32,16,256]{2,1,0:T(8,128)(2,1)S(1)}, bf16[32,16,256]{2,1,0:T(8,128)(2,1)S(1)}, u32[]{:S(2)}, u32[]{:S(2)}) collective-permute-start(bf16[32,16,256]{2,1,0:T(8,128)(2,1)S(1)} %get-tuple-element.41), channel_id=1, source_target_pairs={{0,96},{32,0},{64,32},{96,64},{1,97},{33,1},{65,33},{97,65},{2,98}... | collective-permute-start | bytes 786440 | tf_op jit(solution)/shard_map/ppermute | solution.py:456
  27.5 15.2 %collective-permute-start.6 = (bf16[32,16,256]{2,1,0:T(8,128)(2,1)S(1)}, bf16[32,16,256]{2,1,0:T(8,128)(2,1)S(1)}, u32[]{:S(2)}, u32[]{:S(2)}) collective-permute-start(bf16[32,16,256]{2,1,0:T(8,128)(2,1)S(1)} %get-tuple-element.43), channel_id=1, source_target_pairs={{0,32},{32,64},{64,96},{96,0},{1,33},{33,65},{65,97},{97,1},{2,34}... | collective-permute-start | bytes 786440 | tf_op jit(solution)/shard_map/ppermute | solution.py:456
  28.7 17.4 %collective-permute-start.8 = (bf16[32,16,256]{2,1,0:T(8,128)(2,1)}, bf16[32,16,256]{2,1,0:T(8,128)(2,1)}, u32[]{:S(2)}, u32[]{:S(2)}) collective-permute-start(bf16[32,16,256]{2,1,0:T(8,128)(2,1)} %get-tuple-element.40), channel_id=1, source_target_pairs={{0,96},{32,0},{64,32},{96,64},{1,97},{33,1},{65,33},{97,65},{2,98}... | collective-permute-start | bytes 786440 | tf_op jit(solution)/shard_map/ppermute | solution.py:456
  32.0 0.7 copy-start.4
  34.2 23.0 %all-to-all-start = ((bf16[32,3,16,256]{3,2,1,0:T(8,128)(2,1)}), bf16[32,3,16,256]{3,2,1,0:T(8,128)(2,1)}, u32[]{:S(2)}, u32[]{:S(2)}) async-start(bf16[32,3,16,256]{3,2,1,0:T(8,128)(2,1)} %bitcast.6), calls=%async_computation | async-start | bytes 1572864 | tf_op jit(solution)/shard_map/all_to_all | solution.py:498
  42.7 9.8 %copy-start.3 = (s32[64]{0:T(128)S(1)}, s32[64]{0:T(128)}, u32[]{:S(2)}) copy-start(s32[64]{0:T(128)} %copy-done.2) | copy-start | bytes 772
  42.7 9.8 %copy-start.5 = (s32[96]{0:T(128)S(1)}, s32[96]{0:T(128)}, u32[]{:S(2)}) copy-start(s32[96]{0:T(128)} %broadcast_subtract_fusion.empty_ref._) | copy-start | bytes 1156
  42.8 9.7 %collective-permute-start.9 = (bf16[32,16,256]{2,1,0:T(8,128)(2,1)S(1)}, bf16[32,16,256]{2,1,0:T(8,128)(2,1)S(1)}, u32[]{:S(2)}, u32[]{:S(2)}) collective-permute-start(bf16[32,16,256]{2,1,0:T(8,128)(2,1)S(1)} %get-tuple-element.24), channel_id=1, source_target_pairs={{0,32},{32,64},{64,96},{96,0},{1,33},{33,65},{65,97},{97,1},{2,34}... | collective-permute-start | bytes 786440 | tf_op jit(solution)/shard_map/ppermute | solution.py:456
  42.9 9.6 %collective-permute-start.11 = (bf16[32,16,256]{2,1,0:T(8,128)(2,1)S(1)}, bf16[32,16,256]{2,1,0:T(8,128)(2,1)S(1)}, u32[]{:S(2)}, u32[]{:S(2)}) collective-permute-start(bf16[32,16,256]{2,1,0:T(8,128)(2,1)S(1)} %get-tuple-element.25), channel_id=1, source_target_pairs={{0,96},{32,0},{64,32},{96,64},{1,97},{33,1},{65,33},{97,65},{2,98}... | collective-permute-start | bytes 786440 | tf_op jit(solution)/shard_map/ppermute | solution.py:456
  57.2 19.4 %all-to-all-start.1 = ((bf16[32,3,16,256]{3,2,1,0:T(8,128)(2,1)}), bf16[32,3,16,256]{3,2,1,0:T(8,128)(2,1)S(1)}, u32[]{:S(2)}, u32[]{:S(2)}) async-start(bf16[32,3,16,256]{3,2,1,0:T(8,128)(2,1)} %bitcast.7), calls=%async_computation.1 | async-start | bytes 1572864 | tf_op jit(solution)/shard_map/all_to_all | solution.py:498
  85.9 27.9 %all-to-all-start.2 = ((bf16[32,3,16,512]{3,2,1,0:T(8,128)(2,1)}), bf16[32,3,16,512]{3,2,1,0:T(8,128)(2,1)S(1)}, u32[]{:S(2)}, u32[]{:S(2)}) async-start(bf16[32,3,16,512]{3,2,1,0:T(8,128)(2,1)} %get-tuple-element.29), calls=%async_computation.2 | async-start | bytes 3145728 | tf_op jit(solution)/shard_map/all_to_all | solution.py:506
  90.0 23.8 %copy-start.1 = (s32[64]{0:T(128)S(1)}, s32[64]{0:T(128)}, u32[]{:S(2)}) copy-start(s32[64]{0:T(128)} %copy-done) | copy-start | bytes 772
  90.0 23.7 %copy-start.7 = (s32[64]{0:T(128)S(1)}, s32[64]{0:T(128)}, u32[]{:S(2)}) copy-start(s32[64]{0:T(128)} %copy-done.6) | copy-start | bytes 772

commit v5 on v4

--- a/solution.py
+++ b/solution.py
@@ -12,6 +12,7 @@
 GRAFT_EPS = 1e-12
 NORM_EPS = 1e-12
 MOST = 3
+SPLIT = 2
 
 ROOT_POLY = (
     25.0 / 16.0,
@@ -81,25 +82,20 @@
     return pl.CostEstimate(flops=matmuls * 2 * side**3, bytes_accessed=nbytes, transcendentals=0)
 
 
-def spare_kernel(_, room_ref, done_ref):
-    done_ref[0] = 0
-
-
-def spare_room(after, shape):
-    scalars = pl.BlockSpec(memory_space=SMEM)
+def spare_room(shape):
     return pl.pallas_call(
-        spare_kernel,
-        out_shape=[jax.ShapeDtypeStruct(shape, jnp.bfloat16), token_shape()],
-        in_specs=[scalars],
-        out_specs=[pl.BlockSpec(memory_space=pl.ANY), scalars],
+        lambda room: None,
+        out_shape=jax.ShapeDtypeStruct(shape, jnp.bfloat16),
+        out_specs=pl.BlockSpec(memory_space=pl.ANY),
         compiler_params=pltpu.CompilerParams(vmem_limit_bytes=VMEM_ALL),
         name="spare_room",
-    )(after)
-
-
-def place_kernel(after, place_ref, empty_ref, front_ref, up_ref, back_ref, down_ref, *rest):
-    out_ref, sums, zeros, sem = rest[after], *rest[-3:]
-    half = front_ref.shape[0]
+    )()
+
+
+def place_kernel(place_ref, empty_ref, *rest):
+    (own_front, straight_front, last_front, own_back, straight_back, last_back), rest = rest[:6], rest[6:]
+    out_ref, sums, zeros, sem = rest
+    half = own_front.shape[0]
     zeros[...] = jnp.zeros_like(zeros)
 
     def blank(place, carry):
@@ -109,14 +105,14 @@
 
         return carry
 
-    def put(block):
-        pltpu.make_async_copy(sums.at[block], out_ref.at[place_ref[block]], sem).start()
-
     def add(j, carry):
-        sums[j] = (front_ref[j] + up_ref[j].astype(jnp.float32)).astype(jnp.bfloat16)
-        put(j)
-        sums[half + j] = (back_ref[j] + down_ref[j].astype(jnp.float32)).astype(jnp.bfloat16)
-        put(half + j)
+        for block, own, straight, last in (
+            (j, own_front, straight_front, last_front),
+            (half + j, own_back, straight_back, last_back),
+        ):
+            three = own[j], straight[straight.shape[0] - half + j], last[j]
+            sums[block] = sum(term.astype(jnp.float32) for term in three).astype(jnp.bfloat16)
+            pltpu.make_async_copy(sums.at[block], out_ref.at[place_ref[block]], sem).start()
         return carry
 
     lax.fori_loop(0, half, add, 0, unroll=4)
@@ -124,15 +120,13 @@
     pltpu.make_async_copy(out_ref, out_ref, sem).wait()
 
 
-def place_blocks(place, empty, front, up, back, down, *after):
-    half, rows, cols = front.shape
+def place_blocks(place, empty, front, back, weight=0):
+    half, rows, cols = front[0].shape
     scalars = pl.BlockSpec(memory_space=SMEM)
     return pl.pallas_call(
-        functools.partial(place_kernel, len(after)),
+        place_kernel,
         out_shape=jax.ShapeDtypeStruct((empty.shape[0], rows, cols), jnp.bfloat16),
-        in_specs=[scalars] * 2
-        + [pl.BlockSpec(memory_space=VMEM)] * 4
-        + [pl.BlockSpec(memory_space=pl.ANY)] * len(after),
+        in_specs=[scalars] * 2 + [pl.BlockSpec(memory_space=VMEM)] * 6,
         out_specs=pl.BlockSpec(memory_space=HBM),
         scratch_shapes=[
             VMEM((2 * half, rows, cols), jnp.bfloat16),
@@ -140,9 +134,9 @@
             pltpu.SemaphoreType.DMA(()),
         ],
         compiler_params=pltpu.CompilerParams(vmem_limit_bytes=VMEM_LIMIT),
-        cost_estimate=cost(0, 0, 8 * half * rows * cols * 2),
+        cost_estimate=cost(weight, 512, 8 * half * rows * cols * 2),
         name="place_blocks",
-    )(place, empty, front, up, back, down, *after)
+    )(place, empty, *front, *back)
 
 
 def add_kernel(one_ref, two_ref, three_ref, four_ref, *rest):
@@ -217,7 +211,7 @@
 
 def precondition_kernel(
     live_ref, arrived_a, arrived_b, left_stats, right_stats, left_roots, right_roots, _, out,
-    done_ref, halves, stats, roots, results, grams, raws, applied, low, square, inner, outer, in_sems, out_sems,
+    halves, stats, roots, results, grams, raws, applied, low, square, inner, outer, in_sems, out_sems,
 ):
     side = stats.shape[-1]
     entries = side * side
@@ -241,7 +235,7 @@
     def block_of(slot):
         fetch["a%d" % slot].wait()
         front, back = halves[slot], arrived_b[:, slot]
-        return jnp.concatenate([half.reshape(side, side // 2) for half in (front, back)], axis=1)
+        return jnp.concatenate([half.reshape(side, -1) for half in (front, back)], axis=1)
 
     def give(slot, low=0, high=arrived_a.shape[0], part=0):
         slabs = pl.ds(low, high - low)
@@ -308,7 +302,6 @@
     graft(0, apply_left(0, inner[0]), PARTS)
     for copy in sent:
         copy.wait()
-    done_ref[0] = 0
 
 
 def precondition(live, arrived, left_stats, right_stats, left_roots, right_roots, spare):
@@ -317,9 +310,9 @@
     far = pl.BlockSpec(memory_space=HBM)
     return pl.pallas_call(
         precondition_kernel,
-        out_shape=[jax.ShapeDtypeStruct((owners, MOST, rows, side), jnp.bfloat16), token_shape()],
+        out_shape=jax.ShapeDtypeStruct((owners, MOST, rows, side), jnp.bfloat16),
         in_specs=[pl.BlockSpec(memory_space=SMEM), far, pl.BlockSpec(memory_space=VMEM)] + [far] * 5,
-        out_specs=[far, pl.BlockSpec(memory_space=SMEM)],
+        out_specs=far,
         scratch_shapes=[
             VMEM((MOST, owners, rows, width), jnp.bfloat16),
             VMEM((2, side, side), jnp.float32),
@@ -343,7 +336,7 @@
 
 
 def stats_kernel(
-    live_ref, front_ref, back_ref, lprev_ref, rprev_ref, _, left_ref, right_ref, lroot_ref, rroot_ref,
+    live_ref, front_ref, back_ref, lprev_ref, rprev_ref, left_ref, right_ref, lroot_ref, rroot_ref,
     stats, grams, low, square, inner, outer,
 ):
     side = lprev_ref.shape[-1]
@@ -364,8 +357,8 @@
         rroot_ref[0, 0] = inner[1]
 
 
-def update_stats(live, arrived, left_stats, right_stats, tied):
-    owners, _, rows, width = arrived[0].shape
+def update_stats(live, arrived, left_stats, right_stats):
+    owners, _, rows, _ = arrived[0].shape
     side = left_stats.shape[-1]
     at_slot = pl.BlockSpec((1, 1, 1, side, side), lambda s: (0, 0, s, 0, 0))
     of_first = pl.BlockSpec((1, 1, side, side), lambda s: (0, 0, 0, 0))
@@ -376,8 +369,8 @@
         grid=(MOST,),
         out_shape=[shape, shape, root, root],
         in_specs=[pl.BlockSpec(memory_space=SMEM)]
-        + [pl.BlockSpec((owners, 1, rows, width), lambda s: (0, s, 0, 0))] * 2
-        + [at_slot, at_slot, pl.BlockSpec(memory_space=SMEM)],
+        + [pl.BlockSpec((owners, 1, rows, half.shape[3]), lambda s: (0, s, 0, 0)) for half in arrived]
+        + [at_slot, at_slot],
         out_specs=[at_slot, at_slot, of_first, of_first],
         scratch_shapes=[
             VMEM((2, side, side), jnp.float32),
@@ -390,37 +383,33 @@
         compiler_params=pltpu.CompilerParams(vmem_limit_bytes=VMEM_MOST),
         cost_estimate=cost(2 * MOST + 6, side, 13 * side * side * 4),
         name="update_stats",
-    )(live, *arrived, left_stats, right_stats, tied)
-
-
-def assemble_kernel(slot_ref, owner_ref, back_ref, out_ref, sem):
+    )(live, *arrived, left_stats, right_stats)
+
+
+def assemble_kernel(place_ref, back_ref, out_ref, sem):
     count = out_ref.shape[0]
 
     def start(b, carry):
-        pltpu.make_async_copy(back_ref.at[owner_ref[b], slot_ref[b]], out_ref.at[b], sem).start()
+        pltpu.make_async_copy(back_ref.at[place_ref[b]], out_ref.at[b], sem).start()
         return carry
 
     lax.fori_loop(0, count, start, 0, unroll=8)
     pltpu.make_async_copy(out_ref, out_ref, sem).wait()
 
 
-def assemble(slot_of, owner_of, back):
-    count = slot_of.shape[0]
-    rows, cols = back.shape[2:]
+def assemble(place, back):
+    count = place.shape[0]
+    rows, cols = back.shape[1:]
     return pl.pallas_call(
         assemble_kernel,
         out_shape=jax.ShapeDtypeStruct((count, rows, cols), jnp.bfloat16),
-        in_specs=[pl.BlockSpec(memory_space=SMEM)] * 2 + [pl.BlockSpec(memory_space=pl.ANY)],
+        in_specs=[pl.BlockSpec(memory_space=SMEM), pl.BlockSpec(memory_space=pl.ANY)],
         out_specs=pl.BlockSpec(memory_space=HBM),
         scratch_shapes=[pltpu.SemaphoreType.DMA(())],
         compiler_params=pltpu.CompilerParams(vmem_limit_bytes=VMEM_LIMIT),
         cost_estimate=cost(0, 0, 2 * count * rows * cols * 2),
         name="assemble",
-    )(slot_of, owner_of, back)
-
-
-def token_shape():
-    return jax.ShapeDtypeStruct((1,), jnp.int32)
+    )(place, back)
 
 
 def routing(owner, owners):
@@ -429,7 +418,7 @@
     slot = jnp.sum((same & (ids[None, :] < ids[:, None])).astype(jnp.int32), axis=1)
     place = owner * MOST + slot
     taken = place[None, :] == jnp.arange(owners * MOST, dtype=jnp.int32)[:, None]
-    return slot, place, 1 - jnp.sum(taken.astype(jnp.int32), axis=1)
+    return place, 1 - jnp.sum(taken.astype(jnp.int32), axis=1)
 
 
 def on_device(grads, owner_table, left_stats, right_stats, left_roots, right_roots):
@@ -444,68 +433,65 @@
     up = [(i, (i + 1) % groups) for i in range(groups)]
     down = [(i, (i - 1) % groups) for i in range(groups)]
 
-    width = side // 2
-
-    def part(source, ahead, low, column):
+    owner = lax.dynamic_slice(owner_table[:, 0], (group_id * share,), (share,), allow_negative_indices=False)
+    place, empty = routing(owner, owners)
+    own_count = jnp.sum((owner == owner_id).astype(jnp.int32))
+    live = (jnp.arange(MOST, dtype=jnp.int32) < own_count).astype(jnp.int32)
+    cut = side // SPLIT
+    parts = ((0, cut), (cut, side - cut))
+
+    def part(source, ahead, low, columns):
         start = ((group_id + ahead) & (groups - 1)) * share + low
         return lax.dynamic_slice(
-            source, (start, 0, column), (half, slab_rows, width), allow_negative_indices=False
+            source, (start, 0, columns[0]), (half, slab_rows, columns[1]), allow_negative_indices=False
         )
 
     def send(pair):
         return lax.ppermute(pair[0], "rep", up), lax.ppermute(pair[1], "rep", down)
 
-    def firsts(source, column):
-        return part(source, 2, 0, column), part(source, 2, half, column)
-
-    def seconds(source, column):
-        return part(source, 1, half, column), part(source, 3, 0, column)
-
-    def mids(source, column):
-        return part(source, 1, 0, column), part(source, 3, half, column)
-
-    def own_sums(source, column, up2, down2):
-        front = part(source, 0, 0, column).astype(jnp.float32) + down2.astype(jnp.float32)
-        return front, part(source, 0, half, column).astype(jnp.float32) + up2.astype(jnp.float32)
-
-    first = firsts(local, 0)
+    def firsts(source, columns):
+        return part(source, 2, 0, columns), part(source, 2, half, columns)
+
+    def seconds(source, columns):
+        return part(source, 1, half, columns), part(source, 3, 0, columns)
+
+    def mids(source, columns):
+        return part(source, 1, 0, columns), part(source, 3, half, columns)
+
+    def owns(source, columns):
+        return part(source, 0, 0, columns), part(source, 0, half, columns)
+
+    first = firsts(local, parts[0])
     up1, down1 = send(first)
     later, _ = lax.optimization_barrier((local, first))
-    second = seconds(later, 0)
+    second = seconds(later, parts[0])
     up2, down2 = send(second)
     later, _ = lax.optimization_barrier((later, second))
-    mid = mids(later, 0)
+    own, mid = owns(later, parts[0]), mids(later, parts[0])
     third = mid[0] + up1, mid[1] + down1
     up3, down3 = send(third)
-    later, table, _ = lax.optimization_barrier((later, owner_table, third))
-    owner = lax.dynamic_slice(table[:, 0], (group_id * share,), (share,), allow_negative_indices=False)
-    slot, place, empty = routing(owner, owners)
-    own_count = jnp.sum((owner == owner_id).astype(jnp.int32))
-    live = (jnp.arange(MOST, dtype=jnp.int32) < own_count).astype(jnp.int32)
-    firsts_b, seconds_b = firsts(later, width), seconds(later, width)
-    sums = own_sums(local, 0, up2, down2)
-    up1, down1 = send(firsts_b)
-    up2, down2 = send(seconds_b)
-    outgoing_a = place_blocks(place, empty, sums[0], up3, sums[1], down3)
-    spare, made = spare_room(empty, (owners, MOST, slab_rows, side))
-    mid = mids(later, width)
-    third = add_pairs(mid[0], up1, mid[1], down1, outgoing_a)
+    later, _ = lax.optimization_barrier((later, third))
+    pairs = zip(firsts(later, parts[1]), seconds(later, parts[1]))
+    both = tuple(jnp.concatenate(pair) for pair in pairs)
+    up12, down12 = send(both)
+    outgoing_a = place_blocks(place, empty, (own[0], down2, up3), (own[1], up2, down3), 30)
+    own, mid = owns(later, parts[1]), mids(later, parts[1])
+    third = add_pairs(mid[0], up12, mid[1], down12, outgoing_a)
     up3, down3 = send(third)
-    later, _ = lax.optimization_barrier((later, third))
-    sums = own_sums(later, width, up2, down2)
-    outgoing_b = place_blocks(place, empty, sums[0], up3, sums[1], down3, made)
+    outgoing_b = place_blocks(place, empty, (own[0], down12, up3), (own[1], up12, down3))
+    spare = spare_room((owners, MOST, slab_rows, side))
     arrived = [
         lax.all_to_all(
-            outgoing.reshape(owners, MOST, slab_rows, width), "fsdp", split_axis=0, concat_axis=0, tiled=True
+            outgoing.reshape(owners, MOST, slab_rows, -1), "fsdp", split_axis=0, concat_axis=0, tiled=True
         )
         for outgoing in (outgoing_a, outgoing_b)
     ]
-    results, done = precondition(
+    results = precondition(
         live, arrived, left_stats, right_stats, left_roots, right_roots, spare
     )
     returned = lax.all_to_all(results, "fsdp", split_axis=0, concat_axis=0, tiled=True)
-    left_out, right_out, left_new, right_new = update_stats(live, arrived, left_stats, right_stats, done)
-    preconditioned = assemble(slot, owner, returned)
+    left_out, right_out, left_new, right_new = update_stats(live, arrived, left_stats, right_stats)
+    preconditioned = assemble(place, returned.reshape(owners * MOST, slab_rows, side))
     return (
         preconditioned,
         left_out,

time: 116 us -> 108 us (0.931)
  starting transfers between devices: 35.7 us -> 30.4 us
  waiting for transfers between devices: 39.5 us -> 42.7 us
  Pallas kernels: 27.5 us -> 24.6 us
  local copies, waits for them, and re-layouts: 5.96 us -> 4.49 us
  other arithmetic: 5.73 us -> 4.47 us
    ppermute x6 -> x5, starting transfers between devices: 16.1 us -> 10.6 us  [send(): lax.ppermute(pair[1], 'rep', down)]
    add x2 -> x0, other arithmetic: 2.51 us -> none  [own_sums(): part(source, 0, half, column).astype(jnp.float32) + up2.astype(jnp.float32)]
    pallas_call x4, Pallas kernels: 14.3 us -> 12 us  [the longest x1 8.71 us: precondition(): pl.pallas_call(precondition_kernel, out_shape=jax.ShapeDtypeStruct((owner...]
    ppermute x6 -> x5, waiting for transfers between devices: 8.78 us -> 10.5 us  [send(): lax.ppermute(pair[0], 'rep', up)]
    unnamed x18 -> x8, local copies, waits for them, and re-layouts: 1.6 us -> 0.02 us
    ppermute x6 -> x5, starting transfers between devices: 2.17 us -> 3.01 us  [send(): lax.ppermute(pair[0], 'rep', up)]
    ppermute x6 -> x5, waiting for transfers between devices: 2.35 us -> 2.52 us  [send(): lax.ppermute(pair[1], 'rep', down)]
  transfers between devices with their start and end apart: 15 -> 13, of which waited for: 6 -> 7; matrix products, arithmetic and copies ran while one was open for 8% -> 7% of each run, Pallas kernels for 15% -> 13%
where the time goes in v5:
time: 108 us
  waiting for transfers between devices  42.7 us (40%)
  starting transfers between devices  30.4 us (28%)
  Pallas kernels  24.6 us (23%)
  local copies, waits for them, and re-layouts  4.49 us (4%)
  other arithmetic  4.47 us (4%)
    all_to_all x2, waiting for transfers between devices, on_device(): lax.all_to_all(outgoing.reshape(owners, MOST, slab_rows, -1), 'fsdp', spl...  17 us
    all_to_all x1, waiting for transfers between devices, on_device(): lax.all_to_all(results, 'fsdp', split_axis=0, concat_axis=0, tiled=True)  12.7 us
    all_to_all x2, starting transfers between devices, on_device(): lax.all_to_all(outgoing.reshape(owners, MOST, slab_rows, -1), 'fsdp', spl...  12.6 us
    pallas_call x1, Pallas kernels, update_stats(): pl.pallas_call(stats_kernel, grid=(MOST,), out_shape=[shape, shape, root,...  11 us
    ppermute x5, starting transfers between devices, send(): lax.ppermute(pair[1], 'rep', down)  10.6 us
    ppermute x5, waiting for transfers between devices, send(): lax.ppermute(pair[0], 'rep', up)  10.5 us
    pallas_call x1, Pallas kernels, precondition(): pl.pallas_call(precondition_kernel, out_shape=jax.ShapeDtypeStruct((owner...  8.71 us
    dynamic_slice x3, local copies, waits for them, and re-layouts, part(): lax.dynamic_slice(source, (start, 0, columns[0]), (half, slab_rows, colum...  4.47 us
  transfers between devices with their start and end apart: 13, of which 7 were waited for; matrix products, arithmetic and copies ran while one was open for 7% of the time, Pallas kernels for 13%

profile of v5, /device:TPU:0, one launch (start us, length us, event | category | flops | bytes accessed | tf_op | source)
XLA Modules:
  0.0 107.6 jit_solution(11311404265166907012)
XLA Ops:
  0.6 1.1 dynamic-slice_bitcast_fusion
  1.7 2.9 %collective-permute-start.4 = (bf16[32,16,256]{2,1,0:T(8,128)(2,1)S(1)}, bf16[32,16,256]{2,1,0:T(8,128)(2,1)S(1)}, u32[]{:S(2)}, u32[]{:S(2)}) collective-permute-start(bf16[32,16,256]{2,1,0:T(8,128)(2,1)S(1)} %get-tuple-element.39), channel_id=1, source_target_pairs={{0,96},{32,0},{64,32},{96,64},{1,97},{33,1},{65,33},{97,65},{2,98}... | collective-permute-start | bytes 786440 | tf_op jit(solution)/shard_map/ppermute | solution.py:450
  4.6 1.8 %constant_dynamic-slice_fusion.10 = (bf16[32,16,256]{2,1,0:T(8,128)(2,1)}, bf16[32,16,256]{2,1,0:T(8,128)(2,1)S(1)}) fusion(bf16[256,16,512]{2,1,0:T(8,128)(2,1)} %bitcast.12, s32[]{:T(128)S(6)} %mul.42, s32[]{:T(128)S(6)} %add.47), kind=kLoop, calls=%fused_computation.21 | loop fusion | bytes 1048584 | tf_op jit(solution)/shard_map/dynamic_slice | solution.py:445
  6.4 3.2 %collective-permute-start = (bf16[32,16,256]{2,1,0:T(8,128)(2,1)}, bf16[32,16,256]{2,1,0:T(8,128)(2,1)S(1)}, u32[]{:S(2)}, u32[]{:S(2)}) collective-permute-start(bf16[32,16,256]{2,1,0:T(8,128)(2,1)} %get-tuple-element.37), channel_id=1, source_target_pairs={{0,96},{32,0},{64,32},{96,64},{1,97},{33,1},{65,33},{97,65},{2,98}... | collective-permute-start | bytes 786440 | tf_op jit(solution)/shard_map/ppermute | solution.py:450
  9.6 1.4 %fusion.1 = (s32[]{:T(128)}, s32[64]{0:T(128)S(1)}) fusion(s32[]{:T(128)S(6)} %axis_index.25, s32[256,1]{0,1:T(1,128)} %param.7, s32[]{:T(128)S(6)} %mul.18), kind=kLoop, calls=%fused_computation.26 | loop fusion | flops 191 | bytes 524 | tf_op jit(solution)/shard_map/reduce_sum | solution.py:438
  11.0 0.2 convert_reduce_fusion.1
  11.2 0.1 convert_reduce_fusion
  11.3 3.4 %collective-permute-done.1 = bf16[32,16,256]{2,1,0:T(8,128)(2,1)S(1)} collective-permute-done((bf16[32,16,256]{2,1,0:T(8,128)(2,1)S(1)}, bf16[32,16,256]{2,1,0:T(8,128)(2,1)S(1)}, u32[]{:S(2)}, u32[]{:S(2)}) %collective-permute-start.1) | collective-permute-done | bytes 262176 | tf_op jit(solution)/shard_map/ppermute | solution.py:450
  14.7 1.3 %dynamic-slice_add_fusion = (bf16[32,16,256]{2,1,0:T(8,128)(2,1)S(1)}, bf16[32,16,256]{2,1,0:T(8,128)(2,1)S(1)}, bf16[32,16,256]{2,1,0:T(8,128)(2,1)S(1)}, bf16[32,16,256]{2,1,0:T(8,128)(2,1)S(1)}) fusion(bf16[32,16,256]{2,1,0:T(8,128)(2,1)S(1)} %collective-permute-done.4, bf16[256,16,512]{2,1,0:T(8,128)(2,1)} %bitcast.13, s32[]{:T(128)S(6)} %add.51, ...), kind=kLoop, calls=%fused_computation.2 | loop fusion | flops 262144 | bytes 2621456 | tf_op jit(solution)/shard_map/add | solution.py:471
  16.0 0.1 collective-permute-start.5
  16.1 2.0 %collective-permute-start.2 = (bf16[32,16,256]{2,1,0:T(8,128)(2,1)S(1)}, bf16[32,16,256]{2,1,0:T(8,128)(2,1)S(1)}, u32[]{:S(2)}, u32[]{:S(2)}) collective-permute-start(bf16[32,16,256]{2,1,0:T(8,128)(2,1)S(1)} %get-tuple-element.35), channel_id=1, source_target_pairs={{0,32},{32,64},{64,96},{96,0},{1,33},{33,65},{65,97},{97,1},{2,34}... | collective-permute-start | bytes 786440 | tf_op jit(solution)/shard_map/ppermute | solution.py:450
  18.1 1.6 %constant_dynamic-slice_fusion = (bf16[32,16,256]{2,1,0:T(8,128)(2,1)S(1)}, bf16[32,16,256]{2,1,0:T(8,128)(2,1)S(1)}, bf16[32,16,256]{2,1,0:T(8,128)(2,1)S(1)}, ...) fusion(bf16[256,16,512]{2,1,0:T(8,128)(2,1)} %bitcast.14, ...), kind=kLoop, calls=%fused_computation.11 | loop fusion | bytes 4194336 | tf_op jit(solution)/shard_map/dynamic_slice | solution.py:445
  19.8 1.4 %collective-permute-start.6 = (bf16[64,16,256]{2,1,0:T(8,128)(2,1)S(1)}, bf16[64,16,256]{2,1,0:T(8,128)(2,1)S(1)}, u32[]{:S(2)}, u32[]{:S(2)}) collective-permute-start(bf16[64,16,256]{2,1,0:T(8,128)(2,1)S(1)} %pad_maximum_fusion), channel_id=1, source_target_pairs={{0,96},{32,0},{64,32},{96,64},{1,97},{33,1},{65,33},{97,65},{2,98}... | collective-permute-start | bytes 1572872 | tf_op jit(solution)/shard_map/ppermute | solution.py:450
  21.2 0.8 pad_maximum_fusion.1
  22.0 0.7 collective-permute-start.7
  22.7 2.5 %collective-permute-done.5.rest_5_ = bf16[32,16,256]{2,1,0:T(8,128)(2,1)S(1)} collective-permute-done((bf16[32,16,256]{2,1,0:T(8,128)(2,1)S(1)}, bf16[32,16,256]{2,1,0:T(8,128)(2,1)S(1)}, u32[]{:S(2)}, u32[]{:S(2)}) %collective-permute-start.5) | collective-permute-done | bytes 262176 | tf_op jit(solution)/shard_map/ppermute | solution.py:450
  25.2 0.7 collective-permute-done.2.rest_2_
  25.9 1.6 %place_blocks.2.rest_0_ = bf16[96,16,256]{2,1,0:T(8,128)(2,1)} custom-call(s32[64]{0:T(128)S(1)} %multiply_add_fusion.place_ref, s32[96]{0:T(128)S(1)} %broadcast_subtract_fusion.empty_ref, bf16[32,16,256]{2,1,0:T(8,128)(2,1)S(1)} %get-tuple-element.36.rest_0_, bf16[32,16,256]{2,1,0:T(8,128)(2,1)S(1)} %collective-permute-done.rest_1_, ...), custom_call_target="tpu_custom_call" | custom-call | flops 8053063680 | bytes 2097152 | tf_op jit(solution)/shard_map/place_blocks/pallas_call | solution.py:126
  27.6 8.5 %all-to-all-start = ((bf16[32,3,16,256]{3,2,1,0:T(8,128)(2,1)}), bf16[32,3,16,256]{3,2,1,0:T(8,128)(2,1)}, u32[]{:S(2)}, u32[]{:S(2)}) async-start(bf16[32,3,16,256]{3,2,1,0:T(8,128)(2,1)} %bitcast.4), calls=%async_computation | async-start | bytes 1572864 | tf_op jit(solution)/shard_map/all_to_all | solution.py:484
  36.1 0.3 collective-permute-start.8
  36.5 3.0 %collective-permute-start.9 = (bf16[32,16,256]{2,1,0:T(8,128)(2,1)S(1)}, bf16[32,16,256]{2,1,0:T(8,128)(2,1)S(1)}, u32[]{:S(2)}, u32[]{:S(2)}) collective-permute-start(bf16[32,16,256]{2,1,0:T(8,128)(2,1)S(1)} %get-tuple-element.18), channel_id=1, source_target_pairs={{0,96},{32,0},{64,32},{96,64},{1,97},{33,1},{65,33},{97,65},{2,98}... | collective-permute-start | bytes 786440 | tf_op jit(solution)/shard_map/ppermute | solution.py:450
  39.4 6.4 %collective-permute-done.8.rest_2_ = bf16[32,16,256]{2,1,0:T(8,128)(2,1)S(1)} collective-permute-done((bf16[32,16,256]{2,1,0:T(8,128)(2,1)S(1)}, bf16[32,16,256]{2,1,0:T(8,128)(2,1)S(1)}, u32[]{:S(2)}, u32[]{:S(2)}) %collective-permute-start.8) | collective-permute-done | bytes 262176 | tf_op jit(solution)/shard_map/ppermute | solution.py:450
  45.8 1.6 %place_blocks.3 = bf16[96,16,256]{2,1,0:T(8,128)(2,1)} custom-call(s32[64]{0:T(128)S(1)} %multiply_add_fusion.place_ref, s32[96]{0:T(128)S(1)} %copy-done.3, bf16[32,16,256]{2,1,0:T(8,128)(2,1)S(1)} %get-tuple-element.32.rest_0_, bf16[64,16,256]{2,1,0:T(8,128)(2,1)S(1)} %collective-permute-done.6.four_ref.rest_1_, ...), custom_call_target="tpu_custom_call" | custom-call | bytes 2097152 | tf_op jit(solution)/shard_map/place_blocks/pallas_call | solution.py:126
  47.5 3.1 %all-to-all-done.arrived_a.front_ref = bf16[32,3,16,256]{3,2,1,0:T(8,128)(2,1)} async-done(((bf16[32,3,16,256]{3,2,1,0:T(8,128)(2,1)}), bf16[32,3,16,256]{3,2,1,0:T(8,128)(2,1)}, u32[]{:S(2)}, u32[]{:S(2)}) %all-to-all-start) | async-done | bytes 786464 | tf_op jit(solution)/shard_map/all_to_all | solution.py:484
  50.6 4.2 %all-to-all-start.1 = ((bf16[32,3,16,256]{3,2,1,0:T(8,128)(2,1)}), bf16[32,3,16,256]{3,2,1,0:T(8,128)(2,1)S(1)}, u32[]{:S(2)}, u32[]{:S(2)}) async-start(bf16[32,3,16,256]{3,2,1,0:T(8,128)(2,1)} %bitcast.5), calls=%async_computation.1 | async-start | bytes 1572864 | tf_op jit(solution)/shard_map/all_to_all | solution.py:484
  54.8 0.7 compare_convert_fusion.live_ref
  55.4 13.9 %all-to-all-done.1.arrived_b.back_ref = bf16[32,3,16,256]{3,2,1,0:T(8,128)(2,1)S(1)} async-done(((bf16[32,3,16,256]{3,2,1,0:T(8,128)(2,1)}), bf16[32,3,16,256]{3,2,1,0:T(8,128)(2,1)S(1)}, u32[]{:S(2)}, u32[]{:S(2)}) %all-to-all-start.1) | async-done | bytes 786464 | tf_op jit(solution)/shard_map/all_to_all | solution.py:484
  69.3 8.7 %precondition.1 = bf16[32,3,16,512]{3,2,1,0:T(8,128)(2,1)} custom-call(s32[3]{0:T(128)S(1)} %compare_convert_fusion.live_ref, bf16[32,3,16,256]{3,2,1,0:T(8,128)(2,1)} %all-to-all-done.arrived_a.front_ref, bf16[32,3,16,256]{3,2,1,0:T(8,128)(2,1)S(1)} %all-to-all-done.1.arrived_b.back_ref, ...), custom_call_target="tpu_custom_call", output_to_operand_aliasing={{}: (7, {})} | custom-call | flops 3758096384 | bytes 9437184 | tf_op jit(solution)/shard_map/precondition/pallas_call | solution.py:311
  78.0 4.2 %all-to-all-start.2 = ((bf16[32,3,16,512]{3,2,1,0:T(8,128)(2,1)}), bf16[32,3,16,512]{3,2,1,0:T(8,128)(2,1)S(1)}, u32[]{:S(2)}, u32[]{:S(2)}) async-start(bf16[32,3,16,512]{3,2,1,0:T(8,128)(2,1)} %precondition.1), calls=%async_computation.2 | async-start | bytes 3145728 | tf_op jit(solution)/shard_map/all_to_all | solution.py:492
  82.2 11.0 %update_stats.1 = (f32[1,1,3,512,512]{4,3,2,1,0:T(8,128)}, f32[1,1,3,512,512]{4,3,2,1,0:T(8,128)}, bf16[1,1,512,512]{3,2,1,0:T(8,128)(2,1)}, bf16[1,1,512,512]{3,2,1,0:T(8,128)(2,1)}) custom-call(s32[3]{0:T(128)S(1)} %compare_convert_fusion.live_ref, bf16[32,3,16,256]{3,2,1,0:T(8,128)(2,1)} %all-to-all-done.arrived_a.front_ref, ...), custom_call_target="tpu_custom_call" | custom-call | flops 3221225472 | bytes 13631488 | tf_op jit(solution)/shard_map/update_stats/pallas_call | solution.py:367
  93.3 12.7 %all-to-all-done.2 = bf16[32,3,16,512]{3,2,1,0:T(8,128)(2,1)S(1)} async-done(((bf16[32,3,16,512]{3,2,1,0:T(8,128)(2,1)}), bf16[32,3,16,512]{3,2,1,0:T(8,128)(2,1)S(1)}, u32[]{:S(2)}, u32[]{:S(2)}) %all-to-all-start.2) | async-done | bytes 1572896 | tf_op jit(solution)/shard_map/all_to_all | solution.py:492
  106.0 1.5 %assemble.1 = bf16[64,16,512]{2,1,0:T(8,128)(2,1)} custom-call(s32[64]{0:T(128)S(1)} %copy-done.1, bf16[96,16,512]{2,1,0:T(8,128)(2,1)S(1)} %bitcast.11), custom_call_target="tpu_custom_call" | custom-call | bytes 2097152 | tf_op jit(solution)/shard_map/assemble/pallas_call | solution.py:403
  (21 shorter events, 0.2 us)
Async XLA Ops:
  1.7 9.6 %collective-permute-start.4 = (bf16[32,16,256]{2,1,0:T(8,128)(2,1)S(1)}, bf16[32,16,256]{2,1,0:T(8,128)(2,1)S(1)}, u32[]{:S(2)}, u32[]{:S(2)}) collective-permute-start(bf16[32,16,256]{2,1,0:T(8,128)(2,1)S(1)} %get-tuple-element.39), channel_id=1, source_target_pairs={{0,96},{32,0},{64,32},{96,64},{1,97},{33,1},{65,33},{97,65},{2,98}... | collective-permute-start | bytes 786440 | tf_op jit(solution)/shard_map/ppermute | solution.py:450
  4.6 10.1 %collective-permute-start.1 = (bf16[32,16,256]{2,1,0:T(8,128)(2,1)S(1)}, bf16[32,16,256]{2,1,0:T(8,128)(2,1)S(1)}, u32[]{:S(2)}, u32[]{:S(2)}) collective-permute-start(bf16[32,16,256]{2,1,0:T(8,128)(2,1)S(1)} %get-tuple-element.40), channel_id=1, source_target_pairs={{0,32},{32,64},{64,96},{96,0},{1,33},{33,65},{65,97},{97,1},{2,34}... | collective-permute-start | bytes 786440 | tf_op jit(solution)/shard_map/ppermute | solution.py:450
  6.4 15.6 %collective-permute-start = (bf16[32,16,256]{2,1,0:T(8,128)(2,1)}, bf16[32,16,256]{2,1,0:T(8,128)(2,1)S(1)}, u32[]{:S(2)}, u32[]{:S(2)}) collective-permute-start(bf16[32,16,256]{2,1,0:T(8,128)(2,1)} %get-tuple-element.37), channel_id=1, source_target_pairs={{0,96},{32,0},{64,32},{96,64},{1,97},{33,1},{65,33},{97,65},{2,98}... | collective-permute-start | bytes 786440 | tf_op jit(solution)/shard_map/ppermute | solution.py:450
  9.6 13.1 %collective-permute-start.3 = (bf16[32,16,256]{2,1,0:T(8,128)(2,1)S(1)}, bf16[32,16,256]{2,1,0:T(8,128)(2,1)S(1)}, u32[]{:S(2)}, u32[]{:S(2)}) collective-permute-start(bf16[32,16,256]{2,1,0:T(8,128)(2,1)S(1)} %get-tuple-element.38), channel_id=1, source_target_pairs={{0,32},{32,64},{64,96},{96,0},{1,33},{33,65},{65,97},{97,1},{2,34}... | collective-permute-start | bytes 786440 | tf_op jit(solution)/shard_map/ppermute | solution.py:450
  11.2 34.7 %copy-start = (s32[64]{0:T(128)}, s32[64]{0:T(128)S(1)}, u32[]{:S(2)}) copy-start(s32[64]{0:T(128)S(1)} %multiply_add_fusion.place_ref) | copy-start | bytes 772
  11.3 14.6 %copy-start.2 = (s32[96]{0:T(128)}, s32[96]{0:T(128)S(1)}, u32[]{:S(2)}) copy-start(s32[96]{0:T(128)S(1)} %broadcast_subtract_fusion.empty_ref) | copy-start | bytes 1156
  16.0 9.2 %collective-permute-start.5 = (bf16[32,16,256]{2,1,0:T(8,128)(2,1)S(1)}, bf16[32,16,256]{2,1,0:T(8,128)(2,1)S(1)}, u32[]{:S(2)}, u32[]{:S(2)}) collective-permute-start(bf16[32,16,256]{2,1,0:T(8,128)(2,1)S(1)} %get-tuple-element.33), channel_id=1, source_target_pairs={{0,96},{32,0},{64,32},{96,64},{1,97},{33,1},{65,33},{97,65},{2,98}... | collective-permute-start | bytes 786440 | tf_op jit(solution)/shard_map/ppermute | solution.py:450
  16.1 9.8 %collective-permute-start.2 = (bf16[32,16,256]{2,1,0:T(8,128)(2,1)S(1)}, bf16[32,16,256]{2,1,0:T(8,128)(2,1)S(1)}, u32[]{:S(2)}, u32[]{:S(2)}) collective-permute-start(bf16[32,16,256]{2,1,0:T(8,128)(2,1)S(1)} %get-tuple-element.35), channel_id=1, source_target_pairs={{0,32},{32,64},{64,96},{96,0},{1,33},{33,65},{65,97},{97,1},{2,34}... | collective-permute-start | bytes 786440 | tf_op jit(solution)/shard_map/ppermute | solution.py:450
  19.8 16.2 %collective-permute-start.6 = (bf16[64,16,256]{2,1,0:T(8,128)(2,1)S(1)}, bf16[64,16,256]{2,1,0:T(8,128)(2,1)S(1)}, u32[]{:S(2)}, u32[]{:S(2)}) collective-permute-start(bf16[64,16,256]{2,1,0:T(8,128)(2,1)S(1)} %pad_maximum_fusion), channel_id=1, source_target_pairs={{0,96},{32,0},{64,32},{96,64},{1,97},{33,1},{65,33},{97,65},{2,98}... | collective-permute-start | bytes 1572872 | tf_op jit(solution)/shard_map/ppermute | solution.py:450
  22.0 14.1 %collective-permute-start.7 = (bf16[64,16,256]{2,1,0:T(8,128)(2,1)}, bf16[64,16,256]{2,1,0:T(8,128)(2,1)S(1)}, u32[]{:S(2)}, u32[]{:S(2)}) collective-permute-start(bf16[64,16,256]{2,1,0:T(8,128)(2,1)} %pad_maximum_fusion.1), channel_id=1, source_target_pairs={{0,32},{32,64},{64,96},{96,0},{1,33},{33,65},{65,97},{97,1},{2,34}... | collective-permute-start | bytes 1572872 | tf_op jit(solution)/shard_map/ppermute | solution.py:450
  27.6 23.0 %all-to-all-start = ((bf16[32,3,16,256]{3,2,1,0:T(8,128)(2,1)}), bf16[32,3,16,256]{3,2,1,0:T(8,128)(2,1)}, u32[]{:S(2)}, u32[]{:S(2)}) async-start(bf16[32,3,16,256]{3,2,1,0:T(8,128)(2,1)} %bitcast.4), calls=%async_computation | async-start | bytes 1572864 | tf_op jit(solution)/shard_map/all_to_all | solution.py:484
  36.1 9.8 %copy-start.3 = (s32[96]{0:T(128)S(1)}, s32[96]{0:T(128)}, u32[]{:S(2)}) copy-start(s32[96]{0:T(128)} %copy-done.2) | copy-start | bytes 1156
  36.1 9.7 %collective-permute-start.8 = (bf16[32,16,256]{2,1,0:T(8,128)(2,1)S(1)}, bf16[32,16,256]{2,1,0:T(8,128)(2,1)S(1)}, u32[]{:S(2)}, u32[]{:S(2)}) collective-permute-start(bf16[32,16,256]{2,1,0:T(8,128)(2,1)S(1)} %get-tuple-element.17), channel_id=1, source_target_pairs={{0,32},{32,64},{64,96},{96,0},{1,33},{33,65},{65,97},{97,1},{2,34}... | collective-permute-start | bytes 786440 | tf_op jit(solution)/shard_map/ppermute | solution.py:450
  36.5 9.4 %collective-permute-start.9 = (bf16[32,16,256]{2,1,0:T(8,128)(2,1)S(1)}, bf16[32,16,256]{2,1,0:T(8,128)(2,1)S(1)}, u32[]{:S(2)}, u32[]{:S(2)}) collective-permute-start(bf16[32,16,256]{2,1,0:T(8,128)(2,1)S(1)} %get-tuple-element.18), channel_id=1, source_target_pairs={{0,96},{32,0},{64,32},{96,64},{1,97},{33,1},{65,33},{97,65},{2,98}... | collective-permute-start | bytes 786440 | tf_op jit(solution)/shard_map/ppermute | solution.py:450
  50.6 18.7 %all-to-all-start.1 = ((bf16[32,3,16,256]{3,2,1,0:T(8,128)(2,1)}), bf16[32,3,16,256]{3,2,1,0:T(8,128)(2,1)S(1)}, u32[]{:S(2)}, u32[]{:S(2)}) async-start(bf16[32,3,16,256]{3,2,1,0:T(8,128)(2,1)} %bitcast.5), calls=%async_computation.1 | async-start | bytes 1572864 | tf_op jit(solution)/shard_map/all_to_all | solution.py:484
  78.0 27.9 %all-to-all-start.2 = ((bf16[32,3,16,512]{3,2,1,0:T(8,128)(2,1)}), bf16[32,3,16,512]{3,2,1,0:T(8,128)(2,1)S(1)}, u32[]{:S(2)}, u32[]{:S(2)}) async-start(bf16[32,3,16,512]{3,2,1,0:T(8,128)(2,1)} %precondition.1), calls=%async_computation.2 | async-start | bytes 3145728 | tf_op jit(solution)/shard_map/all_to_all | solution.py:492
  82.2 23.8 %copy-start.1 = (s32[64]{0:T(128)S(1)}, s32[64]{0:T(128)}, u32[]{:S(2)}) copy-start(s32[64]{0:T(128)} %copy-done) | copy-start | bytes 772

commit v6 on v5

--- a/solution.py
+++ b/solution.py
@@ -467,7 +467,7 @@
     second = seconds(later, parts[0])
     up2, down2 = send(second)
     later, _ = lax.optimization_barrier((later, second))
-    own, mid = owns(later, parts[0]), mids(later, parts[0])
+    own, mid = lax.optimization_barrier((owns(later, parts[0]), mids(later, parts[0])))
     third = mid[0] + up1, mid[1] + down1
     up3, down3 = send(third)
     later, _ = lax.optimization_barrier((later, third))

time: 108 us -> 108 us (level)
  waiting for transfers between devices: 42.7 us -> 41.2 us
  local copies, waits for them, and re-layouts: 4.49 us -> 5.85 us
  starting transfers between devices: 30.4 us -> 31.7 us
  other arithmetic: 4.47 us -> 3.33 us
    ppermute x5, waiting for transfers between devices: 2.52 us -> 0.01 us  [send(): lax.ppermute(pair[1], 'rep', down)]
    ppermute x5, starting transfers between devices: 10.6 us -> 12.8 us  [send(): lax.ppermute(pair[1], 'rep', down)]
    dynamic_slice x3 -> x4, local copies, waits for them, and re-layouts: 4.47 us -> 5.83 us  [part(): lax.dynamic_slice(source, (start, 0, columns[0]), (half, slab_rows, colum...]
    add x1 -> x2, other arithmetic: 1.29 us -> 0.15 us  [on_device(): third = (mid[0] + up1, mid[1] + down1)]
  transfers between devices with their start and end apart: 13 -> 13, of which waited for: 7 -> 6; matrix products, arithmetic and copies ran while one was open for 7% -> 8% of each run, Pallas kernels for 13% -> 13%
where the time goes in v6:
time: 108 us
  waiting for transfers between devices  41.2 us (38%)
  starting transfers between devices  31.7 us (29%)
  Pallas kernels  24.6 us (23%)
  local copies, waits for them, and re-layouts  5.85 us (5%)
  other arithmetic  3.33 us (3%)
    all_to_all x2, waiting for transfers between devices, on_device(): lax.all_to_all(outgoing.reshape(owners, MOST, slab_rows, -1), 'fsdp', spl...  17 us
    ppermute x5, starting transfers between devices, send(): lax.ppermute(pair[1], 'rep', down)  12.8 us
    all_to_all x1, waiting for transfers between devices, on_device(): lax.all_to_all(results, 'fsdp', split_axis=0, concat_axis=0, tiled=True)  12.7 us
    all_to_all x2, starting transfers between devices, on_device(): lax.all_to_all(outgoing.reshape(owners, MOST, slab_rows, -1), 'fsdp', spl...  12.7 us
    ppermute x5, waiting for transfers between devices, send(): lax.ppermute(pair[0], 'rep', up)  11.5 us
    pallas_call x1, Pallas kernels, update_stats(): pl.pallas_call(stats_kernel, grid=(MOST,), out_shape=[shape, shape, root,...  11 us
    pallas_call x1, Pallas kernels, precondition(): pl.pallas_call(precondition_kernel, out_shape=jax.ShapeDtypeStruct((owner...  8.71 us
    dynamic_slice x4, local copies, waits for them, and re-layouts, part(): lax.dynamic_slice(source, (start, 0, columns[0]), (half, slab_rows, colum...  5.83 us
  transfers between devices with their start and end apart: 13, of which 6 were waited for; matrix products, arithmetic and copies ran while one was open for 8% of the time, Pallas kernels for 13%

profile of v6, /device:TPU:0, one launch (start us, length us, event | category | flops | bytes accessed | tf_op | source)
XLA Modules:
  0.0 107.7 jit_solution(17835548428832477323)
XLA Ops:
  0.6 1.1 dynamic-slice_bitcast_fusion
  1.7 2.9 %collective-permute-start.4 = (bf16[32,16,256]{2,1,0:T(8,128)(2,1)S(1)}, bf16[32,16,256]{2,1,0:T(8,128)(2,1)S(1)}, u32[]{:S(2)}, u32[]{:S(2)}) collective-permute-start(bf16[32,16,256]{2,1,0:T(8,128)(2,1)S(1)} %get-tuple-element.47), channel_id=1, source_target_pairs={{0,96},{32,0},{64,32},{96,64},{1,97},{33,1},{65,33},{97,65},{2,98}... | collective-permute-start | bytes 786440 | tf_op jit(solution)/shard_map/ppermute | solution.py:450
  4.6 1.8 %constant_dynamic-slice_fusion.12 = (bf16[32,16,256]{2,1,0:T(8,128)(2,1)}, bf16[32,16,256]{2,1,0:T(8,128)(2,1)S(1)}) fusion(bf16[256,16,512]{2,1,0:T(8,128)(2,1)} %bitcast.12, s32[]{:T(128)S(6)} %mul.42, s32[]{:T(128)S(6)} %add.47), kind=kLoop, calls=%fused_computation.21 | loop fusion | bytes 1048584 | tf_op jit(solution)/shard_map/dynamic_slice | solution.py:445
  6.4 3.2 %collective-permute-start = (bf16[32,16,256]{2,1,0:T(8,128)(2,1)}, bf16[32,16,256]{2,1,0:T(8,128)(2,1)S(1)}, u32[]{:S(2)}, u32[]{:S(2)}) collective-permute-start(bf16[32,16,256]{2,1,0:T(8,128)(2,1)} %get-tuple-element.45), channel_id=1, source_target_pairs={{0,96},{32,0},{64,32},{96,64},{1,97},{33,1},{65,33},{97,65},{2,98}... | collective-permute-start | bytes 786440 | tf_op jit(solution)/shard_map/ppermute | solution.py:450
  9.6 1.4 %fusion.1 = (s32[]{:T(128)}, s32[64]{0:T(128)S(1)}) fusion(s32[]{:T(128)S(6)} %axis_index.25, s32[256,1]{0,1:T(1,128)} %param.7, s32[]{:T(128)S(6)} %mul.18), kind=kLoop, calls=%fused_computation.26 | loop fusion | flops 191 | bytes 524 | tf_op jit(solution)/shard_map/reduce_sum | solution.py:438
  11.0 0.2 convert_reduce_fusion.1
  11.2 1.3 %constant_dynamic-slice_fusion.8 = (bf16[32,16,256]{2,1,0:T(8,128)(2,1)S(1)}, bf16[32,16,256]{2,1,0:T(8,128)(2,1)S(1)}, bf16[32,16,256]{2,1,0:T(8,128)(2,1)S(1)}, bf16[32,16,256]{2,1,0:T(8,128)(2,1)S(1)}) fusion(bf16[256,16,512]{2,1,0:T(8,128)(2,1)} %bitcast.13, s32[]{:T(128)S(6)} %add.50, s32[]{:T(128)S(6)} %mul.41, s32[]{:T(128)S(6)} %add.49, s32[]{:T(128)S(6)} %mul.43), kind=kLoop, calls=%fused_computation.17 | loop fusion | bytes 2097168 | tf_op jit(solution)/shard_map/dynamic_slice | solution.py:445
  12.5 0.1 convert_reduce_fusion
  12.6 2.1 %collective-permute-done.1 = bf16[32,16,256]{2,1,0:T(8,128)(2,1)S(1)} collective-permute-done((bf16[32,16,256]{2,1,0:T(8,128)(2,1)S(1)}, bf16[32,16,256]{2,1,0:T(8,128)(2,1)S(1)}, u32[]{:S(2)}, u32[]{:S(2)}) %collective-permute-start.1) | collective-permute-done | bytes 262176 | tf_op jit(solution)/shard_map/ppermute | solution.py:450
  14.8 0.1 collective-permute-start.2
  14.9 0.1 add.52
  15.0 3.3 %collective-permute-start.5 = (bf16[32,16,256]{2,1,0:T(8,128)(2,1)S(1)}, bf16[32,16,256]{2,1,0:T(8,128)(2,1)S(1)}, u32[]{:S(2)}, u32[]{:S(2)}) collective-permute-start(bf16[32,16,256]{2,1,0:T(8,128)(2,1)S(1)} %add.52), channel_id=1, source_target_pairs={{0,96},{32,0},{64,32},{96,64},{1,97},{33,1},{65,33},{97,65},{2,98}... | collective-permute-start | bytes 786440 | tf_op jit(solution)/shard_map/ppermute | solution.py:450
  18.2 1.7 %constant_dynamic-slice_fusion = (bf16[32,16,256]{2,1,0:T(8,128)(2,1)S(1)}, bf16[32,16,256]{2,1,0:T(8,128)(2,1)S(1)}, bf16[32,16,256]{2,1,0:T(8,128)(2,1)S(1)}, ...) fusion(bf16[256,16,512]{2,1,0:T(8,128)(2,1)} %bitcast.14, ...), kind=kLoop, calls=%fused_computation.9 | loop fusion | bytes 4194336 | tf_op jit(solution)/shard_map/dynamic_slice | solution.py:445
  20.0 0.1 collective-permute-start.6
  20.1 0.8 pad_maximum_fusion.1
  21.0 2.0 %collective-permute-start.7 = (bf16[64,16,256]{2,1,0:T(8,128)(2,1)}, bf16[64,16,256]{2,1,0:T(8,128)(2,1)S(1)}, u32[]{:S(2)}, u32[]{:S(2)}) collective-permute-start(bf16[64,16,256]{2,1,0:T(8,128)(2,1)} %pad_maximum_fusion.1), channel_id=1, source_target_pairs={{0,32},{32,64},{64,96},{96,0},{1,33},{33,65},{65,97},{97,1},{2,34}... | collective-permute-start | bytes 1572872 | tf_op jit(solution)/shard_map/ppermute | solution.py:450
  23.0 3.0 %collective-permute-done.2.rest_2_ = bf16[32,16,256]{2,1,0:T(8,128)(2,1)S(1)} collective-permute-done((bf16[32,16,256]{2,1,0:T(8,128)(2,1)S(1)}, bf16[32,16,256]{2,1,0:T(8,128)(2,1)S(1)}, u32[]{:S(2)}, u32[]{:S(2)}) %collective-permute-start.2) | collective-permute-done | bytes 262176 | tf_op jit(solution)/shard_map/ppermute | solution.py:450
  26.0 1.7 %place_blocks.2.rest_0_ = bf16[96,16,256]{2,1,0:T(8,128)(2,1)} custom-call(s32[64]{0:T(128)S(1)} %multiply_add_fusion.place_ref, s32[96]{0:T(128)S(1)} %broadcast_subtract_fusion.empty_ref, bf16[32,16,256]{2,1,0:T(8,128)(2,1)S(1)} %get-tuple-element.20.rest_0_, bf16[32,16,256]{2,1,0:T(8,128)(2,1)S(1)} %collective-permute-done.rest_1_, ...), custom_call_target="tpu_custom_call" | custom-call | flops 8053063680 | bytes 2097152 | tf_op jit(solution)/shard_map/place_blocks/pallas_call | solution.py:126
  27.6 8.5 %all-to-all-start = ((bf16[32,3,16,256]{3,2,1,0:T(8,128)(2,1)}), bf16[32,3,16,256]{3,2,1,0:T(8,128)(2,1)}, u32[]{:S(2)}, u32[]{:S(2)}) async-start(bf16[32,3,16,256]{3,2,1,0:T(8,128)(2,1)} %bitcast.4), calls=%async_computation | async-start | bytes 1572864 | tf_op jit(solution)/shard_map/all_to_all | solution.py:484
  36.2 0.1 collective-permute-start.8
  36.3 3.2 %collective-permute-start.9 = (bf16[32,16,256]{2,1,0:T(8,128)(2,1)S(1)}, bf16[32,16,256]{2,1,0:T(8,128)(2,1)S(1)}, u32[]{:S(2)}, u32[]{:S(2)}) collective-permute-start(bf16[32,16,256]{2,1,0:T(8,128)(2,1)S(1)} %get-tuple-element.26), channel_id=1, source_target_pairs={{0,96},{32,0},{64,32},{96,64},{1,97},{33,1},{65,33},{97,65},{2,98}... | collective-permute-start | bytes 786440 | tf_op jit(solution)/shard_map/ppermute | solution.py:450
  39.5 6.4 %collective-permute-done.8.rest_2_ = bf16[32,16,256]{2,1,0:T(8,128)(2,1)S(1)} collective-permute-done((bf16[32,16,256]{2,1,0:T(8,128)(2,1)S(1)}, bf16[32,16,256]{2,1,0:T(8,128)(2,1)S(1)}, u32[]{:S(2)}, u32[]{:S(2)}) %collective-permute-start.8) | collective-permute-done | bytes 262176 | tf_op jit(solution)/shard_map/ppermute | solution.py:450
  45.9 1.6 %place_blocks.3 = bf16[96,16,256]{2,1,0:T(8,128)(2,1)} custom-call(s32[64]{0:T(128)S(1)} %copy-done.1, s32[96]{0:T(128)S(1)} %copy-done.3, bf16[32,16,256]{2,1,0:T(8,128)(2,1)S(1)} %get-tuple-element.40.rest_0_, bf16[64,16,256]{2,1,0:T(8,128)(2,1)S(1)} %collective-permute-done.6.four_ref.rest_1_, bf16[32,16,256]{2,1,0:T(8,128)(2,1)S(1)} %collective-permute-done.8.rest_2_, ...), custom_call_target="tpu_custom_call" | custom-call | bytes 2097152 | tf_op jit(solution)/shard_map/place_blocks/pallas_call | solution.py:126
  47.5 3.1 %all-to-all-done.arrived_a.front_ref = bf16[32,3,16,256]{3,2,1,0:T(8,128)(2,1)} async-done(((bf16[32,3,16,256]{3,2,1,0:T(8,128)(2,1)}), bf16[32,3,16,256]{3,2,1,0:T(8,128)(2,1)}, u32[]{:S(2)}, u32[]{:S(2)}) %all-to-all-start) | async-done | bytes 786464 | tf_op jit(solution)/shard_map/all_to_all | solution.py:484
  50.6 4.2 %all-to-all-start.1 = ((bf16[32,3,16,256]{3,2,1,0:T(8,128)(2,1)}), bf16[32,3,16,256]{3,2,1,0:T(8,128)(2,1)S(1)}, u32[]{:S(2)}, u32[]{:S(2)}) async-start(bf16[32,3,16,256]{3,2,1,0:T(8,128)(2,1)} %bitcast.5), calls=%async_computation.1 | async-start | bytes 1572864 | tf_op jit(solution)/shard_map/all_to_all | solution.py:484
  54.8 0.7 compare_convert_fusion.live_ref
  55.5 13.9 %all-to-all-done.1.arrived_b.back_ref = bf16[32,3,16,256]{3,2,1,0:T(8,128)(2,1)S(1)} async-done(((bf16[32,3,16,256]{3,2,1,0:T(8,128)(2,1)}), bf16[32,3,16,256]{3,2,1,0:T(8,128)(2,1)S(1)}, u32[]{:S(2)}, u32[]{:S(2)}) %all-to-all-start.1) | async-done | bytes 786464 | tf_op jit(solution)/shard_map/all_to_all | solution.py:484
  69.4 8.7 %precondition.1 = bf16[32,3,16,512]{3,2,1,0:T(8,128)(2,1)} custom-call(s32[3]{0:T(128)S(1)} %compare_convert_fusion.live_ref, bf16[32,3,16,256]{3,2,1,0:T(8,128)(2,1)} %all-to-all-done.arrived_a.front_ref, bf16[32,3,16,256]{3,2,1,0:T(8,128)(2,1)S(1)} %all-to-all-done.1.arrived_b.back_ref, ...), custom_call_target="tpu_custom_call", output_to_operand_aliasing={{}: (7, {})} | custom-call | flops 3758096384 | bytes 9437184 | tf_op jit(solution)/shard_map/precondition/pallas_call | solution.py:311
  78.1 4.2 %all-to-all-start.2 = ((bf16[32,3,16,512]{3,2,1,0:T(8,128)(2,1)}), bf16[32,3,16,512]{3,2,1,0:T(8,128)(2,1)S(1)}, u32[]{:S(2)}, u32[]{:S(2)}) async-start(bf16[32,3,16,512]{3,2,1,0:T(8,128)(2,1)} %precondition.1), calls=%async_computation.2 | async-start | bytes 3145728 | tf_op jit(solution)/shard_map/all_to_all | solution.py:492
  82.3 11.0 %update_stats.1 = (f32[1,1,3,512,512]{4,3,2,1,0:T(8,128)}, f32[1,1,3,512,512]{4,3,2,1,0:T(8,128)}, bf16[1,1,512,512]{3,2,1,0:T(8,128)(2,1)}, bf16[1,1,512,512]{3,2,1,0:T(8,128)(2,1)}) custom-call(s32[3]{0:T(128)S(1)} %compare_convert_fusion.live_ref, bf16[32,3,16,256]{3,2,1,0:T(8,128)(2,1)} %all-to-all-done.arrived_a.front_ref, ...), custom_call_target="tpu_custom_call" | custom-call | flops 3221225472 | bytes 13631488 | tf_op jit(solution)/shard_map/update_stats/pallas_call | solution.py:367
  93.3 12.7 %all-to-all-done.2 = bf16[32,3,16,512]{3,2,1,0:T(8,128)(2,1)S(1)} async-done(((bf16[32,3,16,512]{3,2,1,0:T(8,128)(2,1)}), bf16[32,3,16,512]{3,2,1,0:T(8,128)(2,1)S(1)}, u32[]{:S(2)}, u32[]{:S(2)}) %all-to-all-start.2) | async-done | bytes 1572896 | tf_op jit(solution)/shard_map/all_to_all | solution.py:492
  106.0 1.5 %assemble.1 = bf16[64,16,512]{2,1,0:T(8,128)(2,1)} custom-call(s32[64]{0:T(128)S(1)} %copy-done.1, bf16[96,16,512]{2,1,0:T(8,128)(2,1)S(1)} %bitcast.11), custom_call_target="tpu_custom_call" | custom-call | bytes 2097152 | tf_op jit(solution)/shard_map/assemble/pallas_call | solution.py:403
  (23 shorter events, 0.2 us)
Async XLA Ops:
  1.7 13.2 %collective-permute-start.4 = (bf16[32,16,256]{2,1,0:T(8,128)(2,1)S(1)}, bf16[32,16,256]{2,1,0:T(8,128)(2,1)S(1)}, u32[]{:S(2)}, u32[]{:S(2)}) collective-permute-start(bf16[32,16,256]{2,1,0:T(8,128)(2,1)S(1)} %get-tuple-element.47), channel_id=1, source_target_pairs={{0,96},{32,0},{64,32},{96,64},{1,97},{33,1},{65,33},{97,65},{2,98}... | collective-permute-start | bytes 786440 | tf_op jit(solution)/shard_map/ppermute | solution.py:450
  4.6 10.1 %collective-permute-start.1 = (bf16[32,16,256]{2,1,0:T(8,128)(2,1)S(1)}, bf16[32,16,256]{2,1,0:T(8,128)(2,1)S(1)}, u32[]{:S(2)}, u32[]{:S(2)}) collective-permute-start(bf16[32,16,256]{2,1,0:T(8,128)(2,1)S(1)} %get-tuple-element.48), channel_id=1, source_target_pairs={{0,32},{32,64},{64,96},{96,0},{1,33},{33,65},{65,97},{97,1},{2,34}... | collective-permute-start | bytes 786440 | tf_op jit(solution)/shard_map/ppermute | solution.py:450
  6.4 14.6 %collective-permute-start = (bf16[32,16,256]{2,1,0:T(8,128)(2,1)}, bf16[32,16,256]{2,1,0:T(8,128)(2,1)S(1)}, u32[]{:S(2)}, u32[]{:S(2)}) collective-permute-start(bf16[32,16,256]{2,1,0:T(8,128)(2,1)} %get-tuple-element.45), channel_id=1, source_target_pairs={{0,96},{32,0},{64,32},{96,64},{1,97},{33,1},{65,33},{97,65},{2,98}... | collective-permute-start | bytes 786440 | tf_op jit(solution)/shard_map/ppermute | solution.py:450
  9.6 13.3 %collective-permute-start.3 = (bf16[32,16,256]{2,1,0:T(8,128)(2,1)S(1)}, bf16[32,16,256]{2,1,0:T(8,128)(2,1)S(1)}, u32[]{:S(2)}, u32[]{:S(2)}) collective-permute-start(bf16[32,16,256]{2,1,0:T(8,128)(2,1)S(1)} %get-tuple-element.46), channel_id=1, source_target_pairs={{0,32},{32,64},{64,96},{96,0},{1,33},{33,65},{65,97},{97,1},{2,34}... | collective-permute-start | bytes 786440 | tf_op jit(solution)/shard_map/ppermute | solution.py:450
  11.2 14.8 %copy-start = (s32[64]{0:T(128)}, s32[64]{0:T(128)S(1)}, u32[]{:S(2)}) copy-start(s32[64]{0:T(128)S(1)} %multiply_add_fusion.place_ref) | copy-start | bytes 772
  12.6 13.4 %copy-start.2 = (s32[96]{0:T(128)}, s32[96]{0:T(128)S(1)}, u32[]{:S(2)}) copy-start(s32[96]{0:T(128)S(1)} %broadcast_subtract_fusion.empty_ref) | copy-start | bytes 1156
  14.8 11.2 %collective-permute-start.2 = (bf16[32,16,256]{2,1,0:T(8,128)(2,1)S(1)}, bf16[32,16,256]{2,1,0:T(8,128)(2,1)S(1)}, u32[]{:S(2)}, u32[]{:S(2)}) collective-permute-start(bf16[32,16,256]{2,1,0:T(8,128)(2,1)S(1)} %add.51), channel_id=1, source_target_pairs={{0,32},{32,64},{64,96},{96,0},{1,33},{33,65},{65,97},{97,1},{2,34}... | collective-permute-start | bytes 786440 | tf_op jit(solution)/shard_map/ppermute | solution.py:450
  15.0 11.0 %collective-permute-start.5 = (bf16[32,16,256]{2,1,0:T(8,128)(2,1)S(1)}, bf16[32,16,256]{2,1,0:T(8,128)(2,1)S(1)}, u32[]{:S(2)}, u32[]{:S(2)}) collective-permute-start(bf16[32,16,256]{2,1,0:T(8,128)(2,1)S(1)} %add.52), channel_id=1, source_target_pairs={{0,96},{32,0},{64,32},{96,64},{1,97},{33,1},{65,33},{97,65},{2,98}... | collective-permute-start | bytes 786440 | tf_op jit(solution)/shard_map/ppermute | solution.py:450
  20.0 16.1 %collective-permute-start.6 = (bf16[64,16,256]{2,1,0:T(8,128)(2,1)S(1)}, bf16[64,16,256]{2,1,0:T(8,128)(2,1)S(1)}, u32[]{:S(2)}, u32[]{:S(2)}) collective-permute-start(bf16[64,16,256]{2,1,0:T(8,128)(2,1)S(1)} %pad_maximum_fusion), channel_id=1, source_target_pairs={{0,96},{32,0},{64,32},{96,64},{1,97},{33,1},{65,33},{97,65},{2,98}... | collective-permute-start | bytes 1572872 | tf_op jit(solution)/shard_map/ppermute | solution.py:450
  21.0 15.1 %collective-permute-start.7 = (bf16[64,16,256]{2,1,0:T(8,128)(2,1)}, bf16[64,16,256]{2,1,0:T(8,128)(2,1)S(1)}, u32[]{:S(2)}, u32[]{:S(2)}) collective-permute-start(bf16[64,16,256]{2,1,0:T(8,128)(2,1)} %pad_maximum_fusion.1), channel_id=1, source_target_pairs={{0,32},{32,64},{64,96},{96,0},{1,33},{33,65},{65,97},{97,1},{2,34}... | collective-permute-start | bytes 1572872 | tf_op jit(solution)/shard_map/ppermute | solution.py:450
  27.6 23.0 %all-to-all-start = ((bf16[32,3,16,256]{3,2,1,0:T(8,128)(2,1)}), bf16[32,3,16,256]{3,2,1,0:T(8,128)(2,1)}, u32[]{:S(2)}, u32[]{:S(2)}) async-start(bf16[32,3,16,256]{3,2,1,0:T(8,128)(2,1)} %bitcast.4), calls=%async_computation | async-start | bytes 1572864 | tf_op jit(solution)/shard_map/all_to_all | solution.py:484
  36.1 9.8 %copy-start.1 = (s32[64]{0:T(128)S(1)}, s32[64]{0:T(128)}, u32[]{:S(2)}) copy-start(s32[64]{0:T(128)} %copy-done) | copy-start | bytes 772
  36.1 9.8 %copy-start.3 = (s32[96]{0:T(128)S(1)}, s32[96]{0:T(128)}, u32[]{:S(2)}) copy-start(s32[96]{0:T(128)} %copy-done.2) | copy-start | bytes 1156
  36.2 9.7 %collective-permute-start.8 = (bf16[32,16,256]{2,1,0:T(8,128)(2,1)S(1)}, bf16[32,16,256]{2,1,0:T(8,128)(2,1)S(1)}, u32[]{:S(2)}, u32[]{:S(2)}) collective-permute-start(bf16[32,16,256]{2,1,0:T(8,128)(2,1)S(1)} %get-tuple-element.25), channel_id=1, source_target_pairs={{0,32},{32,64},{64,96},{96,0},{1,33},{33,65},{65,97},{97,1},{2,34}... | collective-permute-start | bytes 786440 | tf_op jit(solution)/shard_map/ppermute | solution.py:450
  36.3 9.6 %collective-permute-start.9 = (bf16[32,16,256]{2,1,0:T(8,128)(2,1)S(1)}, bf16[32,16,256]{2,1,0:T(8,128)(2,1)S(1)}, u32[]{:S(2)}, u32[]{:S(2)}) collective-permute-start(bf16[32,16,256]{2,1,0:T(8,128)(2,1)S(1)} %get-tuple-element.26), channel_id=1, source_target_pairs={{0,96},{32,0},{64,32},{96,64},{1,97},{33,1},{65,33},{97,65},{2,98}... | collective-permute-start | bytes 786440 | tf_op jit(solution)/shard_map/ppermute | solution.py:450
  50.6 18.8 %all-to-all-start.1 = ((bf16[32,3,16,256]{3,2,1,0:T(8,128)(2,1)}), bf16[32,3,16,256]{3,2,1,0:T(8,128)(2,1)S(1)}, u32[]{:S(2)}, u32[]{:S(2)}) async-start(bf16[32,3,16,256]{3,2,1,0:T(8,128)(2,1)} %bitcast.5), calls=%async_computation.1 | async-start | bytes 1572864 | tf_op jit(solution)/shard_map/all_to_all | solution.py:484
  78.1 27.9 %all-to-all-start.2 = ((bf16[32,3,16,512]{3,2,1,0:T(8,128)(2,1)}), bf16[32,3,16,512]{3,2,1,0:T(8,128)(2,1)S(1)}, u32[]{:S(2)}, u32[]{:S(2)}) async-start(bf16[32,3,16,512]{3,2,1,0:T(8,128)(2,1)} %precondition.1), calls=%async_computation.2 | async-start | bytes 3145728 | tf_op jit(solution)/shard_map/all_to_all | solution.py:492

commit v7 on v6

--- a/solution.py
+++ b/solution.py
@@ -98,12 +98,11 @@
     half = own_front.shape[0]
     zeros[...] = jnp.zeros_like(zeros)
 
-    def blank(place, carry):
-        @pl.when(empty_ref[place] > 0)
-        def _():
-            pltpu.make_async_copy(zeros, out_ref.at[place], sem).start()
-
+    def blank(number, carry):
+        pltpu.make_async_copy(zeros, out_ref.at[empty_ref[number]], sem).start()
         return carry
+
+    lax.fori_loop(0, empty_ref.shape[0], blank, 0, unroll=8)
 
     def add(j, carry):
         for block, own, straight, last in (
@@ -116,7 +115,6 @@
         return carry
 
     lax.fori_loop(0, half, add, 0, unroll=4)
-    lax.fori_loop(0, out_ref.shape[0], blank, 0, unroll=4)
     pltpu.make_async_copy(out_ref, out_ref, sem).wait()
 
 
@@ -125,7 +123,7 @@
     scalars = pl.BlockSpec(memory_space=SMEM)
     return pl.pallas_call(
         place_kernel,
-        out_shape=jax.ShapeDtypeStruct((empty.shape[0], rows, cols), jnp.bfloat16),
+        out_shape=jax.ShapeDtypeStruct((2 * half + empty.shape[0], rows, cols), jnp.bfloat16),
         in_specs=[scalars] * 2 + [pl.BlockSpec(memory_space=VMEM)] * 6,
         out_specs=pl.BlockSpec(memory_space=HBM),
         scratch_shapes=[
@@ -418,7 +416,12 @@
     slot = jnp.sum((same & (ids[None, :] < ids[:, None])).astype(jnp.int32), axis=1)
     place = owner * MOST + slot
     taken = place[None, :] == jnp.arange(owners * MOST, dtype=jnp.int32)[:, None]
-    return place, 1 - jnp.sum(taken.astype(jnp.int32), axis=1)
+    spots = jnp.arange(owners * MOST, dtype=jnp.int32)
+    free = 1 - jnp.sum(taken.astype(jnp.int32), axis=1)
+    before = jnp.sum(jnp.where(spots[None, :] < spots[:, None], free[None, :], 0), axis=1)
+    numbers = jnp.arange(owners * MOST - owner.shape[0], dtype=jnp.int32)
+    listed = (before[None, :] == numbers[:, None]) & (free[None, :] > 0)
+    return place, jnp.sum(jnp.where(listed, spots[None, :], 0), axis=1)
 
 
 def on_device(grads, owner_table, left_stats, right_stats, left_roots, right_roots):
@@ -475,9 +478,11 @@
     both = tuple(jnp.concatenate(pair) for pair in pairs)
     up12, down12 = send(both)
     outgoing_a = place_blocks(place, empty, (own[0], down2, up3), (own[1], up2, down3), 30)
-    own, mid = owns(later, parts[1]), mids(later, parts[1])
+    mid = mids(later, parts[1])
     third = add_pairs(mid[0], up12, mid[1], down12, outgoing_a)
     up3, down3 = send(third)
+    later, _ = lax.optimization_barrier((later, third))
+    own = owns(later, parts[1])
     outgoing_b = place_blocks(place, empty, (own[0], down12, up3), (own[1], up12, down3))
     spare = spare_room((owners, MOST, slab_rows, side))
     arrived = [

time: 108 us -> 108 us (level)
  waiting for transfers between devices: 41.2 us -> 39.8 us
  starting transfers between devices: 31.7 us -> 32.8 us
    ppermute x5, starting transfers between devices: 12.8 us -> 15.9 us  [send(): lax.ppermute(pair[1], 'rep', down)]
    ppermute x5, starting transfers between devices: 2.15 us -> 0.23 us  [send(): lax.ppermute(pair[0], 'rep', up)]
    ppermute x5, waiting for transfers between devices: 11.5 us -> 10 us  [send(): lax.ppermute(pair[0], 'rep', up)]
    dynamic_slice x4 -> x5, local copies, waits for them, and re-layouts: 5.83 us -> 6.61 us  [part(): lax.dynamic_slice(source, (start, 0, columns[0]), (half, slab_rows, colum...]
  transfers between devices with their start and end apart: 13 -> 13, of which waited for: 6 -> 7; matrix products, arithmetic and copies ran while one was open for 8% -> 8% of each run, Pallas kernels for 13% -> 13%
where the time goes in v7:
time: 108 us; the launch traced here: 107 us
  waiting for transfers between devices  39.8 us (37%)
  starting transfers between devices  32.8 us (30%)
  Pallas kernels  24.3 us (22%)
  local copies, waits for them, and re-layouts  6.63 us (6%)
  other arithmetic  2.77 us (3%)
    all_to_all x2, waiting for transfers between devices, on_device(): lax.all_to_all(outgoing.reshape(owners, MOST, slab_rows, -1), 'fsdp', spl...  17.1 us
    ppermute x5, starting transfers between devices, send(): lax.ppermute(pair[1], 'rep', down)  15.9 us
    all_to_all x1, waiting for transfers between devices, on_device(): lax.all_to_all(results, 'fsdp', split_axis=0, concat_axis=0, tiled=True)  12.7 us
    all_to_all x2, starting transfers between devices, on_device(): lax.all_to_all(outgoing.reshape(owners, MOST, slab_rows, -1), 'fsdp', spl...  12.5 us
    pallas_call x1, Pallas kernels, update_stats(): pl.pallas_call(stats_kernel, grid=(MOST,), out_shape=[shape, shape, root,...  11 us
    ppermute x5, waiting for transfers between devices, send(): lax.ppermute(pair[0], 'rep', up)  10 us
    pallas_call x1, Pallas kernels, precondition(): pl.pallas_call(precondition_kernel, out_shape=jax.ShapeDtypeStruct((owner...  8.74 us
    dynamic_slice x5, local copies, waits for them, and re-layouts, part(): lax.dynamic_slice(source, (start, 0, columns[0]), (half, slab_rows, colum...  6.61 us
  transfers between devices with their start and end apart: 13, of which 7 were waited for; matrix products, arithmetic and copies ran while one was open for 8% of the time, Pallas kernels for 13%

profile of v7, /device:TPU:0, one launch (start us, length us, event | category | flops | bytes accessed | tf_op | source)
XLA Modules:
  0.0 107.4 jit_solution(6726094295586779479)
XLA Ops:
  0.6 1.1 dynamic-slice_bitcast_fusion
  1.7 2.9 %collective-permute-start.4 = (bf16[32,16,256]{2,1,0:T(8,128)(2,1)S(1)}, bf16[32,16,256]{2,1,0:T(8,128)(2,1)S(1)}, u32[]{:S(2)}, u32[]{:S(2)}) collective-permute-start(bf16[32,16,256]{2,1,0:T(8,128)(2,1)S(1)} %get-tuple-element.49), channel_id=1, source_target_pairs={{0,96},{32,0},{64,32},{96,64},{1,97},{33,1},{65,33},{97,65},{2,98}... | collective-permute-start | bytes 786440 | tf_op jit(solution)/shard_map/ppermute | solution.py:453
  4.6 1.8 %constant_dynamic-slice_fusion.10 = (bf16[32,16,256]{2,1,0:T(8,128)(2,1)}, bf16[32,16,256]{2,1,0:T(8,128)(2,1)S(1)}) fusion(bf16[256,16,512]{2,1,0:T(8,128)(2,1)} %bitcast.12, s32[]{:T(128)S(6)} %mul.42, s32[]{:T(128)S(6)} %add.47), kind=kLoop, calls=%fused_computation.24 | loop fusion | bytes 1048584 | tf_op jit(solution)/shard_map/dynamic_slice | solution.py:448
  6.4 3.2 %collective-permute-start = (bf16[32,16,256]{2,1,0:T(8,128)(2,1)}, bf16[32,16,256]{2,1,0:T(8,128)(2,1)S(1)}, u32[]{:S(2)}, u32[]{:S(2)}) collective-permute-start(bf16[32,16,256]{2,1,0:T(8,128)(2,1)} %get-tuple-element.47), channel_id=1, source_target_pairs={{0,96},{32,0},{64,32},{96,64},{1,97},{33,1},{65,33},{97,65},{2,98}... | collective-permute-start | bytes 786440 | tf_op jit(solution)/shard_map/ppermute | solution.py:453
  9.6 1.4 %fusion.2 = (s32[]{:T(128)}, s32[64]{0:T(128)S(1)}) fusion(s32[]{:T(128)S(6)} %axis_index.25, s32[256,1]{0,1:T(1,128)} %param.7, s32[]{:T(128)S(6)} %mul.18), kind=kLoop, calls=%fused_computation.31 | loop fusion | flops 191 | bytes 524 | tf_op jit(solution)/shard_map/reduce_sum | solution.py:441
  11.0 0.2 convert_reduce_fusion.1
  11.2 0.1 convert_reduce_fusion
  11.3 1.3 %constant_dynamic-slice_fusion.6 = (bf16[32,16,256]{2,1,0:T(8,128)(2,1)S(1)}, bf16[32,16,256]{2,1,0:T(8,128)(2,1)S(1)}, bf16[32,16,256]{2,1,0:T(8,128)(2,1)S(1)}, bf16[32,16,256]{2,1,0:T(8,128)(2,1)S(1)}) fusion(bf16[256,16,512]{2,1,0:T(8,128)(2,1)} %bitcast.13, s32[]{:T(128)S(6)} %add.50, s32[]{:T(128)S(6)} %mul.41, s32[]{:T(128)S(6)} %add.49, s32[]{:T(128)S(6)} %mul.43), kind=kLoop, calls=%fused_computation.20 | loop fusion | bytes 2097168 | tf_op jit(solution)/shard_map/dynamic_slice | solution.py:448
  12.6 0.1 select_reduce_fusion
  12.7 0.1 select_reduce_fusion.1.empty_ref
  12.8 1.9 %collective-permute-done.1 = bf16[32,16,256]{2,1,0:T(8,128)(2,1)S(1)} collective-permute-done((bf16[32,16,256]{2,1,0:T(8,128)(2,1)S(1)}, bf16[32,16,256]{2,1,0:T(8,128)(2,1)S(1)}, u32[]{:S(2)}, u32[]{:S(2)}) %collective-permute-start.1) | collective-permute-done | bytes 262176 | tf_op jit(solution)/shard_map/ppermute | solution.py:453
  14.9 0.1 add.52
  15.0 3.3 %collective-permute-start.5 = (bf16[32,16,256]{2,1,0:T(8,128)(2,1)S(1)}, bf16[32,16,256]{2,1,0:T(8,128)(2,1)S(1)}, u32[]{:S(2)}, u32[]{:S(2)}) collective-permute-start(bf16[32,16,256]{2,1,0:T(8,128)(2,1)S(1)} %add.52), channel_id=1, source_target_pairs={{0,96},{32,0},{64,32},{96,64},{1,97},{33,1},{65,33},{97,65},{2,98}... | collective-permute-start | bytes 786440 | tf_op jit(solution)/shard_map/ppermute | solution.py:453
  18.2 1.4 %constant_dynamic-slice_fusion.1 = (bf16[32,16,256]{2,1,0:T(8,128)(2,1)S(1)}, bf16[32,16,256]{2,1,0:T(8,128)(2,1)S(1)}, bf16[32,16,256]{2,1,0:T(8,128)(2,1)S(1)}...) fusion(bf16[256,16,512]{2,1,0:T(8,128)(2,1)} %bitcast.14, ...), kind=kLoop, calls=%fused_computation.15 | loop fusion | bytes 3145752 | tf_op jit(solution)/shard_map/dynamic_slice | solution.py:448
  19.9 3.3 %collective-permute-start.7 = (bf16[64,16,256]{2,1,0:T(8,128)(2,1)S(1)}, bf16[64,16,256]{2,1,0:T(8,128)(2,1)S(1)}, u32[]{:S(2)}, u32[]{:S(2)}) collective-permute-start(bf16[64,16,256]{2,1,0:T(8,128)(2,1)S(1)} %pad_maximum_fusion.1), channel_id=1, source_target_pairs={{0,96},{32,0},{64,32},{96,64},{1,97},{33,1},{65,33},{97,65},{2,98}... | collective-permute-start | bytes 1572872 | tf_op jit(solution)/shard_map/ppermute | solution.py:453
  23.2 2.8 %collective-permute-done.2.rest_2_ = bf16[32,16,256]{2,1,0:T(8,128)(2,1)S(1)} collective-permute-done((bf16[32,16,256]{2,1,0:T(8,128)(2,1)S(1)}, bf16[32,16,256]{2,1,0:T(8,128)(2,1)S(1)}, u32[]{:S(2)}, u32[]{:S(2)}) %collective-permute-start.2) | collective-permute-done | bytes 262176 | tf_op jit(solution)/shard_map/ppermute | solution.py:453
  25.9 1.5 %place_blocks.2.rest_0_ = bf16[96,16,256]{2,1,0:T(8,128)(2,1)} custom-call(s32[64]{0:T(128)S(1)} %multiply_add_fusion.place_ref, s32[32]{0:T(128)S(1)} %select_reduce_fusion.1.empty_ref, bf16[32,16,256]{2,1,0:T(8,128)(2,1)S(1)} %get-tuple-element.21.rest_0_, bf16[32,16,256]{2,1,0:T(8,128)(2,1)S(1)} %collective-permute-done.rest_1_, ...), custom_call_target="tpu_custom_call" | custom-call | flops 8053063680 | bytes 2097152 | tf_op jit(solution)/shard_map/place_blocks/pallas_call | solution.py:124
  27.5 8.5 %all-to-all-start = ((bf16[32,3,16,256]{3,2,1,0:T(8,128)(2,1)}), bf16[32,3,16,256]{3,2,1,0:T(8,128)(2,1)}, u32[]{:S(2)}, u32[]{:S(2)}) async-start(bf16[32,3,16,256]{3,2,1,0:T(8,128)(2,1)} %bitcast.4), calls=%async_computation | async-start | bytes 1572864 | tf_op jit(solution)/shard_map/all_to_all | solution.py:489
  35.9 0.1 collective-permute-done.6.two_ref.rest_4_
  36.2 3.2 %collective-permute-start.9 = (bf16[32,16,256]{2,1,0:T(8,128)(2,1)S(1)}, bf16[32,16,256]{2,1,0:T(8,128)(2,1)S(1)}, u32[]{:S(2)}, u32[]{:S(2)}) collective-permute-start(bf16[32,16,256]{2,1,0:T(8,128)(2,1)S(1)} %get-tuple-element.27), channel_id=1, source_target_pairs={{0,96},{32,0},{64,32},{96,64},{1,97},{33,1},{65,33},{97,65},{2,98}... | collective-permute-start | bytes 786440 | tf_op jit(solution)/shard_map/ppermute | solution.py:453
  39.5 1.1 constant_dynamic-slice_fusion.13
  40.5 5.2 %collective-permute-done.8.rest_2_ = bf16[32,16,256]{2,1,0:T(8,128)(2,1)S(1)} collective-permute-done((bf16[32,16,256]{2,1,0:T(8,128)(2,1)S(1)}, bf16[32,16,256]{2,1,0:T(8,128)(2,1)S(1)}, u32[]{:S(2)}, u32[]{:S(2)}) %collective-permute-start.8) | collective-permute-done | bytes 262176 | tf_op jit(solution)/shard_map/ppermute | solution.py:453
  45.7 1.5 %place_blocks.3 = bf16[96,16,256]{2,1,0:T(8,128)(2,1)} custom-call(s32[64]{0:T(128)S(1)} %multiply_add_fusion.place_ref, s32[32]{0:T(128)S(1)} %copy-done.3, bf16[32,16,256]{2,1,0:T(8,128)(2,1)S(1)} %get-tuple-element.36.rest_0_, bf16[64,16,256]{2,1,0:T(8,128)(2,1)S(1)} %collective-permute-done.7.four_ref.rest_1_, ...), custom_call_target="tpu_custom_call" | custom-call | bytes 2097152 | tf_op jit(solution)/shard_map/place_blocks/pallas_call | solution.py:124
  47.3 3.2 %all-to-all-done.arrived_a.front_ref = bf16[32,3,16,256]{3,2,1,0:T(8,128)(2,1)} async-done(((bf16[32,3,16,256]{3,2,1,0:T(8,128)(2,1)}), bf16[32,3,16,256]{3,2,1,0:T(8,128)(2,1)}, u32[]{:S(2)}, u32[]{:S(2)}) %all-to-all-start) | async-done | bytes 786464 | tf_op jit(solution)/shard_map/all_to_all | solution.py:489
  50.5 4.1 %all-to-all-start.1 = ((bf16[32,3,16,256]{3,2,1,0:T(8,128)(2,1)}), bf16[32,3,16,256]{3,2,1,0:T(8,128)(2,1)S(1)}, u32[]{:S(2)}, u32[]{:S(2)}) async-start(bf16[32,3,16,256]{3,2,1,0:T(8,128)(2,1)} %bitcast.5), calls=%async_computation.1 | async-start | bytes 1572864 | tf_op jit(solution)/shard_map/all_to_all | solution.py:489
  54.6 0.7 compare_convert_fusion.live_ref
  55.2 13.9 %all-to-all-done.1.arrived_b.back_ref = bf16[32,3,16,256]{3,2,1,0:T(8,128)(2,1)S(1)} async-done(((bf16[32,3,16,256]{3,2,1,0:T(8,128)(2,1)}), bf16[32,3,16,256]{3,2,1,0:T(8,128)(2,1)S(1)}, u32[]{:S(2)}, u32[]{:S(2)}) %all-to-all-start.1) | async-done | bytes 786464 | tf_op jit(solution)/shard_map/all_to_all | solution.py:489
  69.1 8.7 %precondition.1 = bf16[32,3,16,512]{3,2,1,0:T(8,128)(2,1)} custom-call(s32[3]{0:T(128)S(1)} %compare_convert_fusion.live_ref, bf16[32,3,16,256]{3,2,1,0:T(8,128)(2,1)} %all-to-all-done.arrived_a.front_ref, bf16[32,3,16,256]{3,2,1,0:T(8,128)(2,1)S(1)} %all-to-all-done.1.arrived_b.back_ref, ...), custom_call_target="tpu_custom_call", output_to_operand_aliasing={{}: (7, {})} | custom-call | flops 3758096384 | bytes 9437184 | tf_op jit(solution)/shard_map/precondition/pallas_call | solution.py:309
  77.9 4.2 %all-to-all-start.2 = ((bf16[32,3,16,512]{3,2,1,0:T(8,128)(2,1)}), bf16[32,3,16,512]{3,2,1,0:T(8,128)(2,1)S(1)}, u32[]{:S(2)}, u32[]{:S(2)}) async-start(bf16[32,3,16,512]{3,2,1,0:T(8,128)(2,1)} %precondition.1), calls=%async_computation.2 | async-start | bytes 3145728 | tf_op jit(solution)/shard_map/all_to_all | solution.py:497
  82.0 11.0 %update_stats.1 = (f32[1,1,3,512,512]{4,3,2,1,0:T(8,128)}, f32[1,1,3,512,512]{4,3,2,1,0:T(8,128)}, bf16[1,1,512,512]{3,2,1,0:T(8,128)(2,1)}, bf16[1,1,512,512]{3,2,1,0:T(8,128)(2,1)}) custom-call(s32[3]{0:T(128)S(1)} %compare_convert_fusion.live_ref, bf16[32,3,16,256]{3,2,1,0:T(8,128)(2,1)} %all-to-all-done.arrived_a.front_ref, ...), custom_call_target="tpu_custom_call" | custom-call | flops 3221225472 | bytes 13631488 | tf_op jit(solution)/shard_map/update_stats/pallas_call | solution.py:365
  93.1 12.7 %all-to-all-done.2 = bf16[32,3,16,512]{3,2,1,0:T(8,128)(2,1)S(1)} async-done(((bf16[32,3,16,512]{3,2,1,0:T(8,128)(2,1)}), bf16[32,3,16,512]{3,2,1,0:T(8,128)(2,1)S(1)}, u32[]{:S(2)}, u32[]{:S(2)}) %all-to-all-start.2) | async-done | bytes 1572896 | tf_op jit(solution)/shard_map/all_to_all | solution.py:497
  105.8 1.5 %assemble.1 = bf16[64,16,512]{2,1,0:T(8,128)(2,1)} custom-call(s32[64]{0:T(128)S(1)} %copy-done.1, bf16[96,16,512]{2,1,0:T(8,128)(2,1)S(1)} %bitcast.11), custom_call_target="tpu_custom_call" | custom-call | bytes 2097152 | tf_op jit(solution)/shard_map/assemble/pallas_call | solution.py:401
  (27 shorter events, 0.5 us)
Async XLA Ops:
  1.7 13.2 %collective-permute-start.4 = (bf16[32,16,256]{2,1,0:T(8,128)(2,1)S(1)}, bf16[32,16,256]{2,1,0:T(8,128)(2,1)S(1)}, u32[]{:S(2)}, u32[]{:S(2)}) collective-permute-start(bf16[32,16,256]{2,1,0:T(8,128)(2,1)S(1)} %get-tuple-element.49), channel_id=1, source_target_pairs={{0,96},{32,0},{64,32},{96,64},{1,97},{33,1},{65,33},{97,65},{2,98}... | collective-permute-start | bytes 786440 | tf_op jit(solution)/shard_map/ppermute | solution.py:453
  4.6 10.1 %collective-permute-start.1 = (bf16[32,16,256]{2,1,0:T(8,128)(2,1)S(1)}, bf16[32,16,256]{2,1,0:T(8,128)(2,1)S(1)}, u32[]{:S(2)}, u32[]{:S(2)}) collective-permute-start(bf16[32,16,256]{2,1,0:T(8,128)(2,1)S(1)} %get-tuple-element.50), channel_id=1, source_target_pairs={{0,32},{32,64},{64,96},{96,0},{1,33},{33,65},{65,97},{97,1},{2,34}... | collective-permute-start | bytes 786440 | tf_op jit(solution)/shard_map/ppermute | solution.py:453
  6.4 13.5 %collective-permute-start = (bf16[32,16,256]{2,1,0:T(8,128)(2,1)}, bf16[32,16,256]{2,1,0:T(8,128)(2,1)S(1)}, u32[]{:S(2)}, u32[]{:S(2)}) collective-permute-start(bf16[32,16,256]{2,1,0:T(8,128)(2,1)} %get-tuple-element.47), channel_id=1, source_target_pairs={{0,96},{32,0},{64,32},{96,64},{1,97},{33,1},{65,33},{97,65},{2,98}... | collective-permute-start | bytes 786440 | tf_op jit(solution)/shard_map/ppermute | solution.py:453
  9.6 13.6 %collective-permute-start.3 = (bf16[32,16,256]{2,1,0:T(8,128)(2,1)S(1)}, bf16[32,16,256]{2,1,0:T(8,128)(2,1)S(1)}, u32[]{:S(2)}, u32[]{:S(2)}) collective-permute-start(bf16[32,16,256]{2,1,0:T(8,128)(2,1)S(1)} %get-tuple-element.48), channel_id=1, source_target_pairs={{0,32},{32,64},{64,96},{96,0},{1,33},{33,65},{65,97},{97,1},{2,34}... | collective-permute-start | bytes 786440 | tf_op jit(solution)/shard_map/ppermute | solution.py:453
  11.2 34.6 %copy-start = (s32[64]{0:T(128)}, s32[64]{0:T(128)S(1)}, u32[]{:S(2)}) copy-start(s32[64]{0:T(128)S(1)} %multiply_add_fusion.place_ref) | copy-start | bytes 772
  12.8 13.1 %copy-start.2 = (s32[32]{0:T(128)}, s32[32]{0:T(128)S(1)}, u32[]{:S(2)}) copy-start(s32[32]{0:T(128)S(1)} %select_reduce_fusion.1.empty_ref) | copy-start | bytes 388
  14.8 11.2 %collective-permute-start.2 = (bf16[32,16,256]{2,1,0:T(8,128)(2,1)S(1)}, bf16[32,16,256]{2,1,0:T(8,128)(2,1)S(1)}, u32[]{:S(2)}, u32[]{:S(2)}) collective-permute-start(bf16[32,16,256]{2,1,0:T(8,128)(2,1)S(1)} %add.51), channel_id=1, source_target_pairs={{0,32},{32,64},{64,96},{96,0},{1,33},{33,65},{65,97},{97,1},{2,34}... | collective-permute-start | bytes 786440 | tf_op jit(solution)/shard_map/ppermute | solution.py:453
  15.0 11.0 %collective-permute-start.5 = (bf16[32,16,256]{2,1,0:T(8,128)(2,1)S(1)}, bf16[32,16,256]{2,1,0:T(8,128)(2,1)S(1)}, u32[]{:S(2)}, u32[]{:S(2)}) collective-permute-start(bf16[32,16,256]{2,1,0:T(8,128)(2,1)S(1)} %add.52), channel_id=1, source_target_pairs={{0,96},{32,0},{64,32},{96,64},{1,97},{33,1},{65,33},{97,65},{2,98}... | collective-permute-start | bytes 786440 | tf_op jit(solution)/shard_map/ppermute | solution.py:453
  19.8 16.3 %collective-permute-start.6 = (bf16[64,16,256]{2,1,0:T(8,128)(2,1)S(1)}, bf16[64,16,256]{2,1,0:T(8,128)(2,1)S(1)}, u32[]{:S(2)}, u32[]{:S(2)}) collective-permute-start(bf16[64,16,256]{2,1,0:T(8,128)(2,1)S(1)} %pad_maximum_fusion), channel_id=1, source_target_pairs={{0,32},{32,64},{64,96},{96,0},{1,33},{33,65},{65,97},{97,1},{2,34}... | collective-permute-start | bytes 1572872 | tf_op jit(solution)/shard_map/ppermute | solution.py:453
  19.9 16.2 %collective-permute-start.7 = (bf16[64,16,256]{2,1,0:T(8,128)(2,1)S(1)}, bf16[64,16,256]{2,1,0:T(8,128)(2,1)S(1)}, u32[]{:S(2)}, u32[]{:S(2)}) collective-permute-start(bf16[64,16,256]{2,1,0:T(8,128)(2,1)S(1)} %pad_maximum_fusion.1), channel_id=1, source_target_pairs={{0,96},{32,0},{64,32},{96,64},{1,97},{33,1},{65,33},{97,65},{2,98}... | collective-permute-start | bytes 1572872 | tf_op jit(solution)/shard_map/ppermute | solution.py:453
  27.5 23.0 %all-to-all-start = ((bf16[32,3,16,256]{3,2,1,0:T(8,128)(2,1)}), bf16[32,3,16,256]{3,2,1,0:T(8,128)(2,1)}, u32[]{:S(2)}, u32[]{:S(2)}) async-start(bf16[32,3,16,256]{3,2,1,0:T(8,128)(2,1)} %bitcast.4), calls=%async_computation | async-start | bytes 1572864 | tf_op jit(solution)/shard_map/all_to_all | solution.py:489
  36.1 9.7 %copy-start.3 = (s32[32]{0:T(128)S(1)}, s32[32]{0:T(128)}, u32[]{:S(2)}) copy-start(s32[32]{0:T(128)} %copy-done.2) | copy-start | bytes 388
  36.1 9.6 %collective-permute-start.8 = (bf16[32,16,256]{2,1,0:T(8,128)(2,1)S(1)}, bf16[32,16,256]{2,1,0:T(8,128)(2,1)S(1)}, u32[]{:S(2)}, u32[]{:S(2)}) collective-permute-start(bf16[32,16,256]{2,1,0:T(8,128)(2,1)S(1)} %get-tuple-element.26), channel_id=1, source_target_pairs={{0,32},{32,64},{64,96},{96,0},{1,33},{33,65},{65,97},{97,1},{2,34}... | collective-permute-start | bytes 786440 | tf_op jit(solution)/shard_map/ppermute | solution.py:453
  36.2 9.5 %collective-permute-start.9 = (bf16[32,16,256]{2,1,0:T(8,128)(2,1)S(1)}, bf16[32,16,256]{2,1,0:T(8,128)(2,1)S(1)}, u32[]{:S(2)}, u32[]{:S(2)}) collective-permute-start(bf16[32,16,256]{2,1,0:T(8,128)(2,1)S(1)} %get-tuple-element.27), channel_id=1, source_target_pairs={{0,96},{32,0},{64,32},{96,64},{1,97},{33,1},{65,33},{97,65},{2,98}... | collective-permute-start | bytes 786440 | tf_op jit(solution)/shard_map/ppermute | solution.py:453
  50.5 18.6 %all-to-all-start.1 = ((bf16[32,3,16,256]{3,2,1,0:T(8,128)(2,1)}), bf16[32,3,16,256]{3,2,1,0:T(8,128)(2,1)S(1)}, u32[]{:S(2)}, u32[]{:S(2)}) async-start(bf16[32,3,16,256]{3,2,1,0:T(8,128)(2,1)} %bitcast.5), calls=%async_computation.1 | async-start | bytes 1572864 | tf_op jit(solution)/shard_map/all_to_all | solution.py:489
  77.9 27.9 %all-to-all-start.2 = ((bf16[32,3,16,512]{3,2,1,0:T(8,128)(2,1)}), bf16[32,3,16,512]{3,2,1,0:T(8,128)(2,1)S(1)}, u32[]{:S(2)}, u32[]{:S(2)}) async-start(bf16[32,3,16,512]{3,2,1,0:T(8,128)(2,1)} %precondition.1), calls=%async_computation.2 | async-start | bytes 3145728 | tf_op jit(solution)/shard_map/all_to_all | solution.py:497
  82.0 23.8 %copy-start.1 = (s32[64]{0:T(128)S(1)}, s32[64]{0:T(128)}, u32[]{:S(2)}) copy-start(s32[64]{0:T(128)} %copy-done) | copy-start | bytes 772

commit v8 on v6

--- a/solution.py
+++ b/solution.py
@@ -57,13 +57,12 @@
 
 def product(left, right, use):
     side = left.shape[0]
-    for row in range(0, side, PIECE):
-        for col in range(0, side, PIECE):
-            piece = mul(left[row : row + PIECE, :], right[:, col : col + PIECE])
-            for r in range(0, PIECE, ROWS):
-                for c in range(0, PIECE, COLS):
-                    rows, cols = slice(row + r, row + r + ROWS), slice(col + c, col + c + COLS)
-                    use(piece[r : r + ROWS, c : c + COLS], rows, cols)
+    for col in range(0, side, PIECE):
+        piece = mul(left[:, :], right[:, col : col + PIECE])
+        for row in range(0, side, ROWS):
+            for c in range(0, PIECE, COLS):
+                rows, cols = slice(row, row + ROWS), slice(col + c, col + c + COLS)
+                use(piece[row : row + ROWS, c : c + COLS], rows, cols)
 
 
 def plus_diag(tile, rows, cols, value):

time: 108 us -> 108 us (level)
  no operation moved by 1% of the time
where the time goes in v8:
time: 108 us
  waiting for transfers between devices  41.3 us (38%)
  starting transfers between devices  31.7 us (29%)
  Pallas kernels  24.4 us (23%)
  local copies, waits for them, and re-layouts  5.85 us (5%)
  other arithmetic  3.33 us (3%)
    all_to_all x2, waiting for transfers between devices, on_device(): lax.all_to_all(outgoing.reshape(owners, MOST, slab_rows, -1), 'fsdp', spl...  17 us
    all_to_all x1, waiting for transfers between devices, on_device(): lax.all_to_all(results, 'fsdp', split_axis=0, concat_axis=0, tiled=True)  12.8 us
    ppermute x5, starting transfers between devices, send(): lax.ppermute(pair[1], 'rep', down)  12.8 us
    all_to_all x2, starting transfers between devices, on_device(): lax.all_to_all(outgoing.reshape(owners, MOST, slab_rows, -1), 'fsdp', spl...  12.7 us
    ppermute x5, waiting for transfers between devices, send(): lax.ppermute(pair[0], 'rep', up)  11.5 us
    pallas_call x1, Pallas kernels, update_stats(): pl.pallas_call(stats_kernel, grid=(MOST,), out_shape=[shape, shape, root,...  11 us
    pallas_call x1, Pallas kernels, precondition(): pl.pallas_call(precondition_kernel, out_shape=jax.ShapeDtypeStruct((owner...  8.64 us
    dynamic_slice x4, local copies, waits for them, and re-layouts, part(): lax.dynamic_slice(source, (start, 0, columns[0]), (half, slab_rows, colum...  5.83 us
  transfers between devices with their start and end apart: 13, of which 6 were waited for; matrix products, arithmetic and copies ran while one was open for 8% of the time, Pallas kernels for 13%

profile of v8, /device:TPU:0, one launch (start us, length us, event | category | flops | bytes accessed | tf_op | source)
XLA Modules:
  0.0 107.6 jit_solution(12931089358871188604)
XLA Ops:
  0.6 1.1 dynamic-slice_bitcast_fusion
  1.7 2.9 %collective-permute-start.4 = (bf16[32,16,256]{2,1,0:T(8,128)(2,1)S(1)}, bf16[32,16,256]{2,1,0:T(8,128)(2,1)S(1)}, u32[]{:S(2)}, u32[]{:S(2)}) collective-permute-start(bf16[32,16,256]{2,1,0:T(8,128)(2,1)S(1)} %get-tuple-element.47), channel_id=1, source_target_pairs={{0,96},{32,0},{64,32},{96,64},{1,97},{33,1},{65,33},{97,65},{2,98}... | collective-permute-start | bytes 786440 | tf_op jit(solution)/shard_map/ppermute | solution.py:449
  4.6 1.8 %constant_dynamic-slice_fusion.12 = (bf16[32,16,256]{2,1,0:T(8,128)(2,1)}, bf16[32,16,256]{2,1,0:T(8,128)(2,1)S(1)}) fusion(bf16[256,16,512]{2,1,0:T(8,128)(2,1)} %bitcast.12, s32[]{:T(128)S(6)} %mul.42, s32[]{:T(128)S(6)} %add.47), kind=kLoop, calls=%fused_computation.21 | loop fusion | bytes 1048584 | tf_op jit(solution)/shard_map/dynamic_slice | solution.py:444
  6.4 3.2 %collective-permute-start = (bf16[32,16,256]{2,1,0:T(8,128)(2,1)}, bf16[32,16,256]{2,1,0:T(8,128)(2,1)S(1)}, u32[]{:S(2)}, u32[]{:S(2)}) collective-permute-start(bf16[32,16,256]{2,1,0:T(8,128)(2,1)} %get-tuple-element.45), channel_id=1, source_target_pairs={{0,96},{32,0},{64,32},{96,64},{1,97},{33,1},{65,33},{97,65},{2,98}... | collective-permute-start | bytes 786440 | tf_op jit(solution)/shard_map/ppermute | solution.py:449
  9.6 1.4 %fusion.1 = (s32[]{:T(128)}, s32[64]{0:T(128)S(1)}) fusion(s32[]{:T(128)S(6)} %axis_index.25, s32[256,1]{0,1:T(1,128)} %param.7, s32[]{:T(128)S(6)} %mul.18), kind=kLoop, calls=%fused_computation.26 | loop fusion | flops 191 | bytes 524 | tf_op jit(solution)/shard_map/reduce_sum | solution.py:437
  11.0 0.2 convert_reduce_fusion.1
  11.2 1.3 %constant_dynamic-slice_fusion.8 = (bf16[32,16,256]{2,1,0:T(8,128)(2,1)S(1)}, bf16[32,16,256]{2,1,0:T(8,128)(2,1)S(1)}, bf16[32,16,256]{2,1,0:T(8,128)(2,1)S(1)}, bf16[32,16,256]{2,1,0:T(8,128)(2,1)S(1)}) fusion(bf16[256,16,512]{2,1,0:T(8,128)(2,1)} %bitcast.13, s32[]{:T(128)S(6)} %add.50, s32[]{:T(128)S(6)} %mul.41, s32[]{:T(128)S(6)} %add.49, s32[]{:T(128)S(6)} %mul.43), kind=kLoop, calls=%fused_computation.17 | loop fusion | bytes 2097168 | tf_op jit(solution)/shard_map/dynamic_slice | solution.py:444
  12.5 0.1 convert_reduce_fusion
  12.6 2.1 %collective-permute-done.1 = bf16[32,16,256]{2,1,0:T(8,128)(2,1)S(1)} collective-permute-done((bf16[32,16,256]{2,1,0:T(8,128)(2,1)S(1)}, bf16[32,16,256]{2,1,0:T(8,128)(2,1)S(1)}, u32[]{:S(2)}, u32[]{:S(2)}) %collective-permute-start.1) | collective-permute-done | bytes 262176 | tf_op jit(solution)/shard_map/ppermute | solution.py:449
  14.8 0.1 collective-permute-start.2
  14.9 0.1 add.52
  15.0 3.3 %collective-permute-start.5 = (bf16[32,16,256]{2,1,0:T(8,128)(2,1)S(1)}, bf16[32,16,256]{2,1,0:T(8,128)(2,1)S(1)}, u32[]{:S(2)}, u32[]{:S(2)}) collective-permute-start(bf16[32,16,256]{2,1,0:T(8,128)(2,1)S(1)} %add.52), channel_id=1, source_target_pairs={{0,96},{32,0},{64,32},{96,64},{1,97},{33,1},{65,33},{97,65},{2,98}... | collective-permute-start | bytes 786440 | tf_op jit(solution)/shard_map/ppermute | solution.py:449
  18.2 1.7 %constant_dynamic-slice_fusion = (bf16[32,16,256]{2,1,0:T(8,128)(2,1)S(1)}, bf16[32,16,256]{2,1,0:T(8,128)(2,1)S(1)}, bf16[32,16,256]{2,1,0:T(8,128)(2,1)S(1)}, ...) fusion(bf16[256,16,512]{2,1,0:T(8,128)(2,1)} %bitcast.14, ...), kind=kLoop, calls=%fused_computation.9 | loop fusion | bytes 4194336 | tf_op jit(solution)/shard_map/dynamic_slice | solution.py:444
  20.0 0.1 collective-permute-start.6
  20.1 0.8 pad_maximum_fusion.1
  21.0 2.0 %collective-permute-start.7 = (bf16[64,16,256]{2,1,0:T(8,128)(2,1)}, bf16[64,16,256]{2,1,0:T(8,128)(2,1)S(1)}, u32[]{:S(2)}, u32[]{:S(2)}) collective-permute-start(bf16[64,16,256]{2,1,0:T(8,128)(2,1)} %pad_maximum_fusion.1), channel_id=1, source_target_pairs={{0,32},{32,64},{64,96},{96,0},{1,33},{33,65},{65,97},{97,1},{2,34}... | collective-permute-start | bytes 1572872 | tf_op jit(solution)/shard_map/ppermute | solution.py:449
  23.0 3.0 %collective-permute-done.2.rest_2_ = bf16[32,16,256]{2,1,0:T(8,128)(2,1)S(1)} collective-permute-done((bf16[32,16,256]{2,1,0:T(8,128)(2,1)S(1)}, bf16[32,16,256]{2,1,0:T(8,128)(2,1)S(1)}, u32[]{:S(2)}, u32[]{:S(2)}) %collective-permute-start.2) | collective-permute-done | bytes 262176 | tf_op jit(solution)/shard_map/ppermute | solution.py:449
  26.0 1.7 %place_blocks.2.rest_0_ = bf16[96,16,256]{2,1,0:T(8,128)(2,1)} custom-call(s32[64]{0:T(128)S(1)} %multiply_add_fusion.place_ref, s32[96]{0:T(128)S(1)} %broadcast_subtract_fusion.empty_ref, bf16[32,16,256]{2,1,0:T(8,128)(2,1)S(1)} %get-tuple-element.20.rest_0_, bf16[32,16,256]{2,1,0:T(8,128)(2,1)S(1)} %collective-permute-done.rest_1_, ...), custom_call_target="tpu_custom_call" | custom-call | flops 8053063680 | bytes 2097152 | tf_op jit(solution)/shard_map/place_blocks/pallas_call | solution.py:125
  27.6 8.5 %all-to-all-start = ((bf16[32,3,16,256]{3,2,1,0:T(8,128)(2,1)}), bf16[32,3,16,256]{3,2,1,0:T(8,128)(2,1)}, u32[]{:S(2)}, u32[]{:S(2)}) async-start(bf16[32,3,16,256]{3,2,1,0:T(8,128)(2,1)} %bitcast.4), calls=%async_computation | async-start | bytes 1572864 | tf_op jit(solution)/shard_map/all_to_all | solution.py:483
  36.2 0.1 collective-permute-start.8
  36.3 3.2 %collective-permute-start.9 = (bf16[32,16,256]{2,1,0:T(8,128)(2,1)S(1)}, bf16[32,16,256]{2,1,0:T(8,128)(2,1)S(1)}, u32[]{:S(2)}, u32[]{:S(2)}) collective-permute-start(bf16[32,16,256]{2,1,0:T(8,128)(2,1)S(1)} %get-tuple-element.26), channel_id=1, source_target_pairs={{0,96},{32,0},{64,32},{96,64},{1,97},{33,1},{65,33},{97,65},{2,98}... | collective-permute-start | bytes 786440 | tf_op jit(solution)/shard_map/ppermute | solution.py:449
  39.5 6.4 %collective-permute-done.8.rest_2_ = bf16[32,16,256]{2,1,0:T(8,128)(2,1)S(1)} collective-permute-done((bf16[32,16,256]{2,1,0:T(8,128)(2,1)S(1)}, bf16[32,16,256]{2,1,0:T(8,128)(2,1)S(1)}, u32[]{:S(2)}, u32[]{:S(2)}) %collective-permute-start.8) | collective-permute-done | bytes 262176 | tf_op jit(solution)/shard_map/ppermute | solution.py:449
  45.9 1.6 %place_blocks.3 = bf16[96,16,256]{2,1,0:T(8,128)(2,1)} custom-call(s32[64]{0:T(128)S(1)} %copy-done.1, s32[96]{0:T(128)S(1)} %copy-done.3, bf16[32,16,256]{2,1,0:T(8,128)(2,1)S(1)} %get-tuple-element.40.rest_0_, bf16[64,16,256]{2,1,0:T(8,128)(2,1)S(1)} %collective-permute-done.6.four_ref.rest_1_, bf16[32,16,256]{2,1,0:T(8,128)(2,1)S(1)} %collective-permute-done.8.rest_2_, ...), custom_call_target="tpu_custom_call" | custom-call | bytes 2097152 | tf_op jit(solution)/shard_map/place_blocks/pallas_call | solution.py:125
  47.5 3.1 %all-to-all-done.arrived_a.front_ref = bf16[32,3,16,256]{3,2,1,0:T(8,128)(2,1)} async-done(((bf16[32,3,16,256]{3,2,1,0:T(8,128)(2,1)}), bf16[32,3,16,256]{3,2,1,0:T(8,128)(2,1)}, u32[]{:S(2)}, u32[]{:S(2)}) %all-to-all-start) | async-done | bytes 786464 | tf_op jit(solution)/shard_map/all_to_all | solution.py:483
  50.6 4.2 %all-to-all-start.1 = ((bf16[32,3,16,256]{3,2,1,0:T(8,128)(2,1)}), bf16[32,3,16,256]{3,2,1,0:T(8,128)(2,1)S(1)}, u32[]{:S(2)}, u32[]{:S(2)}) async-start(bf16[32,3,16,256]{3,2,1,0:T(8,128)(2,1)} %bitcast.5), calls=%async_computation.1 | async-start | bytes 1572864 | tf_op jit(solution)/shard_map/all_to_all | solution.py:483
  54.8 0.7 compare_convert_fusion.live_ref
  55.5 13.9 %all-to-all-done.1.arrived_b.back_ref = bf16[32,3,16,256]{3,2,1,0:T(8,128)(2,1)S(1)} async-done(((bf16[32,3,16,256]{3,2,1,0:T(8,128)(2,1)}), bf16[32,3,16,256]{3,2,1,0:T(8,128)(2,1)S(1)}, u32[]{:S(2)}, u32[]{:S(2)}) %all-to-all-start.1) | async-done | bytes 786464 | tf_op jit(solution)/shard_map/all_to_all | solution.py:483
  69.4 8.6 %precondition.1 = bf16[32,3,16,512]{3,2,1,0:T(8,128)(2,1)} custom-call(s32[3]{0:T(128)S(1)} %compare_convert_fusion.live_ref, bf16[32,3,16,256]{3,2,1,0:T(8,128)(2,1)} %all-to-all-done.arrived_a.front_ref, bf16[32,3,16,256]{3,2,1,0:T(8,128)(2,1)S(1)} %all-to-all-done.1.arrived_b.back_ref, ...), custom_call_target="tpu_custom_call", output_to_operand_aliasing={{}: (7, {})} | custom-call | flops 3758096384 | bytes 9437184 | tf_op jit(solution)/shard_map/precondition/pallas_call | solution.py:310
  78.0 4.2 %all-to-all-start.2 = ((bf16[32,3,16,512]{3,2,1,0:T(8,128)(2,1)}), bf16[32,3,16,512]{3,2,1,0:T(8,128)(2,1)S(1)}, u32[]{:S(2)}, u32[]{:S(2)}) async-start(bf16[32,3,16,512]{3,2,1,0:T(8,128)(2,1)} %precondition.1), calls=%async_computation.2 | async-start | bytes 3145728 | tf_op jit(solution)/shard_map/all_to_all | solution.py:491
  82.2 11.0 %update_stats.1 = (f32[1,1,3,512,512]{4,3,2,1,0:T(8,128)}, f32[1,1,3,512,512]{4,3,2,1,0:T(8,128)}, bf16[1,1,512,512]{3,2,1,0:T(8,128)(2,1)}, bf16[1,1,512,512]{3,2,1,0:T(8,128)(2,1)}) custom-call(s32[3]{0:T(128)S(1)} %compare_convert_fusion.live_ref, bf16[32,3,16,256]{3,2,1,0:T(8,128)(2,1)} %all-to-all-done.arrived_a.front_ref, ...), custom_call_target="tpu_custom_call" | custom-call | flops 3221225472 | bytes 13631488 | tf_op jit(solution)/shard_map/update_stats/pallas_call | solution.py:366
  93.2 12.8 %all-to-all-done.2 = bf16[32,3,16,512]{3,2,1,0:T(8,128)(2,1)S(1)} async-done(((bf16[32,3,16,512]{3,2,1,0:T(8,128)(2,1)}), bf16[32,3,16,512]{3,2,1,0:T(8,128)(2,1)S(1)}, u32[]{:S(2)}, u32[]{:S(2)}) %all-to-all-start.2) | async-done | bytes 1572896 | tf_op jit(solution)/shard_map/all_to_all | solution.py:491
  106.0 1.5 %assemble.1 = bf16[64,16,512]{2,1,0:T(8,128)(2,1)} custom-call(s32[64]{0:T(128)S(1)} %copy-done.1, bf16[96,16,512]{2,1,0:T(8,128)(2,1)S(1)} %bitcast.11), custom_call_target="tpu_custom_call" | custom-call | bytes 2097152 | tf_op jit(solution)/shard_map/assemble/pallas_call | solution.py:402
  (23 shorter events, 0.2 us)
Async XLA Ops:
  1.7 13.2 %collective-permute-start.4 = (bf16[32,16,256]{2,1,0:T(8,128)(2,1)S(1)}, bf16[32,16,256]{2,1,0:T(8,128)(2,1)S(1)}, u32[]{:S(2)}, u32[]{:S(2)}) collective-permute-start(bf16[32,16,256]{2,1,0:T(8,128)(2,1)S(1)} %get-tuple-element.47), channel_id=1, source_target_pairs={{0,96},{32,0},{64,32},{96,64},{1,97},{33,1},{65,33},{97,65},{2,98}... | collective-permute-start | bytes 786440 | tf_op jit(solution)/shard_map/ppermute | solution.py:449
  4.6 10.1 %collective-permute-start.1 = (bf16[32,16,256]{2,1,0:T(8,128)(2,1)S(1)}, bf16[32,16,256]{2,1,0:T(8,128)(2,1)S(1)}, u32[]{:S(2)}, u32[]{:S(2)}) collective-permute-start(bf16[32,16,256]{2,1,0:T(8,128)(2,1)S(1)} %get-tuple-element.48), channel_id=1, source_target_pairs={{0,32},{32,64},{64,96},{96,0},{1,33},{33,65},{65,97},{97,1},{2,34}... | collective-permute-start | bytes 786440 | tf_op jit(solution)/shard_map/ppermute | solution.py:449
  6.4 14.6 %collective-permute-start = (bf16[32,16,256]{2,1,0:T(8,128)(2,1)}, bf16[32,16,256]{2,1,0:T(8,128)(2,1)S(1)}, u32[]{:S(2)}, u32[]{:S(2)}) collective-permute-start(bf16[32,16,256]{2,1,0:T(8,128)(2,1)} %get-tuple-element.45), channel_id=1, source_target_pairs={{0,96},{32,0},{64,32},{96,64},{1,97},{33,1},{65,33},{97,65},{2,98}... | collective-permute-start | bytes 786440 | tf_op jit(solution)/shard_map/ppermute | solution.py:449
  9.6 13.3 %collective-permute-start.3 = (bf16[32,16,256]{2,1,0:T(8,128)(2,1)S(1)}, bf16[32,16,256]{2,1,0:T(8,128)(2,1)S(1)}, u32[]{:S(2)}, u32[]{:S(2)}) collective-permute-start(bf16[32,16,256]{2,1,0:T(8,128)(2,1)S(1)} %get-tuple-element.46), channel_id=1, source_target_pairs={{0,32},{32,64},{64,96},{96,0},{1,33},{33,65},{65,97},{97,1},{2,34}... | collective-permute-start | bytes 786440 | tf_op jit(solution)/shard_map/ppermute | solution.py:449
  11.2 14.8 %copy-start = (s32[64]{0:T(128)}, s32[64]{0:T(128)S(1)}, u32[]{:S(2)}) copy-start(s32[64]{0:T(128)S(1)} %multiply_add_fusion.place_ref) | copy-start | bytes 772
  12.6 13.4 %copy-start.2 = (s32[96]{0:T(128)}, s32[96]{0:T(128)S(1)}, u32[]{:S(2)}) copy-start(s32[96]{0:T(128)S(1)} %broadcast_subtract_fusion.empty_ref) | copy-start | bytes 1156
  14.8 11.2 %collective-permute-start.2 = (bf16[32,16,256]{2,1,0:T(8,128)(2,1)S(1)}, bf16[32,16,256]{2,1,0:T(8,128)(2,1)S(1)}, u32[]{:S(2)}, u32[]{:S(2)}) collective-permute-start(bf16[32,16,256]{2,1,0:T(8,128)(2,1)S(1)} %add.51), channel_id=1, source_target_pairs={{0,32},{32,64},{64,96},{96,0},{1,33},{33,65},{65,97},{97,1},{2,34}... | collective-permute-start | bytes 786440 | tf_op jit(solution)/shard_map/ppermute | solution.py:449
  15.0 11.0 %collective-permute-start.5 = (bf16[32,16,256]{2,1,0:T(8,128)(2,1)S(1)}, bf16[32,16,256]{2,1,0:T(8,128)(2,1)S(1)}, u32[]{:S(2)}, u32[]{:S(2)}) collective-permute-start(bf16[32,16,256]{2,1,0:T(8,128)(2,1)S(1)} %add.52), channel_id=1, source_target_pairs={{0,96},{32,0},{64,32},{96,64},{1,97},{33,1},{65,33},{97,65},{2,98}... | collective-permute-start | bytes 786440 | tf_op jit(solution)/shard_map/ppermute | solution.py:449
  20.0 16.1 %collective-permute-start.6 = (bf16[64,16,256]{2,1,0:T(8,128)(2,1)S(1)}, bf16[64,16,256]{2,1,0:T(8,128)(2,1)S(1)}, u32[]{:S(2)}, u32[]{:S(2)}) collective-permute-start(bf16[64,16,256]{2,1,0:T(8,128)(2,1)S(1)} %pad_maximum_fusion), channel_id=1, source_target_pairs={{0,96},{32,0},{64,32},{96,64},{1,97},{33,1},{65,33},{97,65},{2,98}... | collective-permute-start | bytes 1572872 | tf_op jit(solution)/shard_map/ppermute | solution.py:449
  21.0 15.1 %collective-permute-start.7 = (bf16[64,16,256]{2,1,0:T(8,128)(2,1)}, bf16[64,16,256]{2,1,0:T(8,128)(2,1)S(1)}, u32[]{:S(2)}, u32[]{:S(2)}) collective-permute-start(bf16[64,16,256]{2,1,0:T(8,128)(2,1)} %pad_maximum_fusion.1), channel_id=1, source_target_pairs={{0,32},{32,64},{64,96},{96,0},{1,33},{33,65},{65,97},{97,1},{2,34}... | collective-permute-start | bytes 1572872 | tf_op jit(solution)/shard_map/ppermute | solution.py:449
  27.6 23.0 %all-to-all-start = ((bf16[32,3,16,256]{3,2,1,0:T(8,128)(2,1)}), bf16[32,3,16,256]{3,2,1,0:T(8,128)(2,1)}, u32[]{:S(2)}, u32[]{:S(2)}) async-start(bf16[32,3,16,256]{3,2,1,0:T(8,128)(2,1)} %bitcast.4), calls=%async_computation | async-start | bytes 1572864 | tf_op jit(solution)/shard_map/all_to_all | solution.py:483
  36.1 9.8 %copy-start.1 = (s32[64]{0:T(128)S(1)}, s32[64]{0:T(128)}, u32[]{:S(2)}) copy-start(s32[64]{0:T(128)} %copy-done) | copy-start | bytes 772
  36.1 9.8 %copy-start.3 = (s32[96]{0:T(128)S(1)}, s32[96]{0:T(128)}, u32[]{:S(2)}) copy-start(s32[96]{0:T(128)} %copy-done.2) | copy-start | bytes 1156
  36.2 9.7 %collective-permute-start.8 = (bf16[32,16,256]{2,1,0:T(8,128)(2,1)S(1)}, bf16[32,16,256]{2,1,0:T(8,128)(2,1)S(1)}, u32[]{:S(2)}, u32[]{:S(2)}) collective-permute-start(bf16[32,16,256]{2,1,0:T(8,128)(2,1)S(1)} %get-tuple-element.25), channel_id=1, source_target_pairs={{0,32},{32,64},{64,96},{96,0},{1,33},{33,65},{65,97},{97,1},{2,34}... | collective-permute-start | bytes 786440 | tf_op jit(solution)/shard_map/ppermute | solution.py:449
  36.3 9.6 %collective-permute-start.9 = (bf16[32,16,256]{2,1,0:T(8,128)(2,1)S(1)}, bf16[32,16,256]{2,1,0:T(8,128)(2,1)S(1)}, u32[]{:S(2)}, u32[]{:S(2)}) collective-permute-start(bf16[32,16,256]{2,1,0:T(8,128)(2,1)S(1)} %get-tuple-element.26), channel_id=1, source_target_pairs={{0,96},{32,0},{64,32},{96,64},{1,97},{33,1},{65,33},{97,65},{2,98}... | collective-permute-start | bytes 786440 | tf_op jit(solution)/shard_map/ppermute | solution.py:449
  50.6 18.8 %all-to-all-start.1 = ((bf16[32,3,16,256]{3,2,1,0:T(8,128)(2,1)}), bf16[32,3,16,256]{3,2,1,0:T(8,128)(2,1)S(1)}, u32[]{:S(2)}, u32[]{:S(2)}) async-start(bf16[32,3,16,256]{3,2,1,0:T(8,128)(2,1)} %bitcast.5), calls=%async_computation.1 | async-start | bytes 1572864 | tf_op jit(solution)/shard_map/all_to_all | solution.py:483
  78.0 27.9 %all-to-all-start.2 = ((bf16[32,3,16,512]{3,2,1,0:T(8,128)(2,1)}), bf16[32,3,16,512]{3,2,1,0:T(8,128)(2,1)S(1)}, u32[]{:S(2)}, u32[]{:S(2)}) async-start(bf16[32,3,16,512]{3,2,1,0:T(8,128)(2,1)} %precondition.1), calls=%async_computation.2 | async-start | bytes 3145728 | tf_op jit(solution)/shard_map/all_to_all | solution.py:491

commit v9 on v8

--- a/solution.py
+++ b/solution.py
@@ -275,8 +275,11 @@
         product(root, applied[slot], use)
         return total(squares) * (1.0 / entries)
 
+    back = arrived_b[:, 0].reshape(side, -1)
+    raws[0] = mul(back, back, ((1,), (1,)))
     blocks = [block_of(0)]
-    grams[0] = mul(blocks[0], blocks[0], ((1,), (1,)))
+    front = halves[0].reshape(side, -1)
+    grams[0] = raws[0] + mul(front, front, ((1,), (1,)))
     grams[1] = mul(blocks[0], blocks[0], ((0,), (0,)))
     for slot in range(1, MOST):
         blocks.append(block_of(slot))

time: 108 us -> 108 us (level)
  no operation moved by 1% of the time
where the time goes in v9:
time: 108 us
  waiting for transfers between devices  41.3 us (38%)
  starting transfers between devices  31.7 us (29%)
  Pallas kernels  24.3 us (22%)
  local copies, waits for them, and re-layouts  5.85 us (5%)
  other arithmetic  3.33 us (3%)
    all_to_all x2, waiting for transfers between devices, on_device(): lax.all_to_all(outgoing.reshape(owners, MOST, slab_rows, -1), 'fsdp', spl...  17 us
    all_to_all x1, waiting for transfers between devices, on_device(): lax.all_to_all(results, 'fsdp', split_axis=0, concat_axis=0, tiled=True)  12.8 us
    ppermute x5, starting transfers between devices, send(): lax.ppermute(pair[1], 'rep', down)  12.8 us
    all_to_all x2, starting transfers between devices, on_device(): lax.all_to_all(outgoing.reshape(owners, MOST, slab_rows, -1), 'fsdp', spl...  12.7 us
    ppermute x5, waiting for transfers between devices, send(): lax.ppermute(pair[0], 'rep', up)  11.5 us
    pallas_call x1, Pallas kernels, update_stats(): pl.pallas_call(stats_kernel, grid=(MOST,), out_shape=[shape, shape, root,...  11 us
    pallas_call x1, Pallas kernels, precondition(): pl.pallas_call(precondition_kernel, out_shape=jax.ShapeDtypeStruct((owner...  8.53 us
    dynamic_slice x4, local copies, waits for them, and re-layouts, part(): lax.dynamic_slice(source, (start, 0, columns[0]), (half, slab_rows, colum...  5.83 us
  transfers between devices with their start and end apart: 13, of which 6 were waited for; matrix products, arithmetic and copies ran while one was open for 8% of the time, Pallas kernels for 13%

profile of v9, /device:TPU:0, one launch (start us, length us, event | category | flops | bytes accessed | tf_op | source)
XLA Modules:
  0.0 107.5 jit_solution(11804310796127376092)
XLA Ops:
  0.6 1.1 dynamic-slice_bitcast_fusion
  1.7 2.9 %collective-permute-start.4 = (bf16[32,16,256]{2,1,0:T(8,128)(2,1)S(1)}, bf16[32,16,256]{2,1,0:T(8,128)(2,1)S(1)}, u32[]{:S(2)}, u32[]{:S(2)}) collective-permute-start(bf16[32,16,256]{2,1,0:T(8,128)(2,1)S(1)} %get-tuple-element.47), channel_id=1, source_target_pairs={{0,96},{32,0},{64,32},{96,64},{1,97},{33,1},{65,33},{97,65},{2,98}... | collective-permute-start | bytes 786440 | tf_op jit(solution)/shard_map/ppermute | solution.py:452
  4.6 1.8 %constant_dynamic-slice_fusion.12 = (bf16[32,16,256]{2,1,0:T(8,128)(2,1)}, bf16[32,16,256]{2,1,0:T(8,128)(2,1)S(1)}) fusion(bf16[256,16,512]{2,1,0:T(8,128)(2,1)} %bitcast.12, s32[]{:T(128)S(6)} %mul.42, s32[]{:T(128)S(6)} %add.47), kind=kLoop, calls=%fused_computation.21 | loop fusion | bytes 1048584 | tf_op jit(solution)/shard_map/dynamic_slice | solution.py:447
  6.4 3.2 %collective-permute-start = (bf16[32,16,256]{2,1,0:T(8,128)(2,1)}, bf16[32,16,256]{2,1,0:T(8,128)(2,1)S(1)}, u32[]{:S(2)}, u32[]{:S(2)}) collective-permute-start(bf16[32,16,256]{2,1,0:T(8,128)(2,1)} %get-tuple-element.45), channel_id=1, source_target_pairs={{0,96},{32,0},{64,32},{96,64},{1,97},{33,1},{65,33},{97,65},{2,98}... | collective-permute-start | bytes 786440 | tf_op jit(solution)/shard_map/ppermute | solution.py:452
  9.6 1.4 %fusion.1 = (s32[]{:T(128)}, s32[64]{0:T(128)S(1)}) fusion(s32[]{:T(128)S(6)} %axis_index.25, s32[256,1]{0,1:T(1,128)} %param.7, s32[]{:T(128)S(6)} %mul.18), kind=kLoop, calls=%fused_computation.26 | loop fusion | flops 191 | bytes 524 | tf_op jit(solution)/shard_map/reduce_sum | solution.py:440
  11.0 0.2 convert_reduce_fusion.1
  11.2 1.3 %constant_dynamic-slice_fusion.8 = (bf16[32,16,256]{2,1,0:T(8,128)(2,1)S(1)}, bf16[32,16,256]{2,1,0:T(8,128)(2,1)S(1)}, bf16[32,16,256]{2,1,0:T(8,128)(2,1)S(1)}, bf16[32,16,256]{2,1,0:T(8,128)(2,1)S(1)}) fusion(bf16[256,16,512]{2,1,0:T(8,128)(2,1)} %bitcast.13, s32[]{:T(128)S(6)} %add.50, s32[]{:T(128)S(6)} %mul.41, s32[]{:T(128)S(6)} %add.49, s32[]{:T(128)S(6)} %mul.43), kind=kLoop, calls=%fused_computation.17 | loop fusion | bytes 2097168 | tf_op jit(solution)/shard_map/dynamic_slice | solution.py:447
  12.5 0.1 convert_reduce_fusion
  12.6 2.1 %collective-permute-done.1 = bf16[32,16,256]{2,1,0:T(8,128)(2,1)S(1)} collective-permute-done((bf16[32,16,256]{2,1,0:T(8,128)(2,1)S(1)}, bf16[32,16,256]{2,1,0:T(8,128)(2,1)S(1)}, u32[]{:S(2)}, u32[]{:S(2)}) %collective-permute-start.1) | collective-permute-done | bytes 262176 | tf_op jit(solution)/shard_map/ppermute | solution.py:452
  14.8 0.1 collective-permute-start.2
  14.9 0.1 add.52
  15.0 3.3 %collective-permute-start.5 = (bf16[32,16,256]{2,1,0:T(8,128)(2,1)S(1)}, bf16[32,16,256]{2,1,0:T(8,128)(2,1)S(1)}, u32[]{:S(2)}, u32[]{:S(2)}) collective-permute-start(bf16[32,16,256]{2,1,0:T(8,128)(2,1)S(1)} %add.52), channel_id=1, source_target_pairs={{0,96},{32,0},{64,32},{96,64},{1,97},{33,1},{65,33},{97,65},{2,98}... | collective-permute-start | bytes 786440 | tf_op jit(solution)/shard_map/ppermute | solution.py:452
  18.2 1.7 %constant_dynamic-slice_fusion = (bf16[32,16,256]{2,1,0:T(8,128)(2,1)S(1)}, bf16[32,16,256]{2,1,0:T(8,128)(2,1)S(1)}, bf16[32,16,256]{2,1,0:T(8,128)(2,1)S(1)}, ...) fusion(bf16[256,16,512]{2,1,0:T(8,128)(2,1)} %bitcast.14, ...), kind=kLoop, calls=%fused_computation.9 | loop fusion | bytes 4194336 | tf_op jit(solution)/shard_map/dynamic_slice | solution.py:447
  20.0 0.1 collective-permute-start.6
  20.1 0.8 pad_maximum_fusion.1
  21.0 2.0 %collective-permute-start.7 = (bf16[64,16,256]{2,1,0:T(8,128)(2,1)}, bf16[64,16,256]{2,1,0:T(8,128)(2,1)S(1)}, u32[]{:S(2)}, u32[]{:S(2)}) collective-permute-start(bf16[64,16,256]{2,1,0:T(8,128)(2,1)} %pad_maximum_fusion.1), channel_id=1, source_target_pairs={{0,32},{32,64},{64,96},{96,0},{1,33},{33,65},{65,97},{97,1},{2,34}... | collective-permute-start | bytes 1572872 | tf_op jit(solution)/shard_map/ppermute | solution.py:452
  23.0 3.0 %collective-permute-done.2.rest_2_ = bf16[32,16,256]{2,1,0:T(8,128)(2,1)S(1)} collective-permute-done((bf16[32,16,256]{2,1,0:T(8,128)(2,1)S(1)}, bf16[32,16,256]{2,1,0:T(8,128)(2,1)S(1)}, u32[]{:S(2)}, u32[]{:S(2)}) %collective-permute-start.2) | collective-permute-done | bytes 262176 | tf_op jit(solution)/shard_map/ppermute | solution.py:452
  26.0 1.7 %place_blocks.2.rest_0_ = bf16[96,16,256]{2,1,0:T(8,128)(2,1)} custom-call(s32[64]{0:T(128)S(1)} %multiply_add_fusion.place_ref, s32[96]{0:T(128)S(1)} %broadcast_subtract_fusion.empty_ref, bf16[32,16,256]{2,1,0:T(8,128)(2,1)S(1)} %get-tuple-element.20.rest_0_, bf16[32,16,256]{2,1,0:T(8,128)(2,1)S(1)} %collective-permute-done.rest_1_, ...), custom_call_target="tpu_custom_call" | custom-call | flops 8053063680 | bytes 2097152 | tf_op jit(solution)/shard_map/place_blocks/pallas_call | solution.py:125
  27.6 8.5 %all-to-all-start = ((bf16[32,3,16,256]{3,2,1,0:T(8,128)(2,1)}), bf16[32,3,16,256]{3,2,1,0:T(8,128)(2,1)}, u32[]{:S(2)}, u32[]{:S(2)}) async-start(bf16[32,3,16,256]{3,2,1,0:T(8,128)(2,1)} %bitcast.4), calls=%async_computation | async-start | bytes 1572864 | tf_op jit(solution)/shard_map/all_to_all | solution.py:486
  36.2 0.1 collective-permute-start.8
  36.3 3.2 %collective-permute-start.9 = (bf16[32,16,256]{2,1,0:T(8,128)(2,1)S(1)}, bf16[32,16,256]{2,1,0:T(8,128)(2,1)S(1)}, u32[]{:S(2)}, u32[]{:S(2)}) collective-permute-start(bf16[32,16,256]{2,1,0:T(8,128)(2,1)S(1)} %get-tuple-element.26), channel_id=1, source_target_pairs={{0,96},{32,0},{64,32},{96,64},{1,97},{33,1},{65,33},{97,65},{2,98}... | collective-permute-start | bytes 786440 | tf_op jit(solution)/shard_map/ppermute | solution.py:452
  39.5 6.4 %collective-permute-done.8.rest_2_ = bf16[32,16,256]{2,1,0:T(8,128)(2,1)S(1)} collective-permute-done((bf16[32,16,256]{2,1,0:T(8,128)(2,1)S(1)}, bf16[32,16,256]{2,1,0:T(8,128)(2,1)S(1)}, u32[]{:S(2)}, u32[]{:S(2)}) %collective-permute-start.8) | collective-permute-done | bytes 262176 | tf_op jit(solution)/shard_map/ppermute | solution.py:452
  45.9 1.6 %place_blocks.3 = bf16[96,16,256]{2,1,0:T(8,128)(2,1)} custom-call(s32[64]{0:T(128)S(1)} %copy-done.1, s32[96]{0:T(128)S(1)} %copy-done.3, bf16[32,16,256]{2,1,0:T(8,128)(2,1)S(1)} %get-tuple-element.40.rest_0_, bf16[64,16,256]{2,1,0:T(8,128)(2,1)S(1)} %collective-permute-done.6.four_ref.rest_1_, bf16[32,16,256]{2,1,0:T(8,128)(2,1)S(1)} %collective-permute-done.8.rest_2_, ...), custom_call_target="tpu_custom_call" | custom-call | bytes 2097152 | tf_op jit(solution)/shard_map/place_blocks/pallas_call | solution.py:125
  47.5 3.1 %all-to-all-done.arrived_a.front_ref = bf16[32,3,16,256]{3,2,1,0:T(8,128)(2,1)} async-done(((bf16[32,3,16,256]{3,2,1,0:T(8,128)(2,1)}), bf16[32,3,16,256]{3,2,1,0:T(8,128)(2,1)}, u32[]{:S(2)}, u32[]{:S(2)}) %all-to-all-start) | async-done | bytes 786464 | tf_op jit(solution)/shard_map/all_to_all | solution.py:486
  50.6 4.2 %all-to-all-start.1 = ((bf16[32,3,16,256]{3,2,1,0:T(8,128)(2,1)}), bf16[32,3,16,256]{3,2,1,0:T(8,128)(2,1)S(1)}, u32[]{:S(2)}, u32[]{:S(2)}) async-start(bf16[32,3,16,256]{3,2,1,0:T(8,128)(2,1)} %bitcast.5), calls=%async_computation.1 | async-start | bytes 1572864 | tf_op jit(solution)/shard_map/all_to_all | solution.py:486
  54.8 0.7 compare_convert_fusion.live_ref
  55.5 13.9 %all-to-all-done.1.arrived_b.back_ref = bf16[32,3,16,256]{3,2,1,0:T(8,128)(2,1)S(1)} async-done(((bf16[32,3,16,256]{3,2,1,0:T(8,128)(2,1)}), bf16[32,3,16,256]{3,2,1,0:T(8,128)(2,1)S(1)}, u32[]{:S(2)}, u32[]{:S(2)}) %all-to-all-start.1) | async-done | bytes 786464 | tf_op jit(solution)/shard_map/all_to_all | solution.py:486
  69.4 8.5 %precondition.1 = bf16[32,3,16,512]{3,2,1,0:T(8,128)(2,1)} custom-call(s32[3]{0:T(128)S(1)} %compare_convert_fusion.live_ref, bf16[32,3,16,256]{3,2,1,0:T(8,128)(2,1)} %all-to-all-done.arrived_a.front_ref, bf16[32,3,16,256]{3,2,1,0:T(8,128)(2,1)S(1)} %all-to-all-done.1.arrived_b.back_ref, ...), custom_call_target="tpu_custom_call", output_to_operand_aliasing={{}: (7, {})} | custom-call | flops 3758096384 | bytes 9437184 | tf_op jit(solution)/shard_map/precondition/pallas_call | solution.py:313
  77.9 4.2 %all-to-all-start.2 = ((bf16[32,3,16,512]{3,2,1,0:T(8,128)(2,1)}), bf16[32,3,16,512]{3,2,1,0:T(8,128)(2,1)S(1)}, u32[]{:S(2)}, u32[]{:S(2)}) async-start(bf16[32,3,16,512]{3,2,1,0:T(8,128)(2,1)} %precondition.1), calls=%async_computation.2 | async-start | bytes 3145728 | tf_op jit(solution)/shard_map/all_to_all | solution.py:494
  82.1 11.0 %update_stats.1 = (f32[1,1,3,512,512]{4,3,2,1,0:T(8,128)}, f32[1,1,3,512,512]{4,3,2,1,0:T(8,128)}, bf16[1,1,512,512]{3,2,1,0:T(8,128)(2,1)}, bf16[1,1,512,512]{3,2,1,0:T(8,128)(2,1)}) custom-call(s32[3]{0:T(128)S(1)} %compare_convert_fusion.live_ref, bf16[32,3,16,256]{3,2,1,0:T(8,128)(2,1)} %all-to-all-done.arrived_a.front_ref, ...), custom_call_target="tpu_custom_call" | custom-call | flops 3221225472 | bytes 13631488 | tf_op jit(solution)/shard_map/update_stats/pallas_call | solution.py:369
  93.1 12.8 %all-to-all-done.2 = bf16[32,3,16,512]{3,2,1,0:T(8,128)(2,1)S(1)} async-done(((bf16[32,3,16,512]{3,2,1,0:T(8,128)(2,1)}), bf16[32,3,16,512]{3,2,1,0:T(8,128)(2,1)S(1)}, u32[]{:S(2)}, u32[]{:S(2)}) %all-to-all-start.2) | async-done | bytes 1572896 | tf_op jit(solution)/shard_map/all_to_all | solution.py:494
  105.9 1.5 %assemble.1 = bf16[64,16,512]{2,1,0:T(8,128)(2,1)} custom-call(s32[64]{0:T(128)S(1)} %copy-done.1, bf16[96,16,512]{2,1,0:T(8,128)(2,1)S(1)} %bitcast.11), custom_call_target="tpu_custom_call" | custom-call | bytes 2097152 | tf_op jit(solution)/shard_map/assemble/pallas_call | solution.py:405
  (23 shorter events, 0.2 us)
Async XLA Ops:
  1.7 13.2 %collective-permute-start.4 = (bf16[32,16,256]{2,1,0:T(8,128)(2,1)S(1)}, bf16[32,16,256]{2,1,0:T(8,128)(2,1)S(1)}, u32[]{:S(2)}, u32[]{:S(2)}) collective-permute-start(bf16[32,16,256]{2,1,0:T(8,128)(2,1)S(1)} %get-tuple-element.47), channel_id=1, source_target_pairs={{0,96},{32,0},{64,32},{96,64},{1,97},{33,1},{65,33},{97,65},{2,98}... | collective-permute-start | bytes 786440 | tf_op jit(solution)/shard_map/ppermute | solution.py:452
  4.6 10.1 %collective-permute-start.1 = (bf16[32,16,256]{2,1,0:T(8,128)(2,1)S(1)}, bf16[32,16,256]{2,1,0:T(8,128)(2,1)S(1)}, u32[]{:S(2)}, u32[]{:S(2)}) collective-permute-start(bf16[32,16,256]{2,1,0:T(8,128)(2,1)S(1)} %get-tuple-element.48), channel_id=1, source_target_pairs={{0,32},{32,64},{64,96},{96,0},{1,33},{33,65},{65,97},{97,1},{2,34}... | collective-permute-start | bytes 786440 | tf_op jit(solution)/shard_map/ppermute | solution.py:452
  6.4 14.6 %collective-permute-start = (bf16[32,16,256]{2,1,0:T(8,128)(2,1)}, bf16[32,16,256]{2,1,0:T(8,128)(2,1)S(1)}, u32[]{:S(2)}, u32[]{:S(2)}) collective-permute-start(bf16[32,16,256]{2,1,0:T(8,128)(2,1)} %get-tuple-element.45), channel_id=1, source_target_pairs={{0,96},{32,0},{64,32},{96,64},{1,97},{33,1},{65,33},{97,65},{2,98}... | collective-permute-start | bytes 786440 | tf_op jit(solution)/shard_map/ppermute | solution.py:452
  9.6 13.3 %collective-permute-start.3 = (bf16[32,16,256]{2,1,0:T(8,128)(2,1)S(1)}, bf16[32,16,256]{2,1,0:T(8,128)(2,1)S(1)}, u32[]{:S(2)}, u32[]{:S(2)}) collective-permute-start(bf16[32,16,256]{2,1,0:T(8,128)(2,1)S(1)} %get-tuple-element.46), channel_id=1, source_target_pairs={{0,32},{32,64},{64,96},{96,0},{1,33},{33,65},{65,97},{97,1},{2,34}... | collective-permute-start | bytes 786440 | tf_op jit(solution)/shard_map/ppermute | solution.py:452
  11.2 14.8 %copy-start = (s32[64]{0:T(128)}, s32[64]{0:T(128)S(1)}, u32[]{:S(2)}) copy-start(s32[64]{0:T(128)S(1)} %multiply_add_fusion.place_ref) | copy-start | bytes 772
  12.6 13.4 %copy-start.2 = (s32[96]{0:T(128)}, s32[96]{0:T(128)S(1)}, u32[]{:S(2)}) copy-start(s32[96]{0:T(128)S(1)} %broadcast_subtract_fusion.empty_ref) | copy-start | bytes 1156
  14.8 11.2 %collective-permute-start.2 = (bf16[32,16,256]{2,1,0:T(8,128)(2,1)S(1)}, bf16[32,16,256]{2,1,0:T(8,128)(2,1)S(1)}, u32[]{:S(2)}, u32[]{:S(2)}) collective-permute-start(bf16[32,16,256]{2,1,0:T(8,128)(2,1)S(1)} %add.51), channel_id=1, source_target_pairs={{0,32},{32,64},{64,96},{96,0},{1,33},{33,65},{65,97},{97,1},{2,34}... | collective-permute-start | bytes 786440 | tf_op jit(solution)/shard_map/ppermute | solution.py:452
  15.0 11.0 %collective-permute-start.5 = (bf16[32,16,256]{2,1,0:T(8,128)(2,1)S(1)}, bf16[32,16,256]{2,1,0:T(8,128)(2,1)S(1)}, u32[]{:S(2)}, u32[]{:S(2)}) collective-permute-start(bf16[32,16,256]{2,1,0:T(8,128)(2,1)S(1)} %add.52), channel_id=1, source_target_pairs={{0,96},{32,0},{64,32},{96,64},{1,97},{33,1},{65,33},{97,65},{2,98}... | collective-permute-start | bytes 786440 | tf_op jit(solution)/shard_map/ppermute | solution.py:452
  20.0 16.1 %collective-permute-start.6 = (bf16[64,16,256]{2,1,0:T(8,128)(2,1)S(1)}, bf16[64,16,256]{2,1,0:T(8,128)(2,1)S(1)}, u32[]{:S(2)}, u32[]{:S(2)}) collective-permute-start(bf16[64,16,256]{2,1,0:T(8,128)(2,1)S(1)} %pad_maximum_fusion), channel_id=1, source_target_pairs={{0,96},{32,0},{64,32},{96,64},{1,97},{33,1},{65,33},{97,65},{2,98}... | collective-permute-start | bytes 1572872 | tf_op jit(solution)/shard_map/ppermute | solution.py:452
  21.0 15.1 %collective-permute-start.7 = (bf16[64,16,256]{2,1,0:T(8,128)(2,1)}, bf16[64,16,256]{2,1,0:T(8,128)(2,1)S(1)}, u32[]{:S(2)}, u32[]{:S(2)}) collective-permute-start(bf16[64,16,256]{2,1,0:T(8,128)(2,1)} %pad_maximum_fusion.1), channel_id=1, source_target_pairs={{0,32},{32,64},{64,96},{96,0},{1,33},{33,65},{65,97},{97,1},{2,34}... | collective-permute-start | bytes 1572872 | tf_op jit(solution)/shard_map/ppermute | solution.py:452
  27.6 23.0 %all-to-all-start = ((bf16[32,3,16,256]{3,2,1,0:T(8,128)(2,1)}), bf16[32,3,16,256]{3,2,1,0:T(8,128)(2,1)}, u32[]{:S(2)}, u32[]{:S(2)}) async-start(bf16[32,3,16,256]{3,2,1,0:T(8,128)(2,1)} %bitcast.4), calls=%async_computation | async-start | bytes 1572864 | tf_op jit(solution)/shard_map/all_to_all | solution.py:486
  36.1 9.8 %copy-start.1 = (s32[64]{0:T(128)S(1)}, s32[64]{0:T(128)}, u32[]{:S(2)}) copy-start(s32[64]{0:T(128)} %copy-done) | copy-start | bytes 772
  36.1 9.8 %copy-start.3 = (s32[96]{0:T(128)S(1)}, s32[96]{0:T(128)}, u32[]{:S(2)}) copy-start(s32[96]{0:T(128)} %copy-done.2) | copy-start | bytes 1156
  36.2 9.7 %collective-permute-start.8 = (bf16[32,16,256]{2,1,0:T(8,128)(2,1)S(1)}, bf16[32,16,256]{2,1,0:T(8,128)(2,1)S(1)}, u32[]{:S(2)}, u32[]{:S(2)}) collective-permute-start(bf16[32,16,256]{2,1,0:T(8,128)(2,1)S(1)} %get-tuple-element.25), channel_id=1, source_target_pairs={{0,32},{32,64},{64,96},{96,0},{1,33},{33,65},{65,97},{97,1},{2,34}... | collective-permute-start | bytes 786440 | tf_op jit(solution)/shard_map/ppermute | solution.py:452
  36.3 9.6 %collective-permute-start.9 = (bf16[32,16,256]{2,1,0:T(8,128)(2,1)S(1)}, bf16[32,16,256]{2,1,0:T(8,128)(2,1)S(1)}, u32[]{:S(2)}, u32[]{:S(2)}) collective-permute-start(bf16[32,16,256]{2,1,0:T(8,128)(2,1)S(1)} %get-tuple-element.26), channel_id=1, source_target_pairs={{0,96},{32,0},{64,32},{96,64},{1,97},{33,1},{65,33},{97,65},{2,98}... | collective-permute-start | bytes 786440 | tf_op jit(solution)/shard_map/ppermute | solution.py:452
  50.6 18.8 %all-to-all-start.1 = ((bf16[32,3,16,256]{3,2,1,0:T(8,128)(2,1)}), bf16[32,3,16,256]{3,2,1,0:T(8,128)(2,1)S(1)}, u32[]{:S(2)}, u32[]{:S(2)}) async-start(bf16[32,3,16,256]{3,2,1,0:T(8,128)(2,1)} %bitcast.5), calls=%async_computation.1 | async-start | bytes 1572864 | tf_op jit(solution)/shard_map/all_to_all | solution.py:486
  77.9 27.9 %all-to-all-start.2 = ((bf16[32,3,16,512]{3,2,1,0:T(8,128)(2,1)}), bf16[32,3,16,512]{3,2,1,0:T(8,128)(2,1)S(1)}, u32[]{:S(2)}, u32[]{:S(2)}) async-start(bf16[32,3,16,512]{3,2,1,0:T(8,128)(2,1)} %precondition.1), calls=%async_computation.2 | async-start | bytes 3145728 | tf_op jit(solution)/shard_map/all_to_all | solution.py:494
